TPU v7x, 32 devices: a whole 2x2x4 slice. The times are simulated.
32 devices in a mesh: dp: 16 (over z, y, x), tower: 2 (over core).
Axes of the slice: x: 2, y: 2, z: 4, core: 2. Of those that a mesh axis runs over, the one named last changes fastest.
Arguments:
- features: bfloat16 [16, 1364, 256], P('dp', None, 'tower'), may hold values from -6 to 6
- bn_mean: float32 [256], replicated, may hold values from -3 to 3
- bn_var: float32 [256], replicated, may hold values from 0.25 to 4
- tower_weight: bfloat16 [2, 4, 3, 3, 256, 256], P('tower'), may hold values from -0.125 to 0.125
- norm_gain: float32 [2, 4, 256], P('tower'), may hold values from 0.5 to 1.5
- norm_bias: float32 [2, 4, 256], P('tower'), may hold values from -1.5 to 1.5
- head_weight: bfloat16 [3, 3, 256, 85], replicated, may hold values from -0.0625 to 0.0625
- head_bias: float32 [85], replicated, may hold values from -2 to 2
- level_scale: float32 [5], replicated, may hold values from 0.5 to 1.5
- cls_cot: bfloat16 [16, 1364, 80], P('dp'), may hold values from -6 to 6
- reg_cot: bfloat16 [16, 1364, 5], P('dp'), may hold values from -6 to 6
- positive: int32 [16, 1364], P('dp'), may hold values from 0 to 1, as said below
Outputs:
- feature_grad: bfloat16 [16, 1364, 256], P('dp', None, 'tower')
- tower_weight_grad: float32 [2, 4, 3, 3, 256, 256], P('tower')
- norm_gain_grad: float32 [2, 4, 256], P('tower')
- norm_bias_grad: float32 [2, 4, 256], P('tower')
- head_weight_grad: float32 [3, 3, 256, 85], replicated
- head_bias_grad: float32 [85], replicated
- level_scale_grad: float32 [5], replicated
Inputs may be any that keep to these rules, and one draw needn't show every extreme that they name: 1 marks a positive location, 0 any other.
All inputs are finite; a program needn't handle non-finite values.
Results may differ from a plain program's by a relative error of at most 0.017.
Values may be sent and summed in bfloat16 or wider, within the bound.
No kernel may reach another device: no remote copies, remote signals or barrier semaphores. Data moves between devices by JAX's collectives and lax.ppermute only.
A program may use at most 128 MiB of HBM per device.

v0:
```python
import jax
import jax.numpy as jnp
from jax import lax
from jax.sharding import PartitionSpec as P

GROUPS = 32
CLASSES = 80
LAYERS = 4
LEVELS = 5
H3 = 16
W3 = 64


norm_epsilon = 1e-05


def convolve(values, kernel):
    return lax.conv_general_dilated(
        values,
        kernel,
        (1, 1),
        "SAME",
        dimension_numbers=("NHWC", "HWIO", "NHWC"),
        preferred_element_type=jnp.float32,
    )


def conv_back(out_grads, kernel):
    return convolve(out_grads, jnp.swapaxes(kernel[::-1, ::-1], 2, 3))


def kernel_grad(inputs, out_grads):
    grid_rows, grid_cols = (inputs.shape[1], inputs.shape[2])
    padded = jnp.pad(inputs, ((0, 0), (1, 1), (1, 1), (0, 0)))
    tap_terms = []
    for row_tap in range(3):
        for col_tap in range(3):
            window = padded[:, row_tap : row_tap + grid_rows, col_tap : col_tap + grid_cols]
            tap_terms.append(
                jnp.einsum("bhwc,bhwo->co", window, out_grads, preferred_element_type=jnp.float32)
            )
    return jnp.stack(tap_terms).reshape(3, 3, inputs.shape[3], out_grads.shape[3])


def group_act(pre_norm, gain, shift):
    batch, grid_rows, grid_cols, channels = pre_norm.shape
    grouped = pre_norm.reshape(batch, grid_rows * grid_cols, GROUPS, channels // GROUPS)
    center = jnp.mean(grouped, axis=(1, 3), keepdims=True)
    spread = jnp.mean(jnp.square(grouped - center), axis=(1, 3), keepdims=True)
    normed = ((grouped - center) * lax.rsqrt(spread + norm_epsilon)).reshape(pre_norm.shape)
    return jax.nn.silu(normed * gain + shift)


def level_slices(flat):
    pieces = []
    offset = 0
    for level_index in range(LEVELS):
        grid_rows = H3 // 2**level_index
        grid_cols = W3 // 2**level_index
        pieces.append(
            flat[:, offset : offset + grid_rows * grid_cols].reshape(
                flat.shape[0], grid_rows, grid_cols, flat.shape[2]
            )
        )
        offset = offset + grid_rows * grid_cols
    return pieces


def body(
    features,
    bn_mean,
    bn_var,
    tower_weight,
    norm_gain,
    norm_bias,
    head_weight,
    head_bias,
    level_scale,
    cls_cot,
    reg_cot,
    positive,
):
    whole = lax.all_gather(features, "tower", axis=2, tiled=True)
    inverse = lax.rsqrt(bn_var + norm_epsilon)
    base = ((whole.astype(jnp.float32) - bn_mean) * inverse).astype(jnp.bfloat16)
    kernels = tower_weight[0]
    gains = norm_gain[0]
    shifts = norm_bias[0]
    kept_inputs = []
    kept_norms = []
    activations = level_slices(base)
    for layer_index in range(LAYERS):
        pre_list = [convolve(level_act, kernels[layer_index]) for level_act in activations]
        kept_inputs.append(activations)
        kept_norms.append(pre_list)
        activations = [
            group_act(pre_norm, gains[layer_index], shifts[layer_index]).astype(jnp.bfloat16)
            for pre_norm in pre_list
        ]
    cls_levels = level_slices(cls_cot)
    reg_levels = level_slices(reg_cot)
    pos_levels = level_slices(positive[:, :, None])
    channels = whole.shape[2]

    def class_head(last_acts):
        class_kernel = head_weight[..., :CLASSES]
        backs = []
        weight_total = jnp.zeros((3, 3, channels, CLASSES), jnp.float32)
        bias_total = jnp.zeros((CLASSES,), jnp.float32)
        for level_index in range(LEVELS):
            head_grad = cls_levels[level_index]
            backs.append(conv_back(head_grad, class_kernel))
            weight_total = weight_total + kernel_grad(last_acts[level_index], head_grad)
            bias_total = bias_total + jnp.sum(head_grad.astype(jnp.float32), axis=(0, 1, 2))
        weight_full = jnp.concatenate(
            [weight_total, jnp.zeros((3, 3, channels, 5), jnp.float32)], axis=-1
        )
        bias_full = jnp.concatenate([bias_total, jnp.zeros((5,), jnp.float32)])
        return (backs, weight_full, bias_full, jnp.zeros((LEVELS,), jnp.float32))

    def box_head(last_acts):
        box_kernel = head_weight[..., CLASSES:]
        backs = []
        scale_terms = []
        weight_total = jnp.zeros((3, 3, channels, 5), jnp.float32)
        bias_total = jnp.zeros((5,), jnp.float32)
        for level_index in range(LEVELS):
            raw_out = convolve(last_acts[level_index], box_kernel) + head_bias[CLASSES:]
            distance = jnp.exp(level_scale[level_index] * raw_out[..., :4])
            masked = reg_levels[level_index].astype(jnp.float32) * pos_levels[level_index].astype(
                jnp.float32
            )
            weighted = masked[..., :4] * distance
            head_grad = jnp.concatenate(
                [weighted * level_scale[level_index], masked[..., 4:]], axis=-1
            ).astype(jnp.bfloat16)
            scale_terms.append(jnp.sum(weighted * raw_out[..., :4]))
            backs.append(conv_back(head_grad, box_kernel))
            weight_total = weight_total + kernel_grad(last_acts[level_index], head_grad)
            bias_total = bias_total + jnp.sum(head_grad.astype(jnp.float32), axis=(0, 1, 2))
        weight_full = jnp.concatenate(
            [jnp.zeros((3, 3, channels, CLASSES), jnp.float32), weight_total], axis=-1
        )
        bias_full = jnp.concatenate([jnp.zeros((CLASSES,), jnp.float32), bias_total])
        return (backs, weight_full, bias_full, jnp.stack(scale_terms))

    side_index = lax.axis_index("tower")
    act_grads, head_term, bias_term, scale_term = lax.cond(
        side_index == 0, class_head, box_head, activations
    )
    kernel_parts = [None] * LAYERS
    gain_parts = [None] * LAYERS
    shift_parts = [None] * LAYERS
    for layer_index in reversed(range(LAYERS)):
        kernel_total = jnp.zeros(kernels.shape[1:], jnp.float32)
        gain_total = jnp.zeros((channels,), jnp.float32)
        shift_total = jnp.zeros((channels,), jnp.float32)
        next_grads = []
        for level_index in range(LEVELS):
            _, pull = jax.vjp(
                group_act,
                kept_norms[layer_index][level_index],
                gains[layer_index],
                shifts[layer_index],
            )
            norm_grad, gain_grad, shift_grad = pull(act_grads[level_index])
            rounded = norm_grad.astype(jnp.bfloat16)
            kernel_total = kernel_total + kernel_grad(
                kept_inputs[layer_index][level_index], rounded
            )
            next_grads.append(conv_back(rounded, kernels[layer_index]))
            gain_total = gain_total + gain_grad
            shift_total = shift_total + shift_grad
        act_grads = next_grads
        kernel_parts[layer_index] = kernel_total
        gain_parts[layer_index] = gain_total
        shift_parts[layer_index] = shift_total
    kernel_sum, gain_sum, shift_sum = lax.psum(
        (jnp.stack(kernel_parts), jnp.stack(gain_parts), jnp.stack(shift_parts)), "dp"
    )
    head_sum, bias_sum, scale_sum = lax.psum((head_term, bias_term, scale_term), ("dp", "tower"))
    batch = whole.shape[0]
    flat_grad = jnp.concatenate(
        [level_grad.reshape(batch, -1, channels) for level_grad in act_grads], axis=1
    )
    own_grad = lax.psum_scatter(
        flat_grad.astype(jnp.bfloat16), "tower", scatter_dimension=2, tiled=True
    ).astype(jnp.float32)
    half_width = own_grad.shape[2]
    inverse_half = lax.dynamic_slice_in_dim(inverse, side_index * half_width, half_width)
    feature_grad = (own_grad * inverse_half).astype(jnp.bfloat16)
    return (
        feature_grad,
        kernel_sum[None],
        gain_sum[None],
        shift_sum[None],
        head_sum,
        bias_sum,
        scale_sum,
    )


def solution(mesh):
    return jax.shard_map(
        body,
        mesh=mesh,
        in_specs=(
            P("dp", None, "tower"),
            P(),
            P(),
            P("tower", None, None, None, None, None),
            P("tower", None, None),
            P("tower", None, None),
            P(),
            P(),
            P(),
            P("dp", None, None),
            P("dp", None, None),
            P("dp", None),
        ),
        out_specs=(
            P("dp", None, "tower"),
            P("tower", None, None, None, None, None),
            P("tower", None, None),
            P("tower", None, None),
            P(),
            P(),
            P(),
        ),
        check_vma=False,
    )
```

profile of v0, /device:TPU:0, one launch (start us, length us, event | category | flops | bytes accessed | tf_op | source)
XLA Modules:
  0.0 1175.8 jit_solution(4164299688515025002)
XLA Ops:
  8.7 2.6 all_gather.3
  13.0 4.8 slice_bitcast_fusion.18
  54.5 2.8 select_reduce_fusion.23
  60.2 3.3 select_reduce_fusion.20
  66.5 3.4 select_reduce_fusion.17
  82.1 1.9 select_bitcast_fusion.3
  84.1 4.4 select_reduce_fusion.14
  90.1 2.1 select_reduce_fusion.13
  96.4 2.3 add_divide_fusion
  103.1 2.4 reverse.18
  105.5 2.5 fusion.1683
  121.3 2.3 reverse.17
  123.6 2.4 fusion.1684
  139.3 2.5 reverse.16
  141.7 2.4 fusion.1685
  157.4 2.4 reverse.15
  159.8 2.4 fusion.1686
  175.5 2.2 fusion.1679
  186.9 2.1 fusion.1680
  202.2 2.8 fusion.1681
  218.4 2.9 fusion.1682
  239.2 66.7 %conditional.1 = (f32[1,16,64,256]{3,1,2,0:T(8,128)}, f32[1,8,32,256]{3,1,2,0:T(8,128)}, f32[1,4,16,256]{3,1,2,0:T(4,128)}, f32[1,1,4,256]{3,0,2,1:T(1,128)}, f3...) conditional(s32[]{:T(128)} %convert_element_type.469, ...), branch_computations={%region_80.91_spmd, %region_91.97_spmd} | conditional | flops 1052948608 | bytes 50544712 | solution.py:148
  244.2 1.9 fusion.35
  261.6 1.9 copy.870
  268.5 1.9 copy.871
  284.5 2.2 add_add_fusion
  292.8 1.9 reshape.6090
  294.8 2.1 copy.1003
  298.0 1.9 convolution_select_fusion
  305.9 1.9 multiply_reduce_fusion.25
  324.0 2.7 multiply_reduce_fusion.26
  342.7 2.7 multiply_reduce_fusion.27
  360.1 1.9 multiply_reduce_fusion.5
  375.1 1.9 multiply_reduce_fusion.6
  391.3 2.0 multiply_reduce_fusion.7
  411.1 2.0 multiply_reduce_fusion.8
  415.9 2.2 multiply_reduce_fusion.4
  434.7 3.1 select_reduce_fusion.58
  454.5 3.2 select_reduce_fusion.54
  478.5 2.1 multiply_reduce_fusion.3
  497.8 3.5 select_reduce_fusion.34
  516.5 1.9 select_bitcast_fusion.8
  518.4 3.5 select_reduce_fusion.30
  537.2 2.0 select_bitcast_fusion.7
  543.5 2.8 multiply_reduce_fusion.2
  555.8 1.9 fusion.1753
  558.1 5.2 select_reduce_fusion.10
  578.2 2.5 select_bitcast_fusion.2
  580.8 5.2 select_reduce_fusion.6
  589.8 3.4 select_reduce_fusion.26
  595.0 4.5 select_reduce_fusion.2
  607.1 3.1 select_reduce_fusion.50
  615.0 2.1 multiply_reduce_fusion.28
  624.5 1.9 convolution_convert_fusion.1
  627.7 2.9 convolution_convert_fusion
  631.0 3.2 copy.986
  634.3 2.5 copy.1415
  695.6 4.0 add_add_fusion.6
  703.2 2.4 add_add_fusion.4
  705.6 4.1 maximum_bitcast_fusion
  710.5 139.6 %all-reduce.34 = (f32[85]{0:T(128)}, f32[5]{0:T(128)}) all-reduce(f32[85]{0:T(128)} %get-tuple-element.108, f32[5]{0:T(128)} %get-tuple-element.109), channel_id=1, replica_groups=mesh['dp'=16,'tower'=2] {'dp','tower'}, use_global_device_ids=true, to_apply=%region_262.263 | all-reduce | flops 90 | bytes 720 | tf_op jit(solution)/shard_map/psum | solution.py:181
  851.1 42.8 %all-reduce.35 = (f32[1,4,256]{2,1,0:T(4,128)}, f32[1,4,256]{2,1,0:T(4,128)}) all-reduce(f32[1,4,256]{2,1,0:T(4,128)S(1)} %maximum_bitcast_fusion.1, f32[1,4,256]{2,1,0:T(4,128)S(1)} %maximum_bitcast_fusion.2), channel_id=1, replica_groups=mesh['dp'=16,'tower'=2] {'dp'}, use_global_device_ids=true, to_apply=%region_239.240 | all-reduce | flops 2048 | bytes 16384 | tf_op jit(solution)/shard_map/psum | solution.py:178
  897.1 261.6 %all-reduce.39.cloned.1.call-done = f32[1,4,3,3,256,256]{5,4,3,2,1,0:T(8,128)} async-done(((f32[1,4,3,3,256,256]{5,4,3,2,1,0:T(8,128)}), f32[1,4,3,3,256,256]{5,4,3,2,1,0:T(8,128)}) %all-reduce.39.cloned.1.call-update) | async-done | bytes 9437200 | tf_op jit(solution)/shard_map/psum | solution.py:178
  1158.7 8.5 copy.1687
  (1479 shorter events, 542.2 us)
Async XLA Ops:
  8.0 886.0 %reduce-scatter.4.cloned.1.call-start = ((), (), s32[]{:S(2)}) async-start(), calls=%async_computation.3 | async-start | bytes 1081344
  12.8 162.7 %copy-start.68 = (bf16[1,2,8,256]{3,2,1,0:T(8,128)(2,1)}, bf16[1,2,8,256]{3,2,1,0:T(8,128)(2,1)S(1)}, u32[]{:S(2)}) copy-start(bf16[1,2,8,256]{3,2,1,0:T(8,128)(2,1)S(1)} %slice_bitcast_fusion.40) | copy-start | bytes 24580
  12.8 21.6 %copy-start.77 = (bf16[1,256,256]{2,1,0:T(8,128)(2,1)}, bf16[1,256,256]{2,1,0:T(8,128)(2,1)S(1)}, u32[]{:S(2)}) copy-start(bf16[1,256,256]{2,1,0:T(8,128)(2,1)S(1)} %slice.1334) | copy-start | bytes 393220
  12.9 41.0 %copy-start.41 = (bf16[1,1024,256]{2,1,0:T(8,128)(2,1)}, bf16[1,1024,256]{2,1,0:T(8,128)(2,1)S(1)}, u32[]{:S(2)}) copy-start(bf16[1,1024,256]{2,1,0:T(8,128)(2,1)S(1)} %slice.1325) | copy-start | bytes 1572868
  17.7 28.5 %copy-start.113 = (f32[1,1,256]{2,1,0:T(1,128)}, f32[1,1,256]{2,1,0:T(1,128)S(1)}, u32[]{:S(2)}) copy-start(f32[1,1,256]{2,1,0:T(1,128)S(1)} %get-tuple-element.576) | copy-start | bytes 3076
  17.7 41.1 %copy-start.107 = (f32[1,1,256]{2,1,0:T(1,128)}, f32[1,1,256]{2,1,0:T(1,128)S(1)}, u32[]{:S(2)}) copy-start(f32[1,1,256]{2,1,0:T(1,128)S(1)} %get-tuple-element.575) | copy-start | bytes 3076
  17.8 47.4 %copy-start.110 = (f32[1,1,256]{2,1,0:T(1,128)}, f32[1,1,256]{2,1,0:T(1,128)S(1)}, u32[]{:S(2)}) copy-start(f32[1,1,256]{2,1,0:T(1,128)S(1)} %get-tuple-element.574) | copy-start | bytes 3076
  17.8 156.5 %copy-start.89 = (f32[1,1,256]{2,1,0:T(1,128)}, f32[1,1,256]{2,1,0:T(1,128)S(1)}, u32[]{:S(2)}) copy-start(f32[1,1,256]{2,1,0:T(1,128)S(1)} %get-tuple-element.573) | copy-start | bytes 3076
  17.8 28.4 %copy-start.134 = (f32[1,1,256]{2,1,0:T(1,128)}, f32[1,1,256]{2,1,0:T(1,128)S(1)}, u32[]{:S(2)}) copy-start(f32[1,1,256]{2,1,0:T(1,128)S(1)} %get-tuple-element.572) | copy-start | bytes 3076
  17.8 32.6 %copy-start.136 = (f32[1,1,256]{2,1,0:T(1,128)}, f32[1,1,256]{2,1,0:T(1,128)S(1)}, u32[]{:S(2)}) copy-start(f32[1,1,256]{2,1,0:T(1,128)S(1)} %get-tuple-element.569) | copy-start | bytes 3076
  17.8 41.1 %copy-start.130 = (f32[1,1,256]{2,1,0:T(1,128)}, f32[1,1,256]{2,1,0:T(1,128)S(1)}, u32[]{:S(2)}) copy-start(f32[1,1,256]{2,1,0:T(1,128)S(1)} %get-tuple-element.571) | copy-start | bytes 3076
  17.8 47.3 %copy-start.132 = (f32[1,1,256]{2,1,0:T(1,128)}, f32[1,1,256]{2,1,0:T(1,128)S(1)}, u32[]{:S(2)}) copy-start(f32[1,1,256]{2,1,0:T(1,128)S(1)} %get-tuple-element.570) | copy-start | bytes 3076
  69.9 18.6 %copy-start = (f32[16,8,9,256]{3,1,2,0:T(8,128)}, f32[16,8,9,256]{3,1,2,0:T(8,128)S(1)}, u32[]{:S(2)}) copy-start(f32[16,8,9,256]{3,1,2,0:T(8,128)S(1)} %get-tuple-element.582) | copy-start | bytes 3538948
  103.1 16.8 %copy-start.108 = (f32[1,1,256]{2,1,0:T(1,128)S(1)}, f32[1,1,256]{2,1,0:T(1,128)}, u32[]{:S(2)}) copy-start(f32[1,1,256]{2,1,0:T(1,128)} %copy-done.107) | copy-start | bytes 3076
  189.0 43.0 %copy-start.81 = (f32[1,2,8,256]{3,0,2,1:T(1,128)}, f32[1,2,8,256]{3,0,2,1:T(1,128)S(1)}, u32[]{:S(2)}) copy-start(f32[1,2,8,256]{3,0,2,1:T(1,128)S(1)} %get-tuple-element.604) | copy-start | bytes 49156
  305.9 54.2 %copy-start.82 = (f32[1,2,8,256]{3,0,2,1:T(1,128)S(1)}, f32[1,2,8,256]{3,0,2,1:T(1,128)}, u32[]{:S(2)}) copy-start(f32[1,2,8,256]{3,0,2,1:T(1,128)} %get-tuple-element.608) | copy-start | bytes 49156
  599.5 14.7 %copy-start.129 = (f32[1,1,4,256]{3,0,2,1:T(1,128)S(1)}, f32[1,1,4,256]{3,0,2,1:T(1,128)}, u32[]{:S(2)}) copy-start(f32[1,1,4,256]{3,0,2,1:T(1,128)} %get-tuple-element.612) | copy-start | bytes 12292
  599.5 15.4 %copy-start.128 = (f32[1,1,4,256]{3,0,2,1:T(1,128)S(1)}, f32[1,1,4,256]{3,0,2,1:T(1,128)}, u32[]{:S(2)}) copy-start(f32[1,1,4,256]{3,0,2,1:T(1,128)} %get-tuple-element.610) | copy-start | bytes 12292
  599.5 15.4 %copy-start.154 = (f32[256]{0:T(256)S(1)}, f32[256]{0:T(256)}, u32[]{:S(2)}) copy-start(f32[256]{0:T(256)} %sub.1000) | copy-start | bytes 3076
  599.5 15.4 %copy-start.197 = (f32[256]{0:T(256)S(1)}, f32[256]{0:T(256)}, u32[]{:S(2)}) copy-start(f32[256]{0:T(256)} %mul.2651) | copy-start | bytes 3076
  599.5 15.4 %copy-start.228 = (f32[1,1,4,256]{3,0,2,1:T(1,128)S(1)}, f32[1,1,4,256]{3,0,2,1:T(1,128)}, u32[]{:S(2)}) copy-start(f32[1,1,4,256]{3,0,2,1:T(1,128)} %get-tuple-element.464) | copy-start | bytes 12292
  599.5 15.4 %copy-start.229 = (f32[1,1,4,256]{3,0,2,1:T(1,128)S(1)}, f32[1,1,4,256]{3,0,2,1:T(1,128)}, u32[]{:S(2)}) copy-start(f32[1,1,4,256]{3,0,2,1:T(1,128)} %get-tuple-element.465) | copy-start | bytes 12292
  601.2 15.8 %copy-start.206 = (f32[256]{0:T(256)}, f32[256]{0:T(256)S(1)}, u32[]{:S(2)}) copy-start(f32[256]{0:T(256)S(1)} %mul.2732) | copy-start | bytes 3076
  636.8 260.4 %all-reduce.41.cloned.1.call-start = ((), (), s32[]{:S(2)}) async-start(), calls=%async_computation.2 | async-start | bytes 1622016 | tf_op jit(solution)/shard_map/psum | solution.py:181
  637.4 521.4 %all-reduce.39.cloned.1.call-start = ((), (), s32[]{:S(2)}) async-start(), calls=%async_computation.1 | async-start | bytes 18874368 | tf_op jit(solution)/shard_map/psum | solution.py:178
  709.7 140.3 %copy-start.218 = (f32[256]{0:T(256)S(1)}, f32[256]{0:T(256)}, u32[]{:S(2)}) copy-start(f32[256]{0:T(256)} %get-tuple-element.367) | copy-start | bytes 3076
  709.7 140.3 %copy-start.219 = (f32[256]{0:T(256)S(1)}, f32[256]{0:T(256)}, u32[]{:S(2)}) copy-start(f32[256]{0:T(256)} %get-tuple-element.379) | copy-start | bytes 3076
  709.7 140.3 %copy-start.254 = (f32[256]{0:T(256)S(1)}, f32[256]{0:T(256)}, u32[]{:S(2)}) copy-start(f32[256]{0:T(256)} %get-tuple-element.335) | copy-start | bytes 3076
  709.7 140.3 %copy-start.255 = (f32[256]{0:T(256)S(1)}, f32[256]{0:T(256)}, u32[]{:S(2)}) copy-start(f32[256]{0:T(256)} %get-tuple-element.344) | copy-start | bytes 3076
  709.7 140.3 %copy-start.256 = (f32[256]{0:T(256)S(1)}, f32[256]{0:T(256)}, u32[]{:S(2)}) copy-start(f32[256]{0:T(256)} %get-tuple-element.319) | copy-start | bytes 3076
  709.8 140.3 %copy-start.257 = (f32[256]{0:T(256)S(1)}, f32[256]{0:T(256)}, u32[]{:S(2)}) copy-start(f32[256]{0:T(256)} %get-tuple-element.328) | copy-start | bytes 3076
  709.8 140.3 %copy-start.258 = (f32[256]{0:T(256)S(1)}, f32[256]{0:T(256)}, u32[]{:S(2)}) copy-start(f32[256]{0:T(256)} %get-tuple-element.351) | copy-start | bytes 3076
  709.8 140.3 %copy-start.259 = (f32[256]{0:T(256)S(1)}, f32[256]{0:T(256)}, u32[]{:S(2)}) copy-start(f32[256]{0:T(256)} %get-tuple-element.360) | copy-start | bytes 3076
  709.8 140.3 %copy-start.260 = (f32[256]{0:T(256)S(1)}, f32[256]{0:T(256)}, u32[]{:S(2)}) copy-start(f32[256]{0:T(256)} %get-tuple-element.383) | copy-start | bytes 3076
  709.8 140.9 %copy-start.214 = (f32[256]{0:T(256)S(1)}, f32[256]{0:T(256)}, u32[]{:S(2)}) copy-start(f32[256]{0:T(256)} %get-tuple-element.369) | copy-start | bytes 3076
  709.8 140.9 %copy-start.215 = (f32[256]{0:T(256)S(1)}, f32[256]{0:T(256)}, u32[]{:S(2)}) copy-start(f32[256]{0:T(256)} %get-tuple-element.380) | copy-start | bytes 3076
  709.8 140.9 %copy-start.240 = (f32[256]{0:T(256)S(1)}, f32[256]{0:T(256)}, u32[]{:S(2)}) copy-start(f32[256]{0:T(256)} %get-tuple-element.385) | copy-start | bytes 3076
  709.8 140.9 %copy-start.241 = (f32[256]{0:T(256)S(1)}, f32[256]{0:T(256)}, u32[]{:S(2)}) copy-start(f32[256]{0:T(256)} %get-tuple-element.396) | copy-start | bytes 3076
  709.8 140.9 %copy-start.244 = (f32[256]{0:T(256)S(1)}, f32[256]{0:T(256)}, u32[]{:S(2)}) copy-start(f32[256]{0:T(256)} %get-tuple-element.353) | copy-start | bytes 3076
  709.8 140.9 %copy-start.245 = (f32[256]{0:T(256)S(1)}, f32[256]{0:T(256)}, u32[]{:S(2)}) copy-start(f32[256]{0:T(256)} %get-tuple-element.361) | copy-start | bytes 3076
  709.9 140.9 %copy-start.248 = (f32[256]{0:T(256)S(1)}, f32[256]{0:T(256)}, u32[]{:S(2)}) copy-start(f32[256]{0:T(256)} %get-tuple-element.337) | copy-start | bytes 3076
  709.9 140.9 %copy-start.249 = (f32[256]{0:T(256)S(1)}, f32[256]{0:T(256)}, u32[]{:S(2)}) copy-start(f32[256]{0:T(256)} %get-tuple-element.345) | copy-start | bytes 3076
  709.9 140.9 %copy-start.252 = (f32[256]{0:T(256)S(1)}, f32[256]{0:T(256)}, u32[]{:S(2)}) copy-start(f32[256]{0:T(256)} %get-tuple-element.321) | copy-start | bytes 3076
  709.9 140.9 %copy-start.253 = (f32[256]{0:T(256)S(1)}, f32[256]{0:T(256)}, u32[]{:S(2)}) copy-start(f32[256]{0:T(256)} %get-tuple-element.329) | copy-start | bytes 3076
  709.9 141.0 %copy-start.212 = (f32[256]{0:T(256)S(1)}, f32[256]{0:T(256)}, u32[]{:S(2)}) copy-start(f32[256]{0:T(256)} %get-tuple-element.371) | copy-start | bytes 3076
  709.9 141.0 %copy-start.213 = (f32[256]{0:T(256)S(1)}, f32[256]{0:T(256)}, u32[]{:S(2)}) copy-start(f32[256]{0:T(256)} %get-tuple-element.381) | copy-start | bytes 3076
  709.9 141.0 %copy-start.238 = (f32[256]{0:T(256)S(1)}, f32[256]{0:T(256)}, u32[]{:S(2)}) copy-start(f32[256]{0:T(256)} %get-tuple-element.387) | copy-start | bytes 3076
  709.9 141.0 %copy-start.239 = (f32[256]{0:T(256)S(1)}, f32[256]{0:T(256)}, u32[]{:S(2)}) copy-start(f32[256]{0:T(256)} %get-tuple-element.397) | copy-start | bytes 3076
  709.9 141.0 %copy-start.242 = (f32[256]{0:T(256)S(1)}, f32[256]{0:T(256)}, u32[]{:S(2)}) copy-start(f32[256]{0:T(256)} %get-tuple-element.355) | copy-start | bytes 3076
  709.9 141.0 %copy-start.243 = (f32[256]{0:T(256)S(1)}, f32[256]{0:T(256)}, u32[]{:S(2)}) copy-start(f32[256]{0:T(256)} %get-tuple-element.362) | copy-start | bytes 3076
  710.0 141.0 %copy-start.246 = (f32[256]{0:T(256)S(1)}, f32[256]{0:T(256)}, u32[]{:S(2)}) copy-start(f32[256]{0:T(256)} %get-tuple-element.339) | copy-start | bytes 3076
  710.0 141.0 %copy-start.247 = (f32[256]{0:T(256)S(1)}, f32[256]{0:T(256)}, u32[]{:S(2)}) copy-start(f32[256]{0:T(256)} %get-tuple-element.346) | copy-start | bytes 3076
  710.0 141.0 %copy-start.250 = (f32[256]{0:T(256)S(1)}, f32[256]{0:T(256)}, u32[]{:S(2)}) copy-start(f32[256]{0:T(256)} %get-tuple-element.323) | copy-start | bytes 3076
  710.0 141.0 %copy-start.251 = (f32[256]{0:T(256)S(1)}, f32[256]{0:T(256)}, u32[]{:S(2)}) copy-start(f32[256]{0:T(256)} %get-tuple-element.330) | copy-start | bytes 3076
  710.0 141.0 %copy-start.210 = (f32[256]{0:T(256)S(1)}, f32[256]{0:T(256)}, u32[]{:S(2)}) copy-start(f32[256]{0:T(256)} %get-tuple-element.373) | copy-start | bytes 3076
  710.0 141.0 %copy-start.211 = (f32[256]{0:T(256)S(1)}, f32[256]{0:T(256)}, u32[]{:S(2)}) copy-start(f32[256]{0:T(256)} %get-tuple-element.382) | copy-start | bytes 3076
  710.0 141.0 %copy-start.216 = (f32[256]{0:T(256)S(1)}, f32[256]{0:T(256)}, u32[]{:S(2)}) copy-start(f32[256]{0:T(256)} %get-tuple-element.365) | copy-start | bytes 3076
  710.0 141.0 %copy-start.217 = (f32[256]{0:T(256)S(1)}, f32[256]{0:T(256)}, u32[]{:S(2)}) copy-start(f32[256]{0:T(256)} %get-tuple-element.366) | copy-start | bytes 3076
  710.0 141.0 %copy-start.220 = (f32[256]{0:T(256)S(1)}, f32[256]{0:T(256)}, u32[]{:S(2)}) copy-start(f32[256]{0:T(256)} %get-tuple-element.349) | copy-start | bytes 3076
  710.0 141.0 %copy-start.221 = (f32[256]{0:T(256)S(1)}, f32[256]{0:T(256)}, u32[]{:S(2)}) copy-start(f32[256]{0:T(256)} %get-tuple-element.350) | copy-start | bytes 3076
  710.1 141.0 %copy-start.226 = (f32[256]{0:T(256)S(1)}, f32[256]{0:T(256)}, u32[]{:S(2)}) copy-start(f32[256]{0:T(256)} %get-tuple-element.389) | copy-start | bytes 3076
  710.1 141.0 %copy-start.227 = (f32[256]{0:T(256)S(1)}, f32[256]{0:T(256)}, u32[]{:S(2)}) copy-start(f32[256]{0:T(256)} %get-tuple-element.398) | copy-start | bytes 3076
  710.1 141.0 %copy-start.235 = (f32[256]{0:T(256)S(1)}, f32[256]{0:T(256)}, u32[]{:S(2)}) copy-start(f32[256]{0:T(256)} %get-tuple-element.333) | copy-start | bytes 3076
  710.1 141.0 %copy-start.236 = (f32[256]{0:T(256)S(1)}, f32[256]{0:T(256)}, u32[]{:S(2)}) copy-start(f32[256]{0:T(256)} %get-tuple-element.334) | copy-start | bytes 3076
  (199 other events, 792.9 us)
Sparse Core Ops, SparseCore 0:
  636.9 109.2 reduce-scatter.3
Sparse Core Ops, SparseCore 1:
  643.9 228.5 all-reduce.40
  880.1 278.6 all-reduce.38
where the time goes:
time: 1200 us; the launch traced here: 1180 us
  local copies, waits for them, and re-layouts  290 us (24%)
  waiting for transfers between devices  262 us (22%)
  other arithmetic  236 us (20%)
  blocking collectives  185 us (15%)
  matrix products  180 us (15%)
  between operations  21.7 us (2%)
    psum x1, waiting for transfers between devices, body(): lax.psum((jnp.stack(kernel_parts), jnp.stack(gain_parts), jnp.stack(shift...  262 us
    psum x1, blocking collectives, body(): lax.psum((head_term, bias_term, scale_term), ('dp', 'tower'))  140 us
    conv_general_dilated x45, matrix products, convolve(): lax.conv_general_dilated(values, kernel, (1, 1), 'SAME', dimension_number...  108 us
    dot_general x200, matrix products, kernel_grad(): jnp.einsum('bhwc,bhwo->co', window, out_grads, preferred_element_type=jnp...  71.9 us
    reduce_sum x80, other arithmetic, group_act(): spread = jnp.mean(jnp.square(grouped - center), axis=(1, 3), keepdims=True)  68.8 us
    psum x1, blocking collectives, body(): lax.psum((jnp.stack(kernel_parts), jnp.stack(gain_parts), jnp.stack(shift...  42.8 us
    unnamed x531, local copies, waits for them, and re-layouts  38.4 us
    mul x43, local copies, waits for them, and re-layouts, group_act(): spread = jnp.mean(jnp.square(grouped - center), axis=(1, 3), keepdims=True)  31.9 us
  transfers between devices with their start and end apart: 3, of which 1 were waited for; matrix products, arithmetic and copies ran while one was open for 6% of the time, Pallas kernels for 0%

commit v1 on v0

v1 whole, which is shorter than its diff:
```python
import functools

import jax
import jax.numpy as jnp
from jax import lax
from jax.experimental import pallas as pl
from jax.experimental.pallas import tpu as pltpu
from jax.sharding import PartitionSpec as P

C = 256
GROUP = 8
CLASSES = 80
HEAD = 85
LANES = 128
LAYERS = 4
CELLS = 1408
PIX = 1364
COUNTS = (1024, 256, 64, 16, 4)
PARTS = ((0, 1024, 64, 64), (1024, 256, 1152, 32), (1280, 128, 1440, 16))
PADDED = 1584
GAPS = ((0, 64), (1088, 64), (1408, 32), (1568, 16))
TILE = 64
EPS = 1e-05
f32 = jnp.float32
bf16 = jnp.bfloat16
VMEM = pl.BlockSpec(memory_space=pltpu.VMEM)
SMEM = pl.BlockSpec(memory_space=pltpu.SMEM)
ANY = pl.BlockSpec(memory_space=pl.ANY)


def params():
    return pltpu.CompilerParams(vmem_limit_bytes=56 << 20)


def tail_masks():
    row = lax.broadcasted_iota(jnp.int32, (TILE, C), 0)
    third = ((row >= 16) & (row < 24)) | ((row >= 32) & (row < 40))
    fourth = (row >= 26) & (row < 30)
    return third, fourth


def pick(third, fourth, vec):
    return jnp.where(third, vec[3:4], jnp.where(fourth, vec[4:5], 0.0))


def fold(tile):
    return jnp.sum(tile.reshape(TILE // 8, 8, tile.shape[1]), axis=0)


def group_sum(vec):
    lane = lax.broadcasted_iota(jnp.int32, vec.shape, 1)
    for step in (1, 2, 4):
        up = pltpu.roll(vec, vec.shape[1] - step, 1)
        down = pltpu.roll(vec, step, 1)
        vec = vec + jnp.where((lane & step) == 0, up, down)
    return vec


def counts_column():
    row = lax.broadcasted_iota(jnp.int32, (8, C), 0)
    out = jnp.full((8, C), 1.0, f32)
    for level, cells in enumerate(COUNTS):
        out = jnp.where(row == level, 1.0 / (cells * GROUP), out)
    return out


def stack_rows(rows):
    row = lax.broadcasted_iota(jnp.int32, (8, rows[0].shape[1]), 0)
    out = jnp.zeros((8, rows[0].shape[1]), f32)
    for place, value in enumerate(rows):
        out = jnp.where(row == place, jnp.sum(value, axis=0, keepdims=True), out)
    return out


def each_tile(step, init):
    results = []
    for level, (tiles, cell, row, width) in enumerate(((16, 0, 64, 64), (4, 1024, 1152, 32), (1, 1280, 1440, 16))):
        carry = init

        def run(i, carry, level=level, cell=cell, row=row, width=width):
            at = pl.multiple_of(i * TILE, TILE)
            return step(level, cell + at, row + at, width, carry)

        if tiles == 1:
            carry = step(level, cell, row, width, carry)
        else:
            carry = lax.fori_loop(0, tiles, run, carry, unroll=2)
        results.append(carry)
    results.append(step(3, 1344, 1504, 16, init))
    return results


def write_shifted(buf, row, width, tile, lanes, flip):
    at = lax.broadcasted_iota(jnp.int32, tile.shape, 0) & (width - 1)
    before = jnp.where(at == 0, 0.0, pltpu.roll(tile, 1, 0))
    after = jnp.where(at == width - 1, 0.0, pltpu.roll(tile, TILE - 1, 0))
    if flip:
        before, after = after, before
    rows = pl.ds(row, TILE)
    buf[rows, 0:lanes] = before.astype(bf16)
    buf[rows, lanes : 2 * lanes] = tile.astype(bf16)
    buf[rows, 2 * lanes : 3 * lanes] = after.astype(bf16)


def clear_gaps(buf):
    for row, rows in GAPS:
        buf[row : row + rows, :] = jnp.zeros((rows, buf.shape[1]), bf16)


def conv_into(out, buf, weight, lanes):
    for cell, cells, row, width in PARTS:
        for first in range(0, cells, 256):
            size = min(256, cells - first)
            at = row + first
            left = jnp.concatenate([buf[at + d * width : at + d * width + size, :] for d in (-1, 0, 1)], axis=1)
            out[cell + first : cell + first + size, :] = jnp.dot(left, weight, preferred_element_type=f32)


def conv_back_into(out, buf, weight, lanes):
    for cell, cells, row, width in PARTS:
        for first in range(0, cells, 256):
            size = min(256, cells - first)
            total = None
            for i in range(3):
                at = row + first - (i - 1) * width
                for j in range(3):
                    term = lax.dot_general(
                        buf[at : at + size, j * lanes : (j + 1) * lanes],
                        weight(i * 3 + j),
                        (((1,), (1,)), ((), ())),
                        preferred_element_type=f32,
                    )
                    total = term if total is None else total + term
            out[cell + first : cell + first + size, :] = total


def kernel_grad(turned, buf, i):
    total = None
    for cell, cells, row, width in PARTS:
        at = row - (i - 1) * width
        term = jnp.dot(turned[:, cell : cell + cells], buf[at : at + cells, :], preferred_element_type=f32)
        total = term if total is None else total + term
    return total


def norm_stats(z):
    third, fourth = tail_masks()

    def sums(level, cell, row, width, carry):
        tile = z[pl.ds(cell, TILE), :]
        if level < 3:
            return carry + fold(tile)
        return (fold(jnp.where(third, tile, 0.0)), fold(jnp.where(fourth, tile, 0.0)))

    zero = jnp.zeros((8, C), f32)
    inv_counts = counts_column()
    r = each_tile(sums, zero)
    mean = group_sum(stack_rows([r[0], r[1], r[2], r[3][0], r[3][1]])) * inv_counts

    def squares(level, cell, row, width, carry):
        tile = z[pl.ds(cell, TILE), :]
        if level < 3:
            d = tile - mean[level : level + 1]
            return carry + fold(d * d)
        d3 = jnp.where(third, tile - mean[3:4], 0.0)
        d4 = jnp.where(fourth, tile - mean[4:5], 0.0)
        return (fold(d3 * d3), fold(d4 * d4))

    r = each_tile(squares, zero)
    var = group_sum(stack_rows([r[0], r[1], r[2], r[3][0], r[3][1]])) * inv_counts
    return mean, lax.rsqrt(var + EPS)


def forward_act(z, mean, rstd, gain, shift, buf):
    scale = rstd * gain
    offset = shift - mean * scale
    third, fourth = tail_masks()

    def act(level, cell, row, width, carry):
        tile = z[pl.ds(cell, TILE), :]
        if level < 3:
            y = tile * scale[level : level + 1] + offset[level : level + 1]
        else:
            y = tile * pick(third, fourth, scale) + pick(third, fourth, offset)
        a = y * (0.5 * jnp.tanh(0.5 * y) + 0.5)
        if level == 3:
            a = jnp.where(third | fourth, a, 0.0)
        write_shifted(buf, row, width, a, C, False)
        return carry

    each_tile(act, jnp.int32(0))


def backward_norm(da, z, mean, rstd, gain, shift, buf):
    third, fourth = tail_masks()
    neg = -mean * rstd
    zero = jnp.zeros((8, C), f32)

    def rows(level, vec):
        if level < 3:
            return vec[level : level + 1]
        return pick(third, fourth, vec)

    def first(level, cell, row, width, carry):
        zhat = z[pl.ds(cell, TILE), :] * rows(level, rstd) + rows(level, neg)
        y = zhat * gain + shift
        s = 0.5 * jnp.tanh(0.5 * y) + 0.5
        dy = da[pl.ds(cell, TILE), :] * (s * (1.0 + y * (1.0 - s)))
        da[pl.ds(cell, TILE), :] = dy
        dyz = dy * zhat
        if level < 3:
            return (carry[0] + fold(dy), carry[1] + fold(dyz))
        return tuple(fold(jnp.where(m, v, 0.0)) for v in (dy, dyz) for m in (third, fourth))

    r = each_tile(first, (zero, zero))
    sum_dy = stack_rows([r[0][0], r[1][0], r[2][0], r[3][0], r[3][1]])
    sum_dyz = stack_rows([r[0][1], r[1][1], r[2][1], r[3][2], r[3][3]])
    inv_counts = counts_column()
    mean_e = group_sum(sum_dy * gain) * inv_counts
    mean_ez = group_sum(sum_dyz * gain) * inv_counts
    on_dy = rstd * gain
    on_zhat = rstd * mean_ez
    on_z = -on_zhat * rstd
    flat = -rstd * mean_e - on_zhat * neg

    def second(level, cell, row, width, carry):
        dz = (
            da[pl.ds(cell, TILE), :] * rows(level, on_dy)
            + z[pl.ds(cell, TILE), :] * rows(level, on_z)
            + rows(level, flat)
        )
        write_shifted(buf, row, width, dz, C, True)
        return carry

    each_tile(second, jnp.int32(0))
    return jnp.sum(sum_dyz, axis=0, keepdims=True), jnp.sum(sum_dy, axis=0, keepdims=True)


def center(buf, cell, cells, row, lanes):
    return buf[row : row + cells, lanes : 2 * lanes]


def layer_back(da, z, a, stats, gain, shift, weight, buf, turned, dw, vec):
    turned[...] = a.T
    dgain, dshift = backward_norm(da, z, stats[0:8], stats[8:16], gain, shift, buf)
    row = lax.broadcasted_iota(jnp.int32, (8, C), 0)
    vec[...] = jnp.where(row == 0, dgain, jnp.where(row == 1, dshift, 0.0))
    for i in range(3):
        grad = kernel_grad(turned, buf, i).astype(bf16)
        for j in range(3):
            dw[i * 3 + j] = grad[:, j * C : (j + 1) * C]
    conv_back_into(da, buf, lambda tap: weight[tap * C : (tap + 1) * C, :], C)


def first_kernel(
    tower, scale, x, bn, w_hbm, gains, shifts, head, head_bias, cot,
    z_out, a_out, stats_out, da_out, dw_out, vec_out, dhead_out, hvec_out,
    w, buf, zs, hw, hg, hbuf, u, turned, sems,
):
    loads = [pltpu.make_async_copy(w_hbm.at[l], w.at[l], sems.at[l]) for l in range(LAYERS)]
    for load in loads:
        load.start()
    clear_gaps(buf)
    clear_gaps(hbuf)
    hw[...] = jnp.zeros(hw.shape, bf16)
    hw[:, 0:HEAD] = head[...]
    inverse = lax.rsqrt(bn[8:9] + EPS)
    mean0 = bn[0:1]

    def base(level, cell, row, width, carry):
        tile = (x[pl.ds(cell, TILE), :].astype(f32) - mean0) * inverse
        if level == 3:
            third, fourth = tail_masks()
            tile = jnp.where(third | fourth, tile, 0.0)
        write_shifted(buf, row, width, tile, C, False)
        return carry

    each_tile(base, jnp.int32(0))
    stats = None
    for l in range(LAYERS):
        if l < LAYERS - 1:
            for cell, cells, row, width in PARTS:
                a_out[l, cell : cell + cells, :] = center(buf, cell, cells, row, C)
        else:
            for cell, cells, row, width in PARTS:
                turned[:, cell : cell + cells] = center(buf, cell, cells, row, C).T
        loads[l].wait()
        z = zs.at[...] if l == LAYERS - 1 else z_out.at[l]
        conv_into(z, buf, w[l], C)
        mean, rstd = norm_stats(z)
        if l < LAYERS - 1:
            stats_out[l, 0:8, :] = mean
            stats_out[l, 8:16, :] = rstd
        else:
            stats = jnp.concatenate([mean, rstd], axis=0)
        forward_act(z, mean, rstd, gains[l : l + 1], shifts[l : l + 1], buf)

    hvec_out[...] = jnp.zeros(hvec_out.shape, f32)
    for cell in range(0, CELLS, TILE):
        hg[cell : cell + TILE, :] = cot[cell : cell + TILE, :].astype(f32)

    @pl.when(tower[0] == 1)
    def _():
        conv_into(u, buf, hw[...], C)
        lane = lax.broadcasted_iota(jnp.int32, (TILE, LANES), 1)
        dist_lane = (lane >= CLASSES) & (lane < CLASSES + 4)
        row = lax.broadcasted_iota(jnp.int32, (TILE, LANES), 0)
        third = ((row >= 16) & (row < 24)) | ((row >= 32) & (row < 40))
        fourth = (row >= 26) & (row < 30)

        def box(level, cell, row, width, carry):
            raw = u[pl.ds(cell, TILE), :] + head_bias[...]
            g = hg[pl.ds(cell, TILE), :]
            if level < 3:
                ls = scale[level]
                use = dist_lane
            else:
                ls = jnp.where(third, scale[3], scale[4])
                use = dist_lane & (third | fourth)
            weighted = jnp.where(use, g * jnp.exp(ls * raw), 0.0)
            hg[pl.ds(cell, TILE), :] = jnp.where(dist_lane, weighted * ls, g)
            term = weighted * raw
            if level < 3:
                return carry + fold(term)
            return (fold(jnp.where(third, term, 0.0)), fold(jnp.where(fourth, term, 0.0)))

        r = each_tile(box, jnp.zeros((8, LANES), f32))
        hvec_out[0:8, :] = stack_rows([r[0], r[1], r[2], r[3][0], r[3][1]])

    def head_rows(level, cell, row, width, carry):
        tile = hg[pl.ds(cell, TILE), :].astype(bf16).astype(f32)
        write_shifted(hbuf, row, width, tile, LANES, True)
        return carry + fold(tile)

    r = each_tile(head_rows, jnp.zeros((8, LANES), f32))
    total = jnp.sum(r[0] + r[1] + r[2] + r[3], axis=0, keepdims=True)
    hvec_out[8:16, :] = jnp.where(lax.broadcasted_iota(jnp.int32, (8, LANES), 0) == 0, total, 0.0)

    a4t = jnp.concatenate([center(buf, c, n, r, C).T for c, n, r, _ in PARTS], axis=1)
    for i in range(3):
        grad = kernel_grad(a4t, hbuf, i).astype(bf16)
        for j in range(3):
            dhead_out[i * 3 + j] = grad[:, j * LANES : (j + 1) * LANES]
    conv_back_into(da_out, hbuf, lambda tap: hw[tap * C : (tap + 1) * C, :], LANES)

    l = LAYERS - 1
    dgain, dshift = backward_norm(da_out, zs, stats[0:8], stats[8:16], gains[l : l + 1], shifts[l : l + 1], buf)
    row = lax.broadcasted_iota(jnp.int32, (8, C), 0)
    vec_out[...] = jnp.where(row == 0, dgain, jnp.where(row == 1, dshift, 0.0))
    for i in range(3):
        grad = kernel_grad(turned, buf, i).astype(bf16)
        for j in range(3):
            dw_out[i * 3 + j] = grad[:, j * C : (j + 1) * C]
    conv_back_into(da_out, buf, lambda tap: w[l, tap * C : (tap + 1) * C, :], C)


def middle_kernel(l, da_in, z, a, stats, gains, shifts, w, da_out, dw_out, vec_out, buf, turned):
    clear_gaps(buf)
    da_out[...] = da_in[...]
    layer_back(
        da_out, z.at[0], a[0], stats[0], gains[l : l + 1], shifts[l : l + 1], w.at[0], buf, turned, dw_out, vec_out
    )


def shape(dims, dtype):
    return jax.ShapeDtypeStruct(dims, dtype)


def run_first(tower, scale, x, bn, w, gains, shifts, head, head_bias, cot):
    return pl.pallas_call(
        first_kernel,
        out_shape=[
            shape((LAYERS - 1, CELLS, C), f32),
            shape((LAYERS - 1, CELLS, C), bf16),
            shape((LAYERS - 1, 16, C), f32),
            shape((CELLS, C), f32),
            shape((9, C, C), bf16),
            shape((8, C), f32),
            shape((9, C, LANES), bf16),
            shape((16, LANES), f32),
        ],
        in_specs=[SMEM, SMEM, VMEM, VMEM, ANY, VMEM, VMEM, VMEM, VMEM, VMEM],
        out_specs=[VMEM] * 8,
        scratch_shapes=[
            pltpu.VMEM((LAYERS, 9 * C, C), bf16),
            pltpu.VMEM((PADDED, 3 * C), bf16),
            pltpu.VMEM((CELLS, C), f32),
            pltpu.VMEM((9 * C, LANES), bf16),
            pltpu.VMEM((CELLS, LANES), f32),
            pltpu.VMEM((PADDED, 3 * LANES), bf16),
            pltpu.VMEM((CELLS, LANES), f32),
            pltpu.VMEM((C, CELLS), bf16),
            pltpu.SemaphoreType.DMA((LAYERS,)),
        ],
        compiler_params=params(),
        name="forward_and_heads",
    )(tower, scale, x, bn, w, gains, shifts, head, head_bias, cot)


def run_middle(l, da, z, a, stats, gains, shifts, w):
    one = lambda dims: pl.BlockSpec((1,) + dims, lambda i: (l,) + (0,) * len(dims))
    whole = lambda dims: pl.BlockSpec(dims, lambda i: (0,) * len(dims))
    return pl.pallas_call(
        functools.partial(middle_kernel, l),
        grid=(1,),
        out_shape=[shape((CELLS, C), f32), shape((9, C, C), bf16), shape((8, C), f32)],
        in_specs=[
            whole((CELLS, C)),
            one((CELLS, C)),
            one((CELLS, C)),
            one((16, C)),
            whole((LAYERS, C)),
            whole((LAYERS, C)),
            one((9 * C, C)),
        ],
        out_specs=[whole((CELLS, C)), whole((9, C, C)), whole((8, C))],
        scratch_shapes=[pltpu.VMEM((PADDED, 3 * C), bf16), pltpu.VMEM((C, CELLS), bf16)],
        compiler_params=params(),
        name=f"layer_gradients_{l}",
    )(da, z, a, stats, gains, shifts, w)


def to_cells(flat):
    gap = lambda rows: jnp.zeros((rows, flat.shape[1]), flat.dtype)
    return jnp.concatenate(
        [flat[:1344], gap(16), flat[1344:1352], gap(2), flat[1360:1364], gap(2), flat[1352:1360], gap(24)], axis=0
    )


def to_flat(cells):
    return jnp.concatenate([cells[:1344], cells[1360:1368], cells[1376:1384], cells[1370:1374]], axis=0)


def body(
    features, bn_mean, bn_var, tower_weight, norm_gain, norm_bias, head_weight, head_bias, level_scale,
    cls_cot, reg_cot, positive, *, dp,
):
    tower = lax.axis_index("tower")
    whole = lax.all_gather(features, "tower", axis=2, tiled=True)[0]
    x = to_cells(whole)
    cls = jnp.where(tower == 0, cls_cot[0], 0)
    box = jnp.where((tower == 1) & (positive[0] == 1)[:, None], reg_cot[0], 0)
    cot = to_cells(jnp.concatenate([cls, box, jnp.zeros((PIX, LANES - HEAD), bf16)], axis=1))
    bn = jnp.concatenate([jnp.broadcast_to(bn_mean, (8, C)), jnp.broadcast_to(bn_var, (8, C))], axis=0)
    w = tower_weight[0].reshape(LAYERS, 9 * C, C)
    bias = jnp.pad(head_bias, (0, LANES - HEAD))[None]
    gains, shifts = norm_gain[0], norm_bias[0]
    z, a, stats, da, dw3, vec3, dhead, hvec = run_first(
        tower.reshape(1), level_scale, x, bn, w, gains, shifts, head_weight.reshape(9 * C, HEAD), bias, cot
    )
    dws, vecs = [None] * LAYERS, [None] * LAYERS
    dws[3], vecs[3] = dw3, vec3
    for l in (2, 1, 0):
        da, dws[l], vecs[l] = run_middle(l, da, z, a, stats, gains, shifts, w)

    kernel_sum = lax.psum(jnp.stack(dws), "dp").astype(f32).reshape(1, LAYERS, 3, 3, C, C)
    vec_sum = lax.psum(jnp.stack(vecs), "dp")
    head_sum, hvec_sum = lax.psum((dhead, hvec), ("dp", "tower"))
    grad = lax.psum_scatter(to_flat(da).astype(bf16), "tower", scatter_dimension=1, tiled=True).astype(f32)
    inverse = lax.rsqrt(lax.dynamic_slice_in_dim(bn_var, tower * (C // 2), C // 2) + EPS)
    feature_grad = (grad * inverse).astype(bf16)[None]
    return (
        feature_grad,
        kernel_sum,
        vec_sum[None, :, 0],
        vec_sum[None, :, 1],
        head_sum[..., :HEAD].astype(f32).reshape(3, 3, C, HEAD),
        hvec_sum[8, :HEAD],
        jnp.sum(hvec_sum[:5], axis=1),
    )


def solution(mesh):
    return jax.shard_map(
        functools.partial(body, dp=mesh.shape["dp"]),
        mesh=mesh,
        in_specs=(
            P("dp", None, "tower"),
            P(),
            P(),
            P("tower", None, None, None, None, None),
            P("tower", None, None),
            P("tower", None, None),
            P(),
            P(),
            P(),
            P("dp", None, None),
            P("dp", None, None),
            P("dp", None),
        ),
        out_specs=(
            P("dp", None, "tower"),
            P("tower", None, None, None, None, None),
            P("tower", None, None),
            P("tower", None, None),
            P(),
            P(),
            P(),
        ),
        check_vma=False,
    )
```

time: 1200 us -> 386 us (0.32); the launches traced: 1180 us -> 386 us
  local copies, waits for them, and re-layouts: 290 us -> 19.6 us
  other arithmetic: 236 us -> 15.2 us
  matrix products: 180 us -> 0 us
  waiting for transfers between devices: 262 us -> 160 us
  blocking collectives: 185 us -> 118 us
  Pallas kernels: 0 us -> 56.5 us
    reduce_sum x153 -> x1, other arithmetic: 138 us -> 0.63 us  [body(): jnp.sum(hvec_sum[:5], axis=1)]
    conv_general_dilated x45 -> x0, matrix products: 108 us -> none  [convolve(): lax.conv_general_dilated(values, kernel, (1, 1), 'SAME', dimension_number...]
    psum x2, waiting for transfers between devices: 262 us -> 160 us  [the longest x1 160 us: body(): lax.psum(jnp.stack(dws), 'dp').astype(f32).reshape(1, LAYERS, 3, 3, C, C)]
    reduce_sum x100 -> x0, local copies, waits for them, and re-layouts: 81 us -> none  [the longest x40 31.4 us: group_act(): spread = jnp.mean(jnp.square(grouped - center), axis=(1, 3), keepdims=True)]
    dot_general x200 -> x0, matrix products: 71.9 us -> none  [kernel_grad(): jnp.einsum('bhwc,bhwo->co', window, out_grads, preferred_element_type=jnp...]
    psum x2, blocking collectives: 182 us -> 115 us  [the longest x1 78.4 us: body(): vec_sum = lax.psum(jnp.stack(vecs), 'dp')]
    mul x89 -> x0, local copies, waits for them, and re-layouts: 59 us -> none  [the longest x43 31.9 us: group_act(): spread = jnp.mean(jnp.square(grouped - center), axis=(1, 3), keepdims=True)]
    pallas_call x0 -> x4, Pallas kernels: none -> 56.5 us  [the longest x1 28.3 us: run_first(): pl.pallas_call(first_kernel, out_shape=[shape((LAYERS - 1, CELLS, C), f32...]
  transfers between devices with their start and end apart: 3 -> 3, of which waited for: 1 -> 1; matrix products, arithmetic and copies ran while one was open for 6% -> 3% of each run, Pallas kernels for 0% -> 7%
where the time goes in v1:
time: 386 us
  waiting for transfers between devices  160 us (41%)
  blocking collectives  118 us (31%)
  Pallas kernels  56.5 us (15%)
  local copies, waits for them, and re-layouts  19.6 us (5%)
  between operations  15.8 us (4%)
  other arithmetic  15.2 us (4%)
    psum x1, waiting for transfers between devices, body(): lax.psum(jnp.stack(dws), 'dp').astype(f32).reshape(1, LAYERS, 3, 3, C, C)  160 us
    psum x1, blocking collectives, body(): vec_sum = lax.psum(jnp.stack(vecs), 'dp')  78.4 us
    psum x1, blocking collectives, body(): head_sum, hvec_sum = lax.psum((dhead, hvec), ('dp', 'tower'))  37 us
    pallas_call x1, Pallas kernels, run_first(): pl.pallas_call(first_kernel, out_shape=[shape((LAYERS - 1, CELLS, C), f32...  28.3 us
    pallas_call x3, Pallas kernels, run_middle(): pl.pallas_call(functools.partial(middle_kernel, l), grid=(1,), out_shape=...  28.2 us
    concatenate x2, local copies, waits for them, and re-layouts, to_cells(): jnp.concatenate([flat[:1344], gap(16), flat[1344:1352], gap(2), flat[1360...  9.4 us
    unnamed x36, local copies, waits for them, and re-layouts  8.95 us
  transfers between devices with their start and end apart: 3, of which 1 were waited for; matrix products, arithmetic and copies ran while one was open for 3% of the time, Pallas kernels for 7%

profile of v1, /device:TPU:0, one launch (start us, length us, event | category | flops | bytes accessed | tf_op | source)
XLA Modules:
  0.0 385.5 jit_solution(16524084212088259584)
XLA Ops:
  8.0 0.0 copy-start.4
  8.0 0.0 copy-start.3
  8.0 0.0 all-reduce.6.cloned.1.call-start
  8.1 0.0 copy-start.10
  8.1 2.7 all_gather.3
  10.9 0.0 copy-done.4
  10.9 0.3 copy.27
  11.2 0.0 copy-done.3
  11.2 0.2 copy.26
  11.4 0.0 copy-done.10
  11.5 0.0 copy-start.2
  11.5 0.2 bitcast_select_fusion
  11.7 0.1 select_bitcast_fusion
  11.8 0.0 copy-start.13
  11.8 0.0 copy-start.12
  11.9 0.0 copy-start.11
  11.9 0.1 pad.19.clone
  12.0 0.2 maximum_maximum_fusion
  12.2 0.3 copy-done.2
  12.5 1.1 copy.25
  13.6 0.0 copy-done.13
  13.6 0.5 pad_bitcast_fusion.head_bias
  14.1 0.0 copy-done.12
  14.1 0.0 copy-done.11
  14.1 0.6 pad_maximum_fusion.3.bn
  14.7 5.1 %concatenate.16.x = bf16[1408,256]{1,0:T(8,128)(2,1)} concatenate(bf16[1344,256]{1,0:T(8,128)(2,1)S(1)} %slice_bitcast_fusion, bf16[16,256]{1,0:T(8,128)(2,1)S(1)} %broadcast_in_dim.45, bf16[8,256]{1,0:T(8,128)(2,1)S(1)} %get-tuple-element.58, bf16[2,256]{1,0:T(2,128)(2,1)S(1)} %broadcast.26, bf16[4,256]{1,0:T(4,128)(2,1)S(1)} %slice_bitcast_fusion.5, ...), dimensions={0} | concatenate | bytes 1441792 | tf_op jit(solution)/shard_map/concatenate | solution.py:425
  19.8 4.3 %concatenate.19.cot = bf16[1408,128]{1,0:T(8,128)(2,1)} concatenate(bf16[1344,128]{1,0:T(8,128)(2,1)S(1)} %slice.92, bf16[16,128]{1,0:T(8,128)(2,1)S(1)} %broadcast_in_dim.54, bf16[8,128]{1,0:T(8,128)(2,1)S(1)} %get-tuple-element.60, bf16[2,128]{1,0:T(2,128)(2,1)S(1)} %broadcast.27, bf16[4,128]{1,0:T(4,128)(2,1)S(1)} %slice.94, bf16[2,128]{1,0:T(2,128)(2,1)S(1)} %broadcast.27, ...), dimensions={0} | concatenate | bytes 720896 | tf_op jit(solution)/shard_map/concatenate | solution.py:425
  24.1 28.3 %forward_and_heads.1 = (f32[3,1408,256]{2,1,0:T(8,128)}, bf16[3,1408,256]{2,1,0:T(8,128)(2,1)}, f32[3,16,256]{2,1,0:T(8,128)}, f32[1408,256]{1,0:T(8,128)}, bf16...) custom-call(s32[1]{0:T(128)} %bitcast.2.tower, f32[5]{0:T(128)} %scale.1, ...), custom_call_target="tpu_custom_call" | custom-call | tf_op jit(solution)/shard_map/forward_and_heads/pallas_call | solution.py:370
  52.5 0.0 all-reduce.6.cloned.1.call-update
  52.5 0.0 reduce-scatter.4.cloned.1.call-start
  52.5 9.3 %layer_gradients_2.1 = (f32[1408,256]{1,0:T(8,128)}, bf16[9,256,256]{2,1,0:T(8,128)(2,1)}, f32[8,256]{1,0:T(8,128)}) custom-call(f32[1408,256]{1,0:T(8,128)} %get-tuple-element.24.da_in, f32[3,1408,256]{2,1,0:T(8,128)} %get-tuple-element.25.z, bf16[3,1408,256]{2,1,0:T(8,128)(2,1)} %get-tuple-element.26.a, f32[3,16,256]{2,1,0:T(8,128)} %get-tuple-element.27.stats, ...), custom_call_target="tpu_custom_call" | custom-call | tf_op jit(solution)/shard_map/layer_gradients_2/pallas_call | solution.py:403
  61.9 9.5 %layer_gradients_1.1 = (f32[1408,256]{1,0:T(8,128)}, bf16[9,256,256]{2,1,0:T(8,128)(2,1)}, f32[8,256]{1,0:T(8,128)}) custom-call(f32[1408,256]{1,0:T(8,128)} %get-tuple-element.28.da_in, f32[3,1408,256]{2,1,0:T(8,128)} %get-tuple-element.25.z, bf16[3,1408,256]{2,1,0:T(8,128)(2,1)} %get-tuple-element.26.a, f32[3,16,256]{2,1,0:T(8,128)} %get-tuple-element.27.stats, ...), custom_call_target="tpu_custom_call" | custom-call | tf_op jit(solution)/shard_map/layer_gradients_1/pallas_call | solution.py:403
  71.4 9.4 %layer_gradients_0.1 = (f32[1408,256]{1,0:T(8,128)}, bf16[9,256,256]{2,1,0:T(8,128)(2,1)}, f32[8,256]{1,0:T(8,128)}) custom-call(f32[1408,256]{1,0:T(8,128)} %get-tuple-element.29.da_in, f32[3,1408,256]{2,1,0:T(8,128)} %get-tuple-element.25.z, bf16[3,1408,256]{2,1,0:T(8,128)(2,1)} %get-tuple-element.26.a, f32[3,16,256]{2,1,0:T(8,128)} %get-tuple-element.27.stats, ...), custom_call_target="tpu_custom_call" | custom-call | tf_op jit(solution)/shard_map/layer_gradients_0/pallas_call | solution.py:403
  80.7 1.4 convert.12
  82.2 0.0 copy-start
  82.2 0.0 copy-start.1
  82.3 1.1 copy.31
  83.5 0.0 reduce-scatter.4.cloned.1.call-update
  83.5 0.0 all-reduce.4.cloned.1.call-start
  83.5 0.0 copy-done
  83.5 0.6 copy-done.1
  84.2 3.7 pad_maximum_fusion
  87.9 0.0 copy-start.6
  87.9 0.0 copy-start.7
  87.9 0.0 copy-start.9
  87.9 0.0 copy-start.5
  87.9 0.0 all-reduce.4.cloned.1.call-update
  87.9 0.6 copy-done.6
  88.6 0.0 copy-done.7
  88.6 0.0 copy-done.8
  88.6 0.0 copy-done.9
  88.6 78.4 %psum.29 = f32[4,8,256]{2,1,0:T(8,128)S(1)} all-reduce(f32[4,8,256]{2,1,0:T(8,128)S(1)} %pad_maximum_fusion.2), channel_id=1, replica_groups=mesh['dp'=16,'tower'=2] {'dp'}, use_global_device_ids=true, to_apply=%region_2.3 | all-reduce | flops 8192 | bytes 65536 | tf_op jit(solution)/shard_map/psum | solution.py:457
  167.0 0.6 copy.28
  167.6 0.6 copy.29
  168.2 0.0 copy-done.5
  168.2 37.0 %psum.31 = f32[16,128]{1,0:T(8,128)S(1)} all-reduce(f32[16,128]{1,0:T(8,128)S(1)} %copy-done.5), channel_id=1, replica_groups=mesh['dp'=16,'tower'=2] {'dp','tower'}, use_global_device_ids=true, to_apply=%region_4.5 | all-reduce | flops 2048 | bytes 16384 | tf_op jit(solution)/shard_map/psum | solution.py:458
  205.2 0.1 add_rsqrt_fusion
  205.3 0.6 slice_reduce_fusion
  205.9 0.5 slice_bitcast_fusion.6
  206.4 2.2 copy.30
  208.7 1.2 copy.32
  209.9 0.8 fusion
  210.7 160.1 %all-reduce.4.cloned.1.call-done = bf16[1,4,3,3,256,256]{5,4,3,2,1,0:T(8,128)(2,1)} async-done(((bf16[1,4,3,3,256,256]{5,4,3,2,1,0:T(8,128)(2,1)}), bf16[1,4,3,3,256,256]{5,4,3,2,1,0:T(8,128)(2,1)}) %all-reduce.4.cloned.1.call-update) | async-done | bytes 4718608 | tf_op jit(solution)/shard_map/psum | solution.py:456
  370.8 7.3 %reshape.54 = f32[1,4,3,3,256,256]{5,4,3,2,1,0:T(8,128)} convert(bf16[1,4,3,3,256,256]{5,4,3,2,1,0:T(8,128)(2,1)} %all-reduce.4.cloned.1.call-done) | non-fusion elementwise | flops 2359296 | bytes 14155776 | tf_op jit(solution)/shard_map/reshape | solution.py:456
  (25 shorter events, 0.3 us)
Async XLA Ops:
  8.0 2.9 copy-start.4
  8.0 3.2 copy-start.3
  8.0 198.4 %all-reduce.6.cloned.1.call-start = ((), (), s32[]{:S(2)}) async-start(), calls=%async_computation.2 | async-start | bytes 1179648 | tf_op jit(solution)/shard_map/psum | solution.py:458
  8.1 3.4 copy-start.10
  11.5 1.0 copy-start.2
  11.8 1.7 copy-start.13
  11.8 2.2 copy-start.12
  11.9 2.2 copy-start.11
  52.5 156.2 %reduce-scatter.4.cloned.1.call-start = ((), (), s32[]{:S(2)}) async-start(), calls=%async_computation.3 | async-start | bytes 1081344
  82.2 1.3 copy-start
  82.2 1.9 copy-start.1
  83.5 287.3 %all-reduce.4.cloned.1.call-start = ((), (), s32[]{:S(2)}) async-start(), calls=%async_computation.1 | async-start | bytes 9437184 | tf_op jit(solution)/shard_map/psum | solution.py:456
  87.9 0.7 copy-start.6
  87.9 0.7 copy-start.7
  87.9 0.7 copy-start.8
  87.9 0.7 copy-start.9
  87.9 80.3 %copy-start.5 = (f32[16,128]{1,0:T(8,128)S(1)}, f32[16,128]{1,0:T(8,128)}, u32[]{:S(2)}) copy-start(f32[16,128]{1,0:T(8,128)} %get-tuple-element.40) | copy-start | bytes 24580
Sparse Core Ops, SparseCore 0:
  52.6 131.8 all-reduce.5
  190.8 179.9 all-reduce.3
Sparse Core Ops, SparseCore 1:
  83.6 12.6 reduce-scatter.3

commit v2 on v1

--- a/solution.py
+++ b/solution.py
@@ -28,8 +28,12 @@
 ANY = pl.BlockSpec(memory_space=pl.ANY)
 
 
-def params():
-    return pltpu.CompilerParams(vmem_limit_bytes=56 << 20)
+VEC = 32
+SPLITS = 3
+
+
+def params(mib=56):
+    return pltpu.CompilerParams(vmem_limit_bytes=mib << 20)
 
 
 def tail_masks():
@@ -236,42 +240,178 @@
     return jnp.sum(sum_dyz, axis=0, keepdims=True), jnp.sum(sum_dy, axis=0, keepdims=True)
 
 
-def center(buf, cell, cells, row, lanes):
+def center(buf, cells, row, lanes):
     return buf[row : row + cells, lanes : 2 * lanes]
 
 
-def layer_back(da, z, a, stats, gain, shift, weight, buf, turned, dw, vec):
-    turned[...] = a.T
-    dgain, dshift = backward_norm(da, z, stats[0:8], stats[8:16], gain, shift, buf)
+def shape(dims, dtype):
+    return jax.ShapeDtypeStruct(dims, dtype)
+
+
+def pack(vec):
+    high = vec.astype(bf16).astype(f32)
+    middle = (vec - high).astype(bf16).astype(f32)
+    low = vec - high - middle
+    return jnp.concatenate([high, middle, low, jnp.zeros_like(vec)], axis=0).astype(bf16)
+
+
+def unpack(block):
+    parts = block.astype(f32)
+    return parts[0:8] + parts[8:16] + parts[16:24]
+
+
+def bit_of(place, order, step):
+    return jnp.where(place[1] == 0, place[0] >> order[0][step], place[0] >> order[1][step]) & 1
+
+
+def split_store(bit, tap, grad, keep, send):
+    half = C // 2
+    low, high = grad[:half], grad[half:]
+    keep[tap * half : (tap + 1) * half, :] = jnp.where(bit == 1, high, low).astype(bf16)
+    send[tap * half : (tap + 1) * half, :] = jnp.where(bit == 1, low, high).astype(bf16)
+
+
+def halve_kernel(taps, rows, order, step, place, keep, got, vec, keep_out, send_out, vec_out):
+    bit = bit_of(place, order, step)
+    half = rows // 2
+
+    def one(t, _):
+        for out, side in ((keep_out, bit), (send_out, 1 - bit)):
+            at = pl.ds(pl.multiple_of(t * rows + side * half, half), half)
+            to = pl.ds(pl.multiple_of(t * half, half), half)
+            out[to, :] = (keep[at, :].astype(f32) + got[at, :].astype(f32)).astype(bf16)
+        return 0
+
+    lax.fori_loop(0, taps, one, 0)
+    total = vec[...] + unpack(got[taps * rows :, :])
+    vec_out[...] = total
+    send_out[taps * half :, :] = pack(total)
+
+
+def add_kernel(taps, rows, keep, got, vec, sum_out, vec_out):
+    def one(t, _):
+        at = pl.ds(pl.multiple_of(t * rows, rows), rows)
+        sum_out[at, :] = (keep[at, :].astype(f32) + got[at, :].astype(f32)).astype(bf16)
+        return 0
+
+    lax.fori_loop(0, taps, one, 0)
+    total = vec[...] + unpack(got[taps * rows :, :])
+    vec_out[...] = total
+    sum_out[taps * rows :, :] = pack(total)
+
+
+def join_kernel(taps, rows, order, step, place, own, got, out):
+    bit = bit_of(place, order, step)
+
+    def one(t, _):
+        at = pl.ds(pl.multiple_of(t * rows, rows), rows)
+        out[pl.ds(pl.multiple_of((2 * t + bit) * rows, rows), rows), :] = own[at, :]
+        out[pl.ds(pl.multiple_of((2 * t + 1 - bit) * rows, rows), rows), :] = got[at, :]
+        return 0
+
+    lax.fori_loop(0, taps, one, 0)
+
+
+def final_kernel(layer, order, first, extra, *refs):
+    if first:
+        place, own, got, vec, out, rest, wide, sems = refs
+    else:
+        place, own, got, _, out, wide, sems = refs
+    bit = bit_of(place, order, 0)
+    half = C // 2
+    copies = []
+    for t in range(9):
+        wide[pl.ds(pl.multiple_of(t * C + bit * half, half), half), :] = own[t * half : (t + 1) * half, :].astype(f32)
+        wide[pl.ds(pl.multiple_of(t * C + (1 - bit) * half, half), half), :] = got[t * half : (t + 1) * half, :].astype(f32)
+        copy = pltpu.make_async_copy(
+            wide.at[t * C : (t + 1) * C], out.at[(layer * 9 + t) * C : (layer * 9 + t + 1) * C], sems.at[t]
+        )
+        copy.start()
+        copies.append(copy)
+    if first:
+        for t in range(extra):
+            rest[pl.ds(pl.multiple_of(t * C + bit * half, half), half), :] = own[(9 + t) * half : (10 + t) * half, :]
+            rest[pl.ds(pl.multiple_of(t * C + (1 - bit) * half, half), half), :] = got[(9 + t) * half : (10 + t) * half, :]
+        rest[extra * C :, :] = pack(vec[...])
+    for copy in copies:
+        copy.wait()
+
+
+def heads_kernel(own, got, vec, dhead_out, vec_out):
+    for i in range(3):
+        at = slice(i * C, (i + 1) * C)
+        turned = (own[at, :].astype(f32) + got[at, :].astype(f32)).T
+        for j in range(3):
+            dhead_out[i, j] = turned[j * HEAD : (j + 1) * HEAD, :]
+    vec_out[...] = vec[...] + unpack(got[3 * C :, :])
+
+
+def features_kernel(place, keep, got, var, out):
+    half = C // 2
+    inverse = lax.rsqrt(jnp.where(place[1] == 0, var[:, :half], var[:, half:]) + EPS)
+
+    def scaled(cell, cells):
+        return (keep[pl.ds(cell, cells), :].astype(f32) + got[pl.ds(cell, cells), :].astype(f32)) * inverse
+
+    def one(t, _):
+        at = pl.multiple_of(t * TILE, TILE)
+        out[pl.ds(at, TILE), :] = scaled(at, TILE).astype(bf16)
+        return 0
+
+    lax.fori_loop(0, 1344 // TILE, one, 0)
+    tail = scaled(1344, TILE)
+    out[1344:PIX, :] = jnp.concatenate([tail[16:24], tail[32:40], tail[26:30]], axis=0).astype(bf16)
+
+
+def gradients_out(bit, turned, buf, keep, send):
+    for i in range(3):
+        grad = kernel_grad(turned, buf, i)
+        for j in range(3):
+            split_store(bit, i * 3 + j, grad[:, j * C : (j + 1) * C], keep, send)
+
+
+def vector_rows(rows):
     row = lax.broadcasted_iota(jnp.int32, (8, C), 0)
-    vec[...] = jnp.where(row == 0, dgain, jnp.where(row == 1, dshift, 0.0))
-    for i in range(3):
-        grad = kernel_grad(turned, buf, i).astype(bf16)
-        for j in range(3):
-            dw[i * 3 + j] = grad[:, j * C : (j + 1) * C]
-    conv_back_into(da, buf, lambda tap: weight[tap * C : (tap + 1) * C, :], C)
+    out = jnp.zeros((8, C), f32)
+    for at, value in enumerate(rows):
+        out = jnp.where(row == at, value, out)
+    return out
+
+
+def spread_tail(tile, scratch):
+    scratch[...] = jnp.zeros(scratch.shape, f32)
+    scratch[16:24, :] = tile[0:8]
+    scratch[32:40, :] = tile[8:16]
+    scratch[26:30, :] = tile[16:20]
 
 
 def first_kernel(
-    tower, scale, x, bn, w_hbm, gains, shifts, head, head_bias, cot,
-    z_out, a_out, stats_out, da_out, dw_out, vec_out, dhead_out, hvec_out,
-    w, buf, zs, hw, hg, hbuf, u, turned, sems,
+    order, place, scale, own, other, bn_mean, bn_var, w_hbm, gains, shifts, head, head_bias, cls, reg, pos,
+    z_hbm, a_hbm, stats_out, da_out, keep_out, send_out, vec_out,
+    w, buf, zs, acts, hw, hg, hbuf, u, turned, tail, sems,
 ):
     loads = [pltpu.make_async_copy(w_hbm.at[l], w.at[l], sems.at[l]) for l in range(LAYERS)]
     for load in loads:
         load.start()
+    saves = []
+    half = C // 2
+    tower = place[1]
     clear_gaps(buf)
     clear_gaps(hbuf)
-    hw[...] = jnp.zeros(hw.shape, bf16)
-    hw[:, 0:HEAD] = head[...]
-    inverse = lax.rsqrt(bn[8:9] + EPS)
-    mean0 = bn[0:1]
+    inverse = lax.rsqrt(bn_var[...] + EPS)
+    mean0 = bn_mean[...]
+
+    def halves(rows):
+        left = jnp.where(tower == 0, own[rows, :].astype(f32), other[rows, :].astype(f32))
+        right = jnp.where(tower == 0, other[rows, :].astype(f32), own[rows, :].astype(f32))
+        return (jnp.concatenate([left, right], axis=1) - mean0) * inverse
 
     def base(level, cell, row, width, carry):
-        tile = (x[pl.ds(cell, TILE), :].astype(f32) - mean0) * inverse
-        if level == 3:
-            third, fourth = tail_masks()
-            tile = jnp.where(third | fourth, tile, 0.0)
+        if level < 3:
+            tile = halves(pl.ds(cell, TILE))
+        else:
+            spread_tail(halves(slice(1344, PIX)), tail)
+            tile = tail[...]
         write_shifted(buf, row, width, tile, C, False)
         return carry
 
@@ -280,36 +420,74 @@
     for l in range(LAYERS):
         if l < LAYERS - 1:
             for cell, cells, row, width in PARTS:
-                a_out[l, cell : cell + cells, :] = center(buf, cell, cells, row, C)
+                acts[l, cell : cell + cells, :] = center(buf, cells, row, C)
+            saves.append(pltpu.make_async_copy(acts.at[l], a_hbm.at[l], sems.at[LAYERS + l]))
+            saves[-1].start()
         else:
             for cell, cells, row, width in PARTS:
-                turned[:, cell : cell + cells] = center(buf, cell, cells, row, C).T
+                turned[:, cell : cell + cells] = center(buf, cells, row, C).T
         loads[l].wait()
-        z = zs.at[...] if l == LAYERS - 1 else z_out.at[l]
+        z = zs.at[l]
         conv_into(z, buf, w[l], C)
+        if l < LAYERS - 1:
+            saves.append(pltpu.make_async_copy(z, z_hbm.at[l], sems.at[2 * LAYERS + l]))
+            saves[-1].start()
         mean, rstd = norm_stats(z)
         if l < LAYERS - 1:
             stats_out[l, 0:8, :] = mean
             stats_out[l, 8:16, :] = rstd
-        else:
-            stats = jnp.concatenate([mean, rstd], axis=0)
         forward_act(z, mean, rstd, gains[l : l + 1], shifts[l : l + 1], buf)
 
-    hvec_out[...] = jnp.zeros(hvec_out.shape, f32)
-    for cell in range(0, CELLS, TILE):
-        hg[cell : cell + TILE, :] = cot[cell : cell + TILE, :].astype(f32)
-
-    @pl.when(tower[0] == 1)
+    box = reg[...].astype(f32) * pos[...].astype(f32)
+    is_class = tower == 0
+    rows = jnp.concatenate(
+        [
+            jnp.where(is_class, cls[...].astype(f32), 0.0),
+            jnp.where(is_class, 0.0, jnp.concatenate([box, jnp.zeros((3, PIX), f32)], axis=0)),
+            jnp.zeros((LANES - CLASSES - 8, PIX), f32),
+        ],
+        axis=0,
+    )
+    rows = jnp.concatenate([rows, jnp.zeros((LANES, CELLS - PIX), f32)], axis=1)
+    hg[...] = rows.T
+    spread_tail(jnp.concatenate([hg[1344:PIX, :]] * 2, axis=1), tail)
+    hg[1344:CELLS, :] = tail[:, 0:LANES]
+
+    hw[...] = jnp.zeros(hw.shape, bf16)
+    for i in range(3):
+        three = jnp.concatenate([head[i, j].astype(f32) for j in range(3)] + [jnp.zeros((1, C), f32)], axis=0)
+        hw[i * C : (i + 1) * C, :] = three.astype(bf16)
+
+    lane = lax.broadcasted_iota(jnp.int32, (TILE, LANES), 1)
+    row = lax.broadcasted_iota(jnp.int32, (TILE, LANES), 0)
+    third = ((row >= 16) & (row < 24)) | ((row >= 32) & (row < 40))
+    fourth = (row >= 26) & (row < 30)
+    hvec = jnp.zeros((1, LANES), f32)
+    u[...] = jnp.zeros(u.shape, f32)
+
+    @pl.when(tower == 1)
     def _():
-        conv_into(u, buf, hw[...], C)
-        lane = lax.broadcasted_iota(jnp.int32, (TILE, LANES), 1)
+        for cell, cells, first, width in PARTS:
+            for at in range(0, cells, 256):
+                size = min(256, cells - at)
+                total = None
+                for i in range(3):
+                    from_row = first + at + (i - 1) * width
+                    for j in range(3):
+                        kernel = jnp.concatenate([head[i, j], jnp.zeros((LANES - HEAD, C), bf16)], axis=0)
+                        term = lax.dot_general(
+                            buf[from_row : from_row + size, j * C : (j + 1) * C],
+                            kernel,
+                            (((1,), (1,)), ((), ())),
+                            preferred_element_type=f32,
+                        )
+                        total = term if total is None else total + term
+                u[cell + at : cell + at + size, :] = total
+        bias = jnp.concatenate([head_bias[...], jnp.zeros((1, LANES - HEAD), f32)], axis=1)
         dist_lane = (lane >= CLASSES) & (lane < CLASSES + 4)
-        row = lax.broadcasted_iota(jnp.int32, (TILE, LANES), 0)
-        third = ((row >= 16) & (row < 24)) | ((row >= 32) & (row < 40))
-        fourth = (row >= 26) & (row < 30)
-
-        def box(level, cell, row, width, carry):
-            raw = u[pl.ds(cell, TILE), :] + head_bias[...]
+
+        def boxes(level, cell, row, width, carry):
+            raw = u[pl.ds(cell, TILE), :] + bias
             g = hg[pl.ds(cell, TILE), :]
             if level < 3:
                 ls = scale[level]
@@ -319,154 +497,296 @@
                 use = dist_lane & (third | fourth)
             weighted = jnp.where(use, g * jnp.exp(ls * raw), 0.0)
             hg[pl.ds(cell, TILE), :] = jnp.where(dist_lane, weighted * ls, g)
-            term = weighted * raw
-            if level < 3:
-                return carry + fold(term)
-            return (fold(jnp.where(third, term, 0.0)), fold(jnp.where(fourth, term, 0.0)))
-
-        r = each_tile(box, jnp.zeros((8, LANES), f32))
-        hvec_out[0:8, :] = stack_rows([r[0], r[1], r[2], r[3][0], r[3][1]])
+            u[pl.ds(cell, TILE), :] = weighted * raw
+            return carry
+
+        each_tile(boxes, jnp.int32(0))
+
+    def scale_sums(level, cell, row, width, carry):
+        term = u[pl.ds(cell, TILE), :]
+        if level < 3:
+            return carry + fold(term)
+        return (fold(jnp.where(third, term, 0.0)), fold(jnp.where(fourth, term, 0.0)))
+
+    r = each_tile(scale_sums, jnp.zeros((8, LANES), f32))
+    scale_rows = [jnp.sum(v, axis=0, keepdims=True) for v in (r[0], r[1], r[2], r[3][0], r[3][1])]
 
     def head_rows(level, cell, row, width, carry):
         tile = hg[pl.ds(cell, TILE), :].astype(bf16).astype(f32)
-        write_shifted(hbuf, row, width, tile, LANES, True)
+        at = lax.broadcasted_iota(jnp.int32, tile.shape, 0) & (width - 1)
+        after = jnp.where(at == 0, 0.0, pltpu.roll(tile, 1, 0))
+        before = jnp.where(at == width - 1, 0.0, pltpu.roll(tile, TILE - 1, 0))
+        middle = pltpu.roll(tile, HEAD, 1)
+        after = pltpu.roll(after, 2 * HEAD - LANES, 1)
+        rows = pl.ds(row, TILE)
+        hbuf[rows, 0:LANES] = jnp.where(lane < HEAD, before, middle).astype(bf16)
+        hbuf[rows, LANES : 2 * LANES] = jnp.where(lane < 2 * HEAD - LANES, middle, after).astype(bf16)
         return carry + fold(tile)
 
     r = each_tile(head_rows, jnp.zeros((8, LANES), f32))
-    total = jnp.sum(r[0] + r[1] + r[2] + r[3], axis=0, keepdims=True)
-    hvec_out[8:16, :] = jnp.where(lax.broadcasted_iota(jnp.int32, (8, LANES), 0) == 0, total, 0.0)
-
-    a4t = jnp.concatenate([center(buf, c, n, r, C).T for c, n, r, _ in PARTS], axis=1)
+    bias_row = jnp.sum(r[0] + r[1] + r[2] + r[3], axis=0, keepdims=True)
+
+    bit = bit_of(place, order, 0)
+    a4t = jnp.concatenate([center(buf, n, r, C).T for _, n, r, _ in PARTS], axis=1)
     for i in range(3):
-        grad = kernel_grad(a4t, hbuf, i).astype(bf16)
-        for j in range(3):
-            dhead_out[i * 3 + j] = grad[:, j * LANES : (j + 1) * LANES]
-    conv_back_into(da_out, hbuf, lambda tap: hw[tap * C : (tap + 1) * C, :], LANES)
+        split_store(bit, 9 + i, kernel_grad(a4t, hbuf, i), keep_out, send_out)
+    for cell, cells, first, width in PARTS:
+        for at in range(0, cells, 256):
+            size = min(256, cells - at)
+            left = jnp.concatenate([hbuf[first + at - d * width : first + at - d * width + size, :] for d in (-1, 0, 1)], axis=1)
+            da_out[cell + at : cell + at + size, :] = jnp.dot(left, hw[...], preferred_element_type=f32)
 
     l = LAYERS - 1
-    dgain, dshift = backward_norm(da_out, zs, stats[0:8], stats[8:16], gains[l : l + 1], shifts[l : l + 1], buf)
-    row = lax.broadcasted_iota(jnp.int32, (8, C), 0)
-    vec_out[...] = jnp.where(row == 0, dgain, jnp.where(row == 1, dshift, 0.0))
-    for i in range(3):
-        grad = kernel_grad(turned, buf, i).astype(bf16)
-        for j in range(3):
-            dw_out[i * 3 + j] = grad[:, j * C : (j + 1) * C]
+    dgain, dshift = backward_norm(da_out, zs.at[l], mean, rstd, gains[l : l + 1], shifts[l : l + 1], buf)
+    wide = lambda v: jnp.concatenate([v, jnp.zeros_like(v)], axis=1)
+    vec = vector_rows([dgain, dshift, wide(bias_row)] + [wide(v) for v in scale_rows])
+    vec_out[...] = vec
+    send_out[12 * half :, :] = pack(vec)
+    gradients_out(bit, turned, buf, keep_out, send_out)
     conv_back_into(da_out, buf, lambda tap: w[l, tap * C : (tap + 1) * C, :], C)
-
-
-def middle_kernel(l, da_in, z, a, stats, gains, shifts, w, da_out, dw_out, vec_out, buf, turned):
+    for save in saves:
+        save.wait()
+
+
+def middle_kernel(
+    l, order, place, da_hbm, z_hbm, a_hbm, stats, gains, shifts, w_hbm, *refs,
+):
+    if l:
+        da_out, keep_out, send_out, vec_out, z, a, w, buf, turned, sems = refs
+        da = da_out
+    else:
+        keep_half, send_half, keep_out, send_out, vec_out, z, a, w, buf, turned, da, sems = refs
+    loads = [
+        pltpu.make_async_copy(src, dst, sems.at[k])
+        for k, (src, dst) in enumerate(((da_hbm, da), (z_hbm.at[l], z), (a_hbm.at[l], a), (w_hbm.at[l], w)))
+    ]
+    for load in loads:
+        load.start()
+    half = C // 2
+    bit = bit_of(place, order, 0)
     clear_gaps(buf)
-    da_out[...] = da_in[...]
-    layer_back(
-        da_out, z.at[0], a[0], stats[0], gains[l : l + 1], shifts[l : l + 1], w.at[0], buf, turned, dw_out, vec_out
+    loads[0].wait()
+    loads[1].wait()
+    dgain, dshift = backward_norm(
+        da, z, stats[l, 0:8, :], stats[l, 8:16, :], gains[l : l + 1], shifts[l : l + 1], buf
     )
-
-
-def shape(dims, dtype):
-    return jax.ShapeDtypeStruct(dims, dtype)
-
-
-def run_first(tower, scale, x, bn, w, gains, shifts, head, head_bias, cot):
+    vec = vector_rows([dgain, dshift])
+    vec_out[...] = vec
+    send_out[9 * half :, :] = pack(vec)
+    loads[2].wait()
+    turned[...] = a[...].T
+    gradients_out(bit, turned, buf, keep_out, send_out)
+    loads[3].wait()
+    conv_back_into(da, buf, lambda tap: w[tap * C : (tap + 1) * C, :], C)
+    if not l:
+        mine = place[1]
+        keep_half[...] = jnp.where(mine == 0, da[:, :half], da[:, half:])
+        send_half[...] = jnp.where(mine == 0, da[:, half:], da[:, :half]).astype(bf16)
+
+
+def run_first(order, place, scale, own, other, mean, var, w, gains, shifts, head, bias, cls, reg, pos):
+    half = C // 2
     return pl.pallas_call(
-        first_kernel,
+        functools.partial(first_kernel, order),
         out_shape=[
             shape((LAYERS - 1, CELLS, C), f32),
             shape((LAYERS - 1, CELLS, C), bf16),
             shape((LAYERS - 1, 16, C), f32),
             shape((CELLS, C), f32),
-            shape((9, C, C), bf16),
+            shape((12 * half, C), bf16),
+            shape((12 * half + VEC, C), bf16),
             shape((8, C), f32),
-            shape((9, C, LANES), bf16),
-            shape((16, LANES), f32),
         ],
-        in_specs=[SMEM, SMEM, VMEM, VMEM, ANY, VMEM, VMEM, VMEM, VMEM, VMEM],
-        out_specs=[VMEM] * 8,
+        in_specs=[SMEM, SMEM, VMEM, VMEM, VMEM, VMEM, ANY] + [VMEM] * 7,
+        out_specs=[ANY, ANY] + [VMEM] * 5,
         scratch_shapes=[
             pltpu.VMEM((LAYERS, 9 * C, C), bf16),
             pltpu.VMEM((PADDED, 3 * C), bf16),
-            pltpu.VMEM((CELLS, C), f32),
-            pltpu.VMEM((9 * C, LANES), bf16),
+            pltpu.VMEM((LAYERS, CELLS, C), f32),
+            pltpu.VMEM((LAYERS - 1, CELLS, C), bf16),
+            pltpu.VMEM((3 * C, C), bf16),
             pltpu.VMEM((CELLS, LANES), f32),
-            pltpu.VMEM((PADDED, 3 * LANES), bf16),
+            pltpu.VMEM((PADDED, 2 * LANES), bf16),
             pltpu.VMEM((CELLS, LANES), f32),
             pltpu.VMEM((C, CELLS), bf16),
-            pltpu.SemaphoreType.DMA((LAYERS,)),
+            pltpu.VMEM((TILE, C), f32),
+            pltpu.SemaphoreType.DMA((3 * LAYERS,)),
         ],
         compiler_params=params(),
         name="forward_and_heads",
-    )(tower, scale, x, bn, w, gains, shifts, head, head_bias, cot)
-
-
-def run_middle(l, da, z, a, stats, gains, shifts, w):
-    one = lambda dims: pl.BlockSpec((1,) + dims, lambda i: (l,) + (0,) * len(dims))
-    whole = lambda dims: pl.BlockSpec(dims, lambda i: (0,) * len(dims))
+    )(place, scale, own, other, mean, var, w, gains, shifts, head, bias, cls, reg, pos)
+
+
+def run_middle(l, order, place, da, z, a, stats, gains, shifts, w):
+    half = C // 2
+    outs = [shape((CELLS, C), f32)] if l else [shape((CELLS, half), f32), shape((CELLS, half), bf16)]
+    outs += [shape((9 * half, C), bf16), shape((9 * half + VEC, C), bf16), shape((8, C), f32)]
+    scratch = [
+        pltpu.VMEM((CELLS, C), f32),
+        pltpu.VMEM((CELLS, C), bf16),
+        pltpu.VMEM((9 * C, C), bf16),
+        pltpu.VMEM((PADDED, 3 * C), bf16),
+        pltpu.VMEM((C, CELLS), bf16),
+    ]
+    if not l:
+        scratch.append(pltpu.VMEM((CELLS, C), f32))
     return pl.pallas_call(
-        functools.partial(middle_kernel, l),
-        grid=(1,),
-        out_shape=[shape((CELLS, C), f32), shape((9, C, C), bf16), shape((8, C), f32)],
-        in_specs=[
-            whole((CELLS, C)),
-            one((CELLS, C)),
-            one((CELLS, C)),
-            one((16, C)),
-            whole((LAYERS, C)),
-            whole((LAYERS, C)),
-            one((9 * C, C)),
-        ],
-        out_specs=[whole((CELLS, C)), whole((9, C, C)), whole((8, C))],
-        scratch_shapes=[pltpu.VMEM((PADDED, 3 * C), bf16), pltpu.VMEM((C, CELLS), bf16)],
-        compiler_params=params(),
+        functools.partial(middle_kernel, l, order),
+        out_shape=outs,
+        in_specs=[SMEM, ANY, ANY, ANY, VMEM, VMEM, VMEM, ANY],
+        out_specs=[VMEM] * len(outs),
+        scratch_shapes=scratch + [pltpu.SemaphoreType.DMA((4,))],
+        compiler_params=params(40),
         name=f"layer_gradients_{l}",
-    )(da, z, a, stats, gains, shifts, w)
-
-
-def to_cells(flat):
-    gap = lambda rows: jnp.zeros((rows, flat.shape[1]), flat.dtype)
-    return jnp.concatenate(
-        [flat[:1344], gap(16), flat[1344:1352], gap(2), flat[1360:1364], gap(2), flat[1352:1360], gap(24)], axis=0
-    )
-
-
-def to_flat(cells):
-    return jnp.concatenate([cells[:1344], cells[1360:1368], cells[1376:1384], cells[1370:1374]], axis=0)
+    )(place, da, z, a, stats, gains, shifts, w)
+
+
+def small_call(kernel, outs, name, ins, **more):
+    return pl.pallas_call(
+        kernel,
+        out_shape=outs,
+        in_specs=[SMEM] * more.pop("scalars", 0) + [VMEM] * more.pop("blocks"),
+        out_specs=[VMEM] * len(outs),
+        compiler_params=params(16),
+        name=name,
+    )(*ins)
+
+
+class Sum:
+    def __init__(self, layer, taps, order, bits, place, keep, send, vec):
+        self.layer, self.taps, self.order, self.bits, self.place = layer, taps, order, bits, place
+        self.keep, self.vec = keep, vec
+        self.splits = min(SPLITS, bits)
+        self.rows = C // 2
+        self.send = send
+        self.step = 0
+
+    def partner(self, value, step):
+        pairs = []
+        for d in range(1 << self.bits):
+            for t in range(2):
+                pairs.append((2 * d + t, 2 * (d ^ (1 << self.order[t][step])) + t))
+        return lax.ppermute(value, ("dp", "tower"), pairs)
+
+    def reduce(self):
+        taps, name = self.taps, f"sum_{self.layer}"
+        got = self.partner(self.send, 0)
+        for step in range(1, self.bits + 1):
+            rows = self.rows
+            vec = shape((8, C), f32)
+            if step < self.splits:
+                half = rows // 2
+                self.keep, self.send, self.vec = small_call(
+                    functools.partial(halve_kernel, taps, rows, self.order, step),
+                    [shape((taps * half, C), bf16), shape((taps * half + VEC, C), bf16), vec],
+                    name, (self.place, self.keep, got, self.vec), scalars=1, blocks=3,
+                )
+                self.rows = half
+            else:
+                self.send, self.vec = small_call(
+                    functools.partial(add_kernel, taps, rows),
+                    [shape((taps * rows + VEC, C), bf16), vec],
+                    name, (self.keep, got, self.vec), blocks=3,
+                )
+                self.keep = self.send
+            if step < self.bits:
+                got = self.partner(self.send, step)
+        self.own = self.send
+
+    def gather(self):
+        for step in range(self.splits - 1, 0, -1):
+            got = self.partner(self.own, step)
+            (self.own,) = small_call(
+                functools.partial(join_kernel, self.taps, self.rows, self.order, step),
+                [shape((self.taps * 2 * self.rows, C), bf16)],
+                f"gather_{self.layer}", (self.place, self.own, got), scalars=1, blocks=2,
+            )
+            self.rows *= 2
+        self.got = self.partner(self.own, 0)
+
+    def finish(self, out):
+        first = out is None
+        extra = self.taps - 9
+        half = C // 2
+        outs = [shape((LAYERS * 9 * C, C), f32)]
+        ins = [self.place, self.own, self.got]
+        if first:
+            outs.append(shape((extra * C + VEC, C), bf16))
+            ins.append(self.vec)
+        else:
+            ins.append(out)
+        return pl.pallas_call(
+            functools.partial(final_kernel, self.layer, self.order, first, extra),
+            out_shape=outs,
+            in_specs=[SMEM, VMEM, VMEM, VMEM if first else ANY],
+            out_specs=[ANY, VMEM] if first else [ANY],
+            scratch_shapes=[pltpu.VMEM((9 * C, C), f32), pltpu.SemaphoreType.DMA((9,))],
+            input_output_aliases={} if first else {3: 0},
+            compiler_params=params(24),
+            name=f"write_{self.layer}",
+        )(*ins)
+
+
+def orders(bits):
+    if bits == 4:
+        p = ((0, 2, 1, 3), (1, 0, 2, 3))
+        q = ((1, 0, 2, 3), (2, 1, 0, 3))
+        r = ((2, 1, 0, 3), (0, 2, 1, 3))
+        return (q, p, r, r)
+    line = tuple(range(bits))
+    return (((line, line[1:] + line[:1]),) * LAYERS)
 
 
 def body(
     features, bn_mean, bn_var, tower_weight, norm_gain, norm_bias, head_weight, head_bias, level_scale,
     cls_cot, reg_cot, positive, *, dp,
 ):
-    tower = lax.axis_index("tower")
-    whole = lax.all_gather(features, "tower", axis=2, tiled=True)[0]
-    x = to_cells(whole)
-    cls = jnp.where(tower == 0, cls_cot[0], 0)
-    box = jnp.where((tower == 1) & (positive[0] == 1)[:, None], reg_cot[0], 0)
-    cot = to_cells(jnp.concatenate([cls, box, jnp.zeros((PIX, LANES - HEAD), bf16)], axis=1))
-    bn = jnp.concatenate([jnp.broadcast_to(bn_mean, (8, C)), jnp.broadcast_to(bn_var, (8, C))], axis=0)
+    bits = dp.bit_length() - 1
+    assert dp == 1 << bits and bits >= 1
+    order = orders(bits)
+    place = jnp.stack([lax.axis_index("dp"), lax.axis_index("tower")])
+    own = features[0]
+    other = lax.ppermute(own, "tower", [(0, 1), (1, 0)])
     w = tower_weight[0].reshape(LAYERS, 9 * C, C)
-    bias = jnp.pad(head_bias, (0, LANES - HEAD))[None]
     gains, shifts = norm_gain[0], norm_bias[0]
-    z, a, stats, da, dw3, vec3, dhead, hvec = run_first(
-        tower.reshape(1), level_scale, x, bn, w, gains, shifts, head_weight.reshape(9 * C, HEAD), bias, cot
+    mean, var = bn_mean[None], bn_var[None]
+    z, a, stats, da, keep, send, vec = run_first(
+        order[3], place, level_scale, own, other, mean, var, w, gains, shifts,
+        jnp.swapaxes(head_weight, 2, 3), head_bias[None],
+        jnp.swapaxes(cls_cot[0], 0, 1), jnp.swapaxes(reg_cot[0], 0, 1), positive,
     )
-    dws, vecs = [None] * LAYERS, [None] * LAYERS
-    dws[3], vecs[3] = dw3, vec3
+    sums = [None] * LAYERS
+    sums[3] = Sum(3, 12, order[3], bits, place, keep, send, vec)
+    for l in (2, 1):
+        da, keep, send, vec = run_middle(l, order[l], place, da, z, a, stats, gains, shifts, w)
+        sums[l] = Sum(l, 9, order[l], bits, place, keep, send, vec)
+    keep_half, send_half, keep, send, vec = run_middle(0, order[0], place, da, z, a, stats, gains, shifts, w)
+    sums[0] = Sum(0, 9, order[0], bits, place, keep, send, vec)
+    got_half = lax.ppermute(send_half, "tower", [(0, 1), (1, 0)])
+    (feature_grad,) = small_call(
+        features_kernel, [shape((PIX, C // 2), bf16)], "feature_gradient",
+        (place, keep_half, got_half, var), scalars=1, blocks=3,
+    )
+    for one in sums[::-1]:
+        one.reduce()
+        one.gather()
+    out, heads = sums[3].finish(None)
+    got_heads = lax.ppermute(heads, "tower", [(0, 1), (1, 0)])
+    dhead, hvec = small_call(
+        heads_kernel, [shape((3, 3, HEAD, C), f32), shape((8, C), f32)], "head_gradients",
+        (heads, got_heads, sums[3].vec), blocks=3,
+    )
     for l in (2, 1, 0):
-        da, dws[l], vecs[l] = run_middle(l, da, z, a, stats, gains, shifts, w)
-
-    kernel_sum = lax.psum(jnp.stack(dws), "dp").astype(f32).reshape(1, LAYERS, 3, 3, C, C)
-    vec_sum = lax.psum(jnp.stack(vecs), "dp")
-    head_sum, hvec_sum = lax.psum((dhead, hvec), ("dp", "tower"))
-    grad = lax.psum_scatter(to_flat(da).astype(bf16), "tower", scatter_dimension=1, tiled=True).astype(f32)
-    inverse = lax.rsqrt(lax.dynamic_slice_in_dim(bn_var, tower * (C // 2), C // 2) + EPS)
-    feature_grad = (grad * inverse).astype(bf16)[None]
+        (out,) = sums[l].finish(out)
+    vecs = jnp.stack([s.vec for s in sums])
     return (
-        feature_grad,
-        kernel_sum,
-        vec_sum[None, :, 0],
-        vec_sum[None, :, 1],
-        head_sum[..., :HEAD].astype(f32).reshape(3, 3, C, HEAD),
-        hvec_sum[8, :HEAD],
-        jnp.sum(hvec_sum[:5], axis=1),
+        feature_grad[None],
+        out.reshape(1, LAYERS, 3, 3, C, C),
+        vecs[None, :, 0],
+        vecs[None, :, 1],
+        jnp.swapaxes(dhead, 2, 3),
+        hvec[2, :HEAD],
+        jnp.sum(hvec[3:8], axis=1),
     )
 
 

time: 386 us -> 181 us (0.47)
  blocking collectives: 118 us -> 0 us
  waiting for transfers between devices: 160 us -> 60.4 us
  starting transfers between devices: 0.12 us -> 35.5 us
  Pallas kernels: 56.5 us -> 72.2 us
  between operations: 15.8 us -> 1 us
  other arithmetic: 15.2 us -> 1.22 us
  local copies, waits for them, and re-layouts: 19.6 us -> 10.3 us
    psum x2 -> x0, waiting for transfers between devices: 160 us -> none  [the longest x1 160 us: body(): lax.psum(jnp.stack(dws), 'dp').astype(f32).reshape(1, LAYERS, 3, 3, C, C)]
    psum x2 -> x0, blocking collectives: 115 us -> none  [the longest x1 78.4 us: body(): vec_sum = lax.psum(jnp.stack(vecs), 'dp')]
    ppermute x0 -> x31, waiting for transfers between devices: none -> 60.4 us  [the longest x28 59.5 us: partner(): return lax.ppermute(value, ('dp', 'tower'), pairs)]
    ppermute x0 -> x31, starting transfers between devices: none -> 35.5 us  [the longest x28 34.4 us: partner(): return lax.ppermute(value, ('dp', 'tower'), pairs)]
    pallas_call x4 -> x34, Pallas kernels: 56.5 us -> 72.2 us  [the longest x1 27.9 us: run_first(): pl.pallas_call(functools.partial(first_kernel, order), out_shape=[shape((...]
    concatenate x3 -> x0, local copies, waits for them, and re-layouts: 9.48 us -> none  [the longest x2 9.4 us: to_cells(): jnp.concatenate([flat[:1344], gap(16), flat[1344:1352], gap(2), flat[1360...]
    reshape x1 -> x0, other arithmetic: 7.28 us -> none  [body(): lax.psum(jnp.stack(dws), 'dp').astype(f32).reshape(1, LAYERS, 3, 3, C, C)]
    another operation x3 -> x2, other arithmetic: 5.17 us -> 0.59 us  [the longest x1 0.58 us: body(): place = jnp.stack([lax.axis_index('dp'), lax.axis_index('tower')])]
  transfers between devices with their start and end apart: 3 -> 31, of which waited for: 1 -> 17; matrix products, arithmetic and copies ran while one was open for 3% -> 1% of each run, Pallas kernels for 7% -> 23%
where the time goes in v2:
time: 181 us
  Pallas kernels  72.2 us (40%)
  waiting for transfers between devices  60.4 us (33%)
  starting transfers between devices  35.5 us (20%)
  local copies, waits for them, and re-layouts  10.3 us (6%)
    ppermute x28, waiting for transfers between devices, partner(): return lax.ppermute(value, ('dp', 'tower'), pairs)  59.5 us
    ppermute x28, starting transfers between devices, partner(): return lax.ppermute(value, ('dp', 'tower'), pairs)  34.4 us
    pallas_call x1, Pallas kernels, run_first(): pl.pallas_call(functools.partial(first_kernel, order), out_shape=[shape((...  27.9 us
    pallas_call x3, Pallas kernels, run_middle(): pl.pallas_call(functools.partial(middle_kernel, l, order), out_shape=outs...  22.1 us
    pallas_call x26, Pallas kernels, small_call(): pl.pallas_call(kernel, out_shape=outs, in_specs=[SMEM] * more.pop('scalar...  14 us
    unnamed x24, local copies, waits for them, and re-layouts  9.76 us
    pallas_call x4, Pallas kernels, finish(): pl.pallas_call(functools.partial(final_kernel, self.layer, self.order, fi...  8.14 us
  transfers between devices with their start and end apart: 31, of which 17 were waited for; matrix products, arithmetic and copies ran while one was open for 1% of the time, Pallas kernels for 23%

profile of v2, /device:TPU:0, one launch (start us, length us, event | category | flops | bytes accessed | tf_op | source)
XLA Modules:
  0.0 180.6 jit_solution(2920011467149056413)
XLA Ops:
  1.8 0.9 collective-permute-done.other
  2.7 0.7 copy-done.10
  3.4 27.9 %forward_and_heads.1 = (f32[3,1408,256]{2,1,0:T(8,128)}, bf16[3,1408,256]{2,1,0:T(8,128)(2,1)}, f32[3,16,256]{2,1,0:T(8,128)}, f32[1408,256]{1,0:T(8,128)}, bf16...) custom-call(s32[2]{0:T(128)} %pad_add_fusion.place.refs_0_, f32[5]{0:T(128)} %scale.1, ...), custom_call_target="tpu_custom_call" | custom-call | tf_op jit(solution)/shard_map/forward_and_heads/pallas_call | solution.py:589
  31.3 3.0 %collective-permute-start.23 = (bf16[1568,256]{1,0:T(8,128)(2,1)}, bf16[1568,256]{1,0:T(8,128)(2,1)S(1)}, u32[]{:S(2)}, u32[]{:S(2)}) collective-permute-start(bf16[1568,256]{1,0:T(8,128)(2,1)} %get-tuple-element.116), channel_id=1, source_target_pairs={{0,8},{1,3},{2,10},{3,1},{4,12},{5,7},{6,14},{7,5},{8,0},{9,11},{1... | collective-permute-start | bytes 2408456 | tf_op jit(solution)/shard_map/ppermute | solution.py:669
  34.4 10.4 %collective-permute-done.23.got = bf16[1568,256]{1,0:T(8,128)(2,1)S(1)} collective-permute-done((bf16[1568,256]{1,0:T(8,128)(2,1)}, bf16[1568,256]{1,0:T(8,128)(2,1)S(1)}, u32[]{:S(2)}, u32[]{:S(2)}) %collective-permute-start.23) | collective-permute-done | bytes 802848 | tf_op jit(solution)/shard_map/ppermute | solution.py:669
  44.7 1.1 copy-done.3
  45.8 0.7 copy-done.8
  46.5 0.8 sum_3.4
  47.4 2.0 %collective-permute-start.24 = (bf16[800,256]{1,0:T(8,128)(2,1)S(1)}, bf16[800,256]{1,0:T(8,128)(2,1)S(1)}, u32[]{:S(2)}, u32[]{:S(2)}) collective-permute-start(bf16[800,256]{1,0:T(8,128)(2,1)S(1)} %get-tuple-element.119), channel_id=1, source_target_pairs={{0,4},{1,9},{2,6},{3,11},{4,0},{5,13},{6,2},{7,15},{8,12},{9,1},{1... | collective-permute-start | bytes 1228808 | tf_op jit(solution)/shard_map/ppermute | solution.py:669
  49.4 2.2 %copy-done = f32[3,1408,256]{2,1,0:T(8,128)S(1)} copy-done((f32[3,1408,256]{2,1,0:T(8,128)S(1)}, f32[3,1408,256]{2,1,0:T(8,128)}, u32[]{:S(2)}) %copy-start) | copy-done | bytes 4325400
  51.6 1.6 copy-done.1
  53.2 1.4 copy-done.2
  54.6 0.8 copy-done.4
  55.4 7.3 %layer_gradients_2.1 = (f32[1408,256]{1,0:T(8,128)S(1)}, bf16[1152,256]{1,0:T(8,128)(2,1)S(1)}, bf16[1184,256]{1,0:T(8,128)(2,1)S(1)}, f32[8,256]{1,0:T(8,128)S(1)}) custom-call(s32[2]{0:T(128)S(1)} %copy-done.5, f32[1408,256]{1,0:T(8,128)S(1)} %copy-done.2, f32[3,1408,256]{2,1,0:T(8,128)S(1)} %copy-done, bf16[3,1408,256]{2,1,0:T(8,128)(2,1)S(1)} %copy-done.1, ...), custom_call_target="tpu_custom_call" | custom-call | tf_op jit(solution)/shard_map/layer_gradients_2/pallas_call | solution.py:633
  62.7 1.6 collective-permute-start.16
  64.4 7.3 %layer_gradients_1.1 = (f32[1408,256]{1,0:T(8,128)S(1)}, bf16[1152,256]{1,0:T(8,128)(2,1)S(1)}, bf16[1184,256]{1,0:T(8,128)(2,1)S(1)}, f32[8,256]{1,0:T(8,128)S(1)}) custom-call(s32[2]{0:T(128)S(1)} %copy-done.5, f32[1408,256]{1,0:T(8,128)S(1)} %get-tuple-element.75.da_hbm, f32[3,1408,256]{2,1,0:T(8,128)S(1)} %copy-done, ...), custom_call_target="tpu_custom_call" | custom-call | tf_op jit(solution)/shard_map/layer_gradients_1/pallas_call | solution.py:633
  71.6 1.6 collective-permute-start.9
  73.2 7.5 %layer_gradients_0.1 = (f32[1408,128]{1,0:T(8,128)S(1)}, bf16[1408,128]{1,0:T(8,128)(2,1)S(1)}, bf16[1152,256]{1,0:T(8,128)(2,1)S(1)}, bf16[1184,256]{1,0:T(8,128)(2,1)S(1)}, f32[8,256]{1,0:T(8,128)S(1)}) custom-call(s32[2]{0:T(128)S(1)} %copy-done.5, f32[1408,256]{1,0:T(8,128)S(1)} %get-tuple-element.76.da_hbm, f32[3,1408,256]{2,1,0:T(8,128)S(1)} %copy-done, ...), custom_call_target="tpu_custom_call" | custom-call | tf_op jit(solution)/shard_map/layer_gradients_0/pallas_call | solution.py:633
  81.3 0.7 sum_3.5
  82.6 5.3 %collective-permute-done.25.got = bf16[416,256]{1,0:T(8,128)(2,1)S(1)} collective-permute-done((bf16[416,256]{1,0:T(8,128)(2,1)S(1)}, bf16[416,256]{1,0:T(8,128)(2,1)S(1)}, u32[]{:S(2)}, u32[]{:S(2)}) %collective-permute-start.25) | collective-permute-done | bytes 213024 | tf_op jit(solution)/shard_map/ppermute | solution.py:669
  88.1 2.6 %collective-permute-start.26 = (bf16[416,256]{1,0:T(8,128)(2,1)S(1)}, bf16[416,256]{1,0:T(8,128)(2,1)S(1)}, u32[]{:S(2)}, u32[]{:S(2)}) collective-permute-start(bf16[416,256]{1,0:T(8,128)(2,1)S(1)} %get-tuple-element.124.keep), channel_id=1, source_target_pairs={{0,16},{1,17},{2,18},{3,19},{4,20},{5,21},{6,22},{7,23},{8,24},{9,... | collective-permute-start | bytes 638984 | tf_op jit(solution)/shard_map/ppermute | solution.py:669
  90.7 10.9 %collective-permute-done.26.got = bf16[416,256]{1,0:T(8,128)(2,1)S(1)} collective-permute-done((bf16[416,256]{1,0:T(8,128)(2,1)S(1)}, bf16[416,256]{1,0:T(8,128)(2,1)S(1)}, u32[]{:S(2)}, u32[]{:S(2)}) %collective-permute-start.26) | collective-permute-done | bytes 213024 | tf_op jit(solution)/shard_map/ppermute | solution.py:669
  102.0 0.7 sum_2.4
  102.7 1.3 collective-permute-start.17
  104.1 0.7 sum_1.4
  104.9 0.7 sum_0.4
  105.7 1.6 collective-permute-start.3
  107.3 1.0 collective-permute-done.27.got
  108.3 0.6 gather_3.2.own
  108.9 1.1 collective-permute-start.28
  110.0 2.1 %collective-permute-done.17.got = bf16[608,256]{1,0:T(8,128)(2,1)S(1)} collective-permute-done((bf16[608,256]{1,0:T(8,128)(2,1)S(1)}, bf16[608,256]{1,0:T(8,128)(2,1)S(1)}, u32[]{:S(2)}, u32[]{:S(2)}) %collective-permute-start.17) | collective-permute-done | bytes 311328 | tf_op jit(solution)/shard_map/ppermute | solution.py:669
  112.2 0.7 sum_2.5
  112.8 1.4 collective-permute-start.18
  114.3 0.7 sum_1.5
  115.0 1.7 collective-permute-start.11
  116.7 0.7 sum_0.5
  117.5 1.1 collective-permute-done.18.got
  118.6 2.1 %collective-permute-start.19 = (bf16[320,256]{1,0:T(8,128)(2,1)S(1)}, bf16[320,256]{1,0:T(8,128)(2,1)S(1)}, u32[]{:S(2)}, u32[]{:S(2)}) collective-permute-start(bf16[320,256]{1,0:T(8,128)(2,1)S(1)} %get-tuple-element.112.keep), channel_id=1, source_target_pairs={{0,16},{1,17},{2,18},{3,19},{4,20},{5,21},{6,22},{7,23},{8,24},{9,... | collective-permute-start | bytes 491528 | tf_op jit(solution)/shard_map/ppermute | solution.py:669
  121.2 1.5 collective-permute-start.12
  122.7 1.3 collective-permute-done.4.got
  124.1 1.6 collective-permute-start.5
  125.8 0.6 gather_3.3.refs_1_
  126.4 1.1 collective-permute-start.29
  127.5 8.8 %collective-permute-done.19.got = bf16[320,256]{1,0:T(8,128)(2,1)S(1)} collective-permute-done((bf16[320,256]{1,0:T(8,128)(2,1)S(1)}, bf16[320,256]{1,0:T(8,128)(2,1)S(1)}, u32[]{:S(2)}, u32[]{:S(2)}) %collective-permute-start.19) | collective-permute-done | bytes 163872 | tf_op jit(solution)/shard_map/ppermute | solution.py:669
  136.4 1.1 collective-permute-start.20
  137.6 2.3 %collective-permute-done.12.got = bf16[320,256]{1,0:T(8,128)(2,1)S(1)} collective-permute-done((bf16[320,256]{1,0:T(8,128)(2,1)S(1)}, bf16[320,256]{1,0:T(8,128)(2,1)S(1)}, u32[]{:S(2)}, u32[]{:S(2)}) %collective-permute-start.12) | collective-permute-done | bytes 163872 | tf_op jit(solution)/shard_map/ppermute | solution.py:669
  139.9 1.0 collective-permute-start.13
  140.9 1.6 collective-permute-done.5.got
  142.7 0.6 gather_2.2.own
  143.3 1.0 collective-permute-start.21
  144.3 1.1 collective-permute-done.13.got
  145.9 1.0 collective-permute-start.14
  146.9 7.0 %collective-permute-done.6.got = bf16[320,256]{1,0:T(8,128)(2,1)S(1)} collective-permute-done((bf16[320,256]{1,0:T(8,128)(2,1)S(1)}, bf16[320,256]{1,0:T(8,128)(2,1)S(1)}, u32[]{:S(2)}, u32[]{:S(2)}) %collective-permute-start.6) | collective-permute-done | bytes 163872 | tf_op jit(solution)/shard_map/ppermute | solution.py:669
  154.5 1.4 collective-permute-start.7
  157.7 1.4 collective-permute-start.15
  159.1 5.5 %collective-permute-done.7.got = bf16[576,256]{1,0:T(8,128)(2,1)S(1)} collective-permute-done((bf16[576,256]{1,0:T(8,128)(2,1)S(1)}, bf16[576,256]{1,0:T(8,128)(2,1)S(1)}, u32[]{:S(2)}, u32[]{:S(2)}) %collective-permute-start.7) | collective-permute-done | bytes 294944 | tf_op jit(solution)/shard_map/ppermute | solution.py:669
  165.1 1.4 collective-permute-start.8
  166.5 2.0 %write_3.1 = (f32[9216,256]{1,0:T(8,128)}, bf16[800,256]{1,0:T(8,128)(2,1)S(1)}) custom-call(s32[2]{0:T(128)S(1)} %copy-done.5, bf16[1536,256]{1,0:T(8,128)(2,1)S(1)} %gather_3.3.refs_1_, bf16[1536,256]{1,0:T(8,128)(2,1)S(1)} %collective-permute-done.29.refs_2_, f32[8,256]{1,0:T(8,128)S(1)} %get-tuple-element.127.refs_3_.vec), custom_call_target="tpu_custom_call" | custom-call | tf_op jit(solution)/shard_map/write_3/pallas_call | solution.py:718
  169.1 1.5 feature_gradient.1
  172.1 2.0 %write_2.1.refs_3_ = f32[9216,256]{1,0:T(8,128)} custom-call(s32[2]{0:T(128)S(1)} %copy-done.5, bf16[1152,256]{1,0:T(8,128)(2,1)S(1)} %gather_2.3.refs_1_, bf16[1152,256]{1,0:T(8,128)(2,1)S(1)} %collective-permute-done.22.refs_2_, f32[9216,256]{1,0:T(8,128)} %get-tuple-element.128.refs_3_), custom_call_target="tpu_custom_call", output_to_operand_aliasing={{}: (3, {})} | custom-call | tf_op jit(solution)/shard_map/write_2/pallas_call | solution.py:718
  174.2 2.0 %write_1.1.refs_3_ = f32[9216,256]{1,0:T(8,128)} custom-call(s32[2]{0:T(128)S(1)} %copy-done.5, bf16[1152,256]{1,0:T(8,128)(2,1)S(1)} %gather_1.3.refs_1_, bf16[1152,256]{1,0:T(8,128)(2,1)S(1)} %collective-permute-done.15.refs_2_, f32[9216,256]{1,0:T(8,128)} %write_2.1.refs_3_), custom_call_target="tpu_custom_call", output_to_operand_aliasing={{}: (3, {})} | custom-call | tf_op jit(solution)/shard_map/write_1/pallas_call | solution.py:718
  176.2 2.0 %write_0.1 = f32[9216,256]{1,0:T(8,128)} custom-call(s32[2]{0:T(128)S(1)} %copy-done.5, bf16[1152,256]{1,0:T(8,128)(2,1)S(1)} %gather_0.3.refs_1_, bf16[1152,256]{1,0:T(8,128)(2,1)S(1)} %collective-permute-done.8.refs_2_, f32[9216,256]{1,0:T(8,128)} %write_1.1.refs_3_), custom_call_target="tpu_custom_call", output_to_operand_aliasing={{}: (3, {})} | custom-call | tf_op jit(solution)/shard_map/write_0/pallas_call | solution.py:718
  178.3 1.2 head_gradients.1
  179.9 0.6 slice_reduce_fusion
  (60 shorter events, 10.1 us)
Async XLA Ops:
  0.6 48.8 %copy-start.6 = (f32[1,4,256]{2,1,0:T(4,128)S(1)}, f32[1,4,256]{2,1,0:T(4,128)}, u32[]{:S(2)}) copy-start(f32[1,4,256]{2,1,0:T(4,128)} %param.16) | copy-start | bytes 12292
  0.6 48.7 %copy-start.7 = (f32[1,4,256]{2,1,0:T(4,128)S(1)}, f32[1,4,256]{2,1,0:T(4,128)}, u32[]{:S(2)}) copy-start(f32[1,4,256]{2,1,0:T(4,128)} %param.17) | copy-start | bytes 12292
  0.7 2.0 %collective-permute-start = (bf16[1364,128]{1,0:T(8,128)(2,1)}, bf16[1364,128]{1,0:T(8,128)(2,1)S(1)}, u32[]{:S(2)}, u32[]{:S(2)}) collective-permute-start(bf16[1364,128]{1,0:T(8,128)(2,1)} %bitcast.49), channel_id=1, source_target_pairs={{0,1},{1,0},{2,3},{3,2},{4,5},{5,4},{6,7},{7,6},{8,9},{9,8},{10,11... | collective-permute-start | bytes 1047560 | tf_op jit(solution)/shard_map/ppermute | solution.py:749
  1.8 43.0 %copy-start.5 = (s32[2]{0:T(128)S(1)}, s32[2]{0:T(128)}, u32[]{:S(2)}) copy-start(s32[2]{0:T(128)} %pad_add_fusion.place.refs_0_) | copy-start | bytes 28
  2.7 0.7 copy-start.10
  31.3 13.4 %collective-permute-start.23 = (bf16[1568,256]{1,0:T(8,128)(2,1)}, bf16[1568,256]{1,0:T(8,128)(2,1)S(1)}, u32[]{:S(2)}, u32[]{:S(2)}) collective-permute-start(bf16[1568,256]{1,0:T(8,128)(2,1)} %get-tuple-element.116), channel_id=1, source_target_pairs={{0,8},{1,3},{2,10},{3,1},{4,12},{5,7},{6,14},{7,5},{8,0},{9,11},{1... | collective-permute-start | bytes 2408456 | tf_op jit(solution)/shard_map/ppermute | solution.py:669
  44.7 1.1 copy-start.3
  45.8 0.7 copy-start.8
  47.4 34.0 %collective-permute-start.24 = (bf16[800,256]{1,0:T(8,128)(2,1)S(1)}, bf16[800,256]{1,0:T(8,128)(2,1)S(1)}, u32[]{:S(2)}, u32[]{:S(2)}) collective-permute-start(bf16[800,256]{1,0:T(8,128)(2,1)S(1)} %get-tuple-element.119), channel_id=1, source_target_pairs={{0,4},{1,9},{2,6},{3,11},{4,0},{5,13},{6,2},{7,15},{8,12},{9,1},{1... | collective-permute-start | bytes 1228808 | tf_op jit(solution)/shard_map/ppermute | solution.py:669
  49.4 2.2 %copy-start = (f32[3,1408,256]{2,1,0:T(8,128)S(1)}, f32[3,1408,256]{2,1,0:T(8,128)}, u32[]{:S(2)}) copy-start(f32[3,1408,256]{2,1,0:T(8,128)} %get-tuple-element.72.z_hbm) | copy-start | bytes 12976132
  51.6 1.6 copy-start.1
  53.2 1.4 copy-start.2
  54.6 0.8 copy-start.4
  62.7 39.3 %collective-permute-start.16 = (bf16[1184,256]{1,0:T(8,128)(2,1)S(1)}, bf16[1184,256]{1,0:T(8,128)(2,1)S(1)}, u32[]{:S(2)}, u32[]{:S(2)}) collective-permute-start(bf16[1184,256]{1,0:T(8,128)(2,1)S(1)} %get-tuple-element.104), channel_id=1, source_target_pairs={{0,8},{1,3},{2,10},{3,1},{4,12},{5,7},{6,14},{7,5},{8,0},{9,11},{1... | collective-permute-start | bytes 1818632 | tf_op jit(solution)/shard_map/ppermute | solution.py:669
  71.6 32.4 %collective-permute-start.9 = (bf16[1184,256]{1,0:T(8,128)(2,1)S(1)}, bf16[1184,256]{1,0:T(8,128)(2,1)S(1)}, u32[]{:S(2)}, u32[]{:S(2)}) collective-permute-start(bf16[1184,256]{1,0:T(8,128)(2,1)S(1)} %get-tuple-element.92), channel_id=1, source_target_pairs={{0,2},{1,5},{2,0},{3,7},{4,6},{5,1},{6,4},{7,3},{8,10},{9,13},{10,... | collective-permute-start | bytes 1818632 | tf_op jit(solution)/shard_map/ppermute | solution.py:669
  80.7 24.2 %collective-permute-start.2 = (bf16[1184,256]{1,0:T(8,128)(2,1)S(1)}, bf16[1184,256]{1,0:T(8,128)(2,1)S(1)}, u32[]{:S(2)}, u32[]{:S(2)}) collective-permute-start(bf16[1184,256]{1,0:T(8,128)(2,1)S(1)} %get-tuple-element.80), channel_id=1, source_target_pairs={{0,4},{1,9},{2,6},{3,11},{4,0},{5,13},{6,2},{7,15},{8,12},{9,1},{1... | collective-permute-start | bytes 1818632 | tf_op jit(solution)/shard_map/ppermute | solution.py:669
  82.0 5.9 %collective-permute-start.25 = (bf16[416,256]{1,0:T(8,128)(2,1)S(1)}, bf16[416,256]{1,0:T(8,128)(2,1)S(1)}, u32[]{:S(2)}, u32[]{:S(2)}) collective-permute-start(bf16[416,256]{1,0:T(8,128)(2,1)S(1)} %get-tuple-element.122), channel_id=1, source_target_pairs={{0,2},{1,5},{2,0},{3,7},{4,6},{5,1},{6,4},{7,3},{8,10},{9,13},{10,... | collective-permute-start | bytes 638984 | tf_op jit(solution)/shard_map/ppermute | solution.py:669
  88.1 13.5 %collective-permute-start.26 = (bf16[416,256]{1,0:T(8,128)(2,1)S(1)}, bf16[416,256]{1,0:T(8,128)(2,1)S(1)}, u32[]{:S(2)}, u32[]{:S(2)}) collective-permute-start(bf16[416,256]{1,0:T(8,128)(2,1)S(1)} %get-tuple-element.124.keep), channel_id=1, source_target_pairs={{0,16},{1,17},{2,18},{3,19},{4,20},{5,21},{6,22},{7,23},{8,24},{9,... | collective-permute-start | bytes 638984 | tf_op jit(solution)/shard_map/ppermute | solution.py:669
  101.7 6.6 %collective-permute-start.27 = (bf16[416,256]{1,0:T(8,128)(2,1)S(1)}, bf16[416,256]{1,0:T(8,128)(2,1)S(1)}, u32[]{:S(2)}, u32[]{:S(2)}) collective-permute-start(bf16[416,256]{1,0:T(8,128)(2,1)S(1)} %get-tuple-element.126.own), channel_id=1, source_target_pairs={{0,2},{1,5},{2,0},{3,7},{4,6},{5,1},{6,4},{7,3},{8,10},{9,13},{10,... | collective-permute-start | bytes 638984 | tf_op jit(solution)/shard_map/ppermute | solution.py:669
  102.7 9.4 %collective-permute-start.17 = (bf16[608,256]{1,0:T(8,128)(2,1)S(1)}, bf16[608,256]{1,0:T(8,128)(2,1)S(1)}, u32[]{:S(2)}, u32[]{:S(2)}) collective-permute-start(bf16[608,256]{1,0:T(8,128)(2,1)S(1)} %get-tuple-element.107), channel_id=1, source_target_pairs={{0,4},{1,9},{2,6},{3,11},{4,0},{5,13},{6,2},{7,15},{8,12},{9,1},{1... | collective-permute-start | bytes 933896 | tf_op jit(solution)/shard_map/ppermute | solution.py:669
  104.8 9.4 %collective-permute-start.10 = (bf16[608,256]{1,0:T(8,128)(2,1)S(1)}, bf16[608,256]{1,0:T(8,128)(2,1)S(1)}, u32[]{:S(2)}, u32[]{:S(2)}) collective-permute-start(bf16[608,256]{1,0:T(8,128)(2,1)S(1)} %get-tuple-element.95), channel_id=1, source_target_pairs={{0,8},{1,3},{2,10},{3,1},{4,12},{5,7},{6,14},{7,5},{8,0},{9,11},{1... | collective-permute-start | bytes 933896 | tf_op jit(solution)/shard_map/ppermute | solution.py:669
  105.7 11.0 %collective-permute-start.3 = (bf16[608,256]{1,0:T(8,128)(2,1)S(1)}, bf16[608,256]{1,0:T(8,128)(2,1)S(1)}, u32[]{:S(2)}, u32[]{:S(2)}) collective-permute-start(bf16[608,256]{1,0:T(8,128)(2,1)S(1)} %get-tuple-element.83), channel_id=1, source_target_pairs={{0,2},{1,5},{2,0},{3,7},{4,6},{5,1},{6,4},{7,3},{8,10},{9,13},{10,... | collective-permute-start | bytes 933896 | tf_op jit(solution)/shard_map/ppermute | solution.py:669
  108.9 16.9 %collective-permute-start.28 = (bf16[768,256]{1,0:T(8,128)(2,1)S(1)}, bf16[768,256]{1,0:T(8,128)(2,1)S(1)}, u32[]{:S(2)}, u32[]{:S(2)}) collective-permute-start(bf16[768,256]{1,0:T(8,128)(2,1)S(1)} %gather_3.2.own), channel_id=1, source_target_pairs={{0,4},{1,9},{2,6},{3,11},{4,0},{5,13},{6,2},{7,15},{8,12},{9,1},{1... | collective-permute-start | bytes 1179656 | tf_op jit(solution)/shard_map/ppermute | solution.py:669
  112.8 5.7 %collective-permute-start.18 = (bf16[320,256]{1,0:T(8,128)(2,1)S(1)}, bf16[320,256]{1,0:T(8,128)(2,1)S(1)}, u32[]{:S(2)}, u32[]{:S(2)}) collective-permute-start(bf16[320,256]{1,0:T(8,128)(2,1)S(1)} %get-tuple-element.110), channel_id=1, source_target_pairs={{0,2},{1,5},{2,0},{3,7},{4,6},{5,1},{6,4},{7,3},{8,10},{9,13},{10,... | collective-permute-start | bytes 491528 | tf_op jit(solution)/shard_map/ppermute | solution.py:669
  115.0 6.2 %collective-permute-start.11 = (bf16[320,256]{1,0:T(8,128)(2,1)S(1)}, bf16[320,256]{1,0:T(8,128)(2,1)S(1)}, u32[]{:S(2)}, u32[]{:S(2)}) collective-permute-start(bf16[320,256]{1,0:T(8,128)(2,1)S(1)} %get-tuple-element.98), channel_id=1, source_target_pairs={{0,4},{1,9},{2,6},{3,11},{4,0},{5,13},{6,2},{7,15},{8,12},{9,1},{1... | collective-permute-start | bytes 491528 | tf_op jit(solution)/shard_map/ppermute | solution.py:669
  117.4 6.6 %collective-permute-start.4 = (bf16[320,256]{1,0:T(8,128)(2,1)S(1)}, bf16[320,256]{1,0:T(8,128)(2,1)S(1)}, u32[]{:S(2)}, u32[]{:S(2)}) collective-permute-start(bf16[320,256]{1,0:T(8,128)(2,1)S(1)} %get-tuple-element.86), channel_id=1, source_target_pairs={{0,8},{1,3},{2,10},{3,1},{4,12},{5,7},{6,14},{7,5},{8,0},{9,11},{1... | collective-permute-start | bytes 491528 | tf_op jit(solution)/shard_map/ppermute | solution.py:669
  118.6 17.7 %collective-permute-start.19 = (bf16[320,256]{1,0:T(8,128)(2,1)S(1)}, bf16[320,256]{1,0:T(8,128)(2,1)S(1)}, u32[]{:S(2)}, u32[]{:S(2)}) collective-permute-start(bf16[320,256]{1,0:T(8,128)(2,1)S(1)} %get-tuple-element.112.keep), channel_id=1, source_target_pairs={{0,16},{1,17},{2,18},{3,19},{4,20},{5,21},{6,22},{7,23},{8,24},{9,... | collective-permute-start | bytes 491528 | tf_op jit(solution)/shard_map/ppermute | solution.py:669
  121.2 18.6 %collective-permute-start.12 = (bf16[320,256]{1,0:T(8,128)(2,1)S(1)}, bf16[320,256]{1,0:T(8,128)(2,1)S(1)}, u32[]{:S(2)}, u32[]{:S(2)}) collective-permute-start(bf16[320,256]{1,0:T(8,128)(2,1)S(1)} %get-tuple-element.100.keep), channel_id=1, source_target_pairs={{0,16},{1,17},{2,18},{3,19},{4,20},{5,21},{6,22},{7,23},{8,24},{9,... | collective-permute-start | bytes 491528 | tf_op jit(solution)/shard_map/ppermute | solution.py:669
  124.1 45.0 %copy-start.9 = (f32[256]{0:T(256)S(1)}, f32[256]{0:T(256)}, u32[]{:S(2)}) copy-start(f32[256]{0:T(256)} %param.14) | copy-start | bytes 3076
  124.1 18.4 %collective-permute-start.5 = (bf16[320,256]{1,0:T(8,128)(2,1)S(1)}, bf16[320,256]{1,0:T(8,128)(2,1)S(1)}, u32[]{:S(2)}, u32[]{:S(2)}) collective-permute-start(bf16[320,256]{1,0:T(8,128)(2,1)S(1)} %get-tuple-element.88.keep), channel_id=1, source_target_pairs={{0,16},{1,17},{2,18},{3,19},{4,20},{5,21},{6,22},{7,23},{8,24},{9,... | collective-permute-start | bytes 491528 | tf_op jit(solution)/shard_map/ppermute | solution.py:669
  126.4 40.1 %collective-permute-start.29 = (bf16[1536,256]{1,0:T(8,128)(2,1)S(1)}, bf16[1536,256]{1,0:T(8,128)(2,1)S(1)}, u32[]{:S(2)}, u32[]{:S(2)}) collective-permute-start(bf16[1536,256]{1,0:T(8,128)(2,1)S(1)} %gather_3.3.refs_1_), channel_id=1, source_target_pairs={{0,8},{1,3},{2,10},{3,1},{4,12},{5,7},{6,14},{7,5},{8,0},{9,11},{1... | collective-permute-start | bytes 2359304 | tf_op jit(solution)/shard_map/ppermute | solution.py:669
  136.4 6.2 %collective-permute-start.20 = (bf16[320,256]{1,0:T(8,128)(2,1)S(1)}, bf16[320,256]{1,0:T(8,128)(2,1)S(1)}, u32[]{:S(2)}, u32[]{:S(2)}) collective-permute-start(bf16[320,256]{1,0:T(8,128)(2,1)S(1)} %get-tuple-element.114.own), channel_id=1, source_target_pairs={{0,2},{1,5},{2,0},{3,7},{4,6},{5,1},{6,4},{7,3},{8,10},{9,13},{10,... | collective-permute-start | bytes 491528 | tf_op jit(solution)/shard_map/ppermute | solution.py:669
  139.9 5.4 %collective-permute-start.13 = (bf16[320,256]{1,0:T(8,128)(2,1)S(1)}, bf16[320,256]{1,0:T(8,128)(2,1)S(1)}, u32[]{:S(2)}, u32[]{:S(2)}) collective-permute-start(bf16[320,256]{1,0:T(8,128)(2,1)S(1)} %get-tuple-element.102.own), channel_id=1, source_target_pairs={{0,4},{1,9},{2,6},{3,11},{4,0},{5,13},{6,2},{7,15},{8,12},{9,1},{1... | collective-permute-start | bytes 491528 | tf_op jit(solution)/shard_map/ppermute | solution.py:669
  142.6 11.3 %collective-permute-start.6 = (bf16[320,256]{1,0:T(8,128)(2,1)S(1)}, bf16[320,256]{1,0:T(8,128)(2,1)S(1)}, u32[]{:S(2)}, u32[]{:S(2)}) collective-permute-start(bf16[320,256]{1,0:T(8,128)(2,1)S(1)} %get-tuple-element.90.own), channel_id=1, source_target_pairs={{0,8},{1,3},{2,10},{3,1},{4,12},{5,7},{6,14},{7,5},{8,0},{9,11},{1... | collective-permute-start | bytes 491528 | tf_op jit(solution)/shard_map/ppermute | solution.py:669
  143.3 12.6 %collective-permute-start.21 = (bf16[576,256]{1,0:T(8,128)(2,1)S(1)}, bf16[576,256]{1,0:T(8,128)(2,1)S(1)}, u32[]{:S(2)}, u32[]{:S(2)}) collective-permute-start(bf16[576,256]{1,0:T(8,128)(2,1)S(1)} %gather_2.2.own), channel_id=1, source_target_pairs={{0,4},{1,9},{2,6},{3,11},{4,0},{5,13},{6,2},{7,15},{8,12},{9,1},{1... | collective-permute-start | bytes 884744 | tf_op jit(solution)/shard_map/ppermute | solution.py:669
  145.9 11.1 %collective-permute-start.14 = (bf16[576,256]{1,0:T(8,128)(2,1)S(1)}, bf16[576,256]{1,0:T(8,128)(2,1)S(1)}, u32[]{:S(2)}, u32[]{:S(2)}) collective-permute-start(bf16[576,256]{1,0:T(8,128)(2,1)S(1)} %gather_1.2.own), channel_id=1, source_target_pairs={{0,8},{1,3},{2,10},{3,1},{4,12},{5,7},{6,14},{7,5},{8,0},{9,11},{1... | collective-permute-start | bytes 884744 | tf_op jit(solution)/shard_map/ppermute | solution.py:669
  154.5 10.0 %collective-permute-start.7 = (bf16[576,256]{1,0:T(8,128)(2,1)S(1)}, bf16[576,256]{1,0:T(8,128)(2,1)S(1)}, u32[]{:S(2)}, u32[]{:S(2)}) collective-permute-start(bf16[576,256]{1,0:T(8,128)(2,1)S(1)} %gather_0.2.own), channel_id=1, source_target_pairs={{0,2},{1,5},{2,0},{3,7},{4,6},{5,1},{6,4},{7,3},{8,10},{9,13},{10,... | collective-permute-start | bytes 884744 | tf_op jit(solution)/shard_map/ppermute | solution.py:669
  156.5 15.6 %collective-permute-start.22 = (bf16[1152,256]{1,0:T(8,128)(2,1)S(1)}, bf16[1152,256]{1,0:T(8,128)(2,1)S(1)}, u32[]{:S(2)}, u32[]{:S(2)}) collective-permute-start(bf16[1152,256]{1,0:T(8,128)(2,1)S(1)} %gather_2.3.refs_1_), channel_id=1, source_target_pairs={{0,8},{1,3},{2,10},{3,1},{4,12},{5,7},{6,14},{7,5},{8,0},{9,11},{1... | collective-permute-start | bytes 1769480 | tf_op jit(solution)/shard_map/ppermute | solution.py:669
  157.7 16.5 %collective-permute-start.15 = (bf16[1152,256]{1,0:T(8,128)(2,1)S(1)}, bf16[1152,256]{1,0:T(8,128)(2,1)S(1)}, u32[]{:S(2)}, u32[]{:S(2)}) collective-permute-start(bf16[1152,256]{1,0:T(8,128)(2,1)S(1)} %gather_1.3.refs_1_), channel_id=1, source_target_pairs={{0,2},{1,5},{2,0},{3,7},{4,6},{5,1},{6,4},{7,3},{8,10},{9,13},{10,... | collective-permute-start | bytes 1769480 | tf_op jit(solution)/shard_map/ppermute | solution.py:669
  165.1 11.1 %collective-permute-start.8 = (bf16[1152,256]{1,0:T(8,128)(2,1)S(1)}, bf16[1152,256]{1,0:T(8,128)(2,1)S(1)}, u32[]{:S(2)}, u32[]{:S(2)}) collective-permute-start(bf16[1152,256]{1,0:T(8,128)(2,1)S(1)} %gather_0.3.refs_1_), channel_id=1, source_target_pairs={{0,4},{1,9},{2,6},{3,11},{4,0},{5,13},{6,2},{7,15},{8,12},{9,1},{1... | collective-permute-start | bytes 1769480 | tf_op jit(solution)/shard_map/ppermute | solution.py:669
  166.5 2.6 %collective-permute-start.1 = (bf16[1408,128]{1,0:T(8,128)(2,1)S(1)}, bf16[1408,128]{1,0:T(8,128)(2,1)S(1)}, u32[]{:S(2)}, u32[]{:S(2)}) collective-permute-start(bf16[1408,128]{1,0:T(8,128)(2,1)S(1)} %get-tuple-element.78), channel_id=1, source_target_pairs={{0,1},{1,0},{2,3},{3,2},{4,5},{5,4},{6,7},{7,6},{8,9},{9,8},{10,11... | collective-permute-start | bytes 1081352 | tf_op jit(solution)/shard_map/ppermute | solution.py:765
  168.6 9.7 %collective-permute-start.30 = (bf16[800,256]{1,0:T(8,128)(2,1)S(1)}, bf16[800,256]{1,0:T(8,128)(2,1)S(1)}, u32[]{:S(2)}, u32[]{:S(2)}) collective-permute-start(bf16[800,256]{1,0:T(8,128)(2,1)S(1)} %get-tuple-element.132.own), channel_id=1, source_target_pairs={{0,1},{1,0},{2,3},{3,2},{4,5},{5,4},{6,7},{7,6},{8,9},{9,8},{10,11... | collective-permute-start | bytes 1228808 | tf_op jit(solution)/shard_map/ppermute | solution.py:774

commit v3 on v2

v3 whole, which is shorter than its diff:
```python
import functools

import jax
import jax.numpy as jnp
from jax import lax
from jax.experimental import pallas as pl
from jax.experimental.pallas import tpu as pltpu
from jax.sharding import PartitionSpec as P

C = 256
GROUP = 8
CLASSES = 80
HEAD = 85
LANES = 128
LAYERS = 4
CELLS = 1408
PIX = 1364
COUNTS = (1024, 256, 64, 16, 4)
PARTS = ((0, 1024, 64, 64), (1024, 256, 1152, 32), (1280, 128, 1440, 16))
PADDED = 1584
GAPS = ((0, 64), (1088, 64), (1408, 32), (1568, 16))
TILE = 64
BLOCKS = tuple((256 * i, 256, 64 + 256 * i, 64, 0) for i in range(4)) + ((1024, 256, 1152, 32, 1), (1280, 128, 1440, 16, 2))
EPS = 1e-05
f32 = jnp.float32
bf16 = jnp.bfloat16
VMEM = pl.BlockSpec(memory_space=pltpu.VMEM)
SMEM = pl.BlockSpec(memory_space=pltpu.SMEM)
HBM = pl.BlockSpec(memory_space=pltpu.HBM)


VEC = 32
FEATURES, HEADS = 8, 9
COST = 300000000
COSTS = {
    "add_3_3": 3000000000,
    "join_0_5": 2000000000,
    "add_3_4": 3000000000,
    "halve_3_2": 1000000000,
    "join_1_6": 300000000,
    "add_2_4": 300000000,
    "feature_gradient": 3000000000,
    "join_2_5": 1000000000,
    "write_1_got": 1000000,
    "add_1_4": 2000000000,
    "join_2_6": 1000000,
    "write_3_got": 300000000,
    "layer_gradients_1": 1000000,
    "write_0_own": 3000000000,
    "write_2_own": 1500000000,
    "halve_2_1": 1000000,
    "halve_1_2": 100000000,
    "add_1_3": 100000000,
    "head_gradients": 1000000,
    "halve_0_2": 1000000,
    "add_0_3": 100000000,
    "write_1_own": 2000000000,
    "layer_gradients_2": 1000000,
    "join_3_6": 2000000000,
    "join_3_5": 1000000000,
    "halve_3_1": 5000000000,
    "layer_gradients_0": 100000000,
}
FIRST_MIB = 32
MIDDLE_MIB = 24
SPLITS = 3


def params(mib=56):
    return pltpu.CompilerParams(vmem_limit_bytes=mib << 20)


def tail_masks():
    row = lax.broadcasted_iota(jnp.int32, (TILE, C), 0)
    third = ((row >= 16) & (row < 24)) | ((row >= 32) & (row < 40))
    fourth = (row >= 26) & (row < 30)
    return third, fourth


def pick(third, fourth, vec):
    return jnp.where(third, vec[3:4], jnp.where(fourth, vec[4:5], 0.0))


def fold(tile):
    return jnp.sum(tile.reshape(TILE // 8, 8, tile.shape[1]), axis=0)


def group_sum(vec):
    lane = lax.broadcasted_iota(jnp.int32, vec.shape, 1)
    for step in (1, 2, 4):
        up = pltpu.roll(vec, vec.shape[1] - step, 1)
        down = pltpu.roll(vec, step, 1)
        vec = vec + jnp.where((lane & step) == 0, up, down)
    return vec


def counts_column():
    row = lax.broadcasted_iota(jnp.int32, (8, C), 0)
    out = jnp.full((8, C), 1.0, f32)
    for level, cells in enumerate(COUNTS):
        out = jnp.where(row == level, 1.0 / (cells * GROUP), out)
    return out


def stack_rows(rows):
    row = lax.broadcasted_iota(jnp.int32, (8, rows[0].shape[1]), 0)
    out = jnp.zeros((8, rows[0].shape[1]), f32)
    for place, value in enumerate(rows):
        out = jnp.where(row == place, jnp.sum(value, axis=0, keepdims=True), out)
    return out


def each_tile(step, init):
    results = []
    for level, (tiles, cell, row, width) in enumerate(((16, 0, 64, 64), (4, 1024, 1152, 32), (1, 1280, 1440, 16))):
        carry = init

        def run(i, carry, level=level, cell=cell, row=row, width=width):
            at = pl.multiple_of(i * TILE, TILE)
            return step(level, cell + at, row + at, width, carry)

        if tiles == 1:
            carry = step(level, cell, row, width, carry)
        else:
            carry = lax.fori_loop(0, tiles, run, carry, unroll=2)
        results.append(carry)
    results.append(step(3, 1344, 1504, 16, init))
    return results


def write_shifted(buf, row, width, tile, lanes, flip):
    at = lax.broadcasted_iota(jnp.int32, tile.shape, 0) & (width - 1)
    before = jnp.where(at == 0, 0.0, pltpu.roll(tile, 1, 0))
    after = jnp.where(at == width - 1, 0.0, pltpu.roll(tile, TILE - 1, 0))
    if flip:
        before, after = after, before
    rows = pl.ds(row, TILE)
    buf[rows, 0:lanes] = before.astype(bf16)
    buf[rows, lanes : 2 * lanes] = tile.astype(bf16)
    buf[rows, 2 * lanes : 3 * lanes] = after.astype(bf16)


def clear_gaps(buf):
    for row, rows in GAPS:
        buf[row : row + rows, :] = jnp.zeros((rows, buf.shape[1]), bf16)


def conv_block(block, buf, weight):
    _, cells, row, width, _ = block
    left = jnp.concatenate([buf[row + d * width : row + d * width + cells, :] for d in (-1, 0, 1)], axis=1)
    return jnp.dot(left, weight, preferred_element_type=f32)


def conv_back_block(block, buf, weight):
    _, cells, row, width, _ = block
    total = None
    for i in range(3):
        at = row - (i - 1) * width
        for j in range(3):
            term = lax.dot_general(
                buf[at : at + cells, j * C : (j + 1) * C],
                weight(i * 3 + j),
                (((1,), (1,)), ((), ())),
                preferred_element_type=f32,
            )
            total = term if total is None else total + term
    return total


def kernel_grad(turned, buf, i):
    total = None
    for cell, cells, row, width in PARTS:
        at = row - (i - 1) * width
        term = jnp.dot(turned[:, cell : cell + cells], buf[at : at + cells, :], preferred_element_type=f32)
        total = term if total is None else total + term
    return total


def tiles_of(block):
    cell, cells, row, width, level = block
    return [(level if at == 0 or level < 2 else 3, cell + at, row + at, width, at) for at in range(0, cells, TILE)]


def pipelined(produce, consume):
    produce(BLOCKS[0])
    for i, block in enumerate(BLOCKS):
        if i + 1 < len(BLOCKS):
            produce(BLOCKS[i + 1])
        consume(block)


class Stats:
    def __init__(self):
        self.center = None
        self.sums = [jnp.zeros((8, C), f32), jnp.zeros((8, C), f32)]
        self.rows = []

    def own(self, tile, cells, mask=None):
        kept = tile if mask is None else jnp.where(mask, tile, 0.0)
        mean = jnp.sum(kept, axis=0, keepdims=True) * (1.0 / cells)
        d = tile - mean
        d = d if mask is None else jnp.where(mask, d, 0.0)
        self.rows.append((mean, jnp.sum(d * d, axis=0, keepdims=True)))

    def add(self, block, z):
        level = block[4]
        if level == 0:
            if self.center is None:
                self.center = jnp.sum(z, axis=0, keepdims=True) * (1.0 / z.shape[0])
            d = z - self.center
            wide = lambda v: jnp.sum(v.reshape(z.shape[0] // 8, 8, C), axis=0)
            self.sums = [self.sums[0] + wide(d), self.sums[1] + wide(d * d)]
        elif level == 1:
            self.own(z, COUNTS[1])
        else:
            third, fourth = tail_masks()
            self.own(z[:TILE], COUNTS[2])
            self.own(z[TILE:], COUNTS[3], third)
            self.own(z[TILE:], COUNTS[4], fourth)

    def finish(self):
        first, second = (jnp.sum(v, axis=0, keepdims=True) for v in self.sums)
        shift = first * (1.0 / COUNTS[0])
        rows = [(self.center + shift, second - first * shift)] + self.rows
        means = stack_rows([r[0] for r in rows])
        squares = stack_rows([r[1] for r in rows])
        inv_counts = counts_column()
        mean = group_sum(means) * (1.0 / GROUP)
        d = means - mean
        var = group_sum(squares * inv_counts + d * d * (1.0 / GROUP))
        return mean, lax.rsqrt(var + EPS)


def level_rows(level, vec, masks):
    if level < 3:
        return vec[level : level + 1]
    return pick(*masks, vec)


def act_tiles(block, z, scale, offset, buf, keep=None):
    masks = tail_masks()
    for level, cell, row, width, _ in tiles_of(block):
        y = z[cell : cell + TILE, :] * level_rows(level, scale, masks) + level_rows(level, offset, masks)
        a = y * (0.5 * jnp.tanh(0.5 * y) + 0.5)
        if level == 3:
            a = jnp.where(masks[0] | masks[1], a, 0.0)
        write_shifted(buf, row, width, a, C, False)
        if keep is not None:
            keep[cell : cell + TILE, :] = a.astype(bf16)


class Upward:
    def __init__(self, dy_out, z, mean, rstd, gain, shift):
        self.dy_out, self.z, self.rstd, self.neg, self.gain, self.shift = dy_out, z, rstd, -mean * rstd, gain, shift
        self.sums = [[jnp.zeros((8, C), f32), jnp.zeros((8, C), f32)] for _ in COUNTS]

    def add(self, block, da):
        masks = tail_masks()
        for level, cell, _, _, at in tiles_of(block):
            zhat = self.z[cell : cell + TILE, :] * level_rows(level, self.rstd, masks) + level_rows(level, self.neg, masks)
            y = zhat * self.gain + self.shift
            s = 0.5 * jnp.tanh(0.5 * y) + 0.5
            dy = da[at : at + TILE] * (s * (1.0 + y * (1.0 - s)))
            self.dy_out[cell : cell + TILE, :] = dy
            dyz = dy * zhat
            if level < 3:
                parts = [(level, dy, dyz)]
            else:
                parts = [(3 + k, jnp.where(m, dy, 0.0), jnp.where(m, dyz, 0.0)) for k, m in enumerate(masks)]
            for to, one, two in parts:
                self.sums[to] = [self.sums[to][0] + fold(one), self.sums[to][1] + fold(two)]

    def finish(self, sums_out):
        sums_out[0:8, :] = stack_rows([v[0] for v in self.sums])
        sums_out[8:16, :] = stack_rows([v[1] for v in self.sums])


def norm_back(dy, z, mean, rstd, gain, sums, buf):
    sum_dy, sum_dyz = sums[0:8, :], sums[8:16, :]
    inv_counts = counts_column()
    mean_e = group_sum(sum_dy * gain) * inv_counts
    mean_ez = group_sum(sum_dyz * gain) * inv_counts
    on_dy = rstd * gain
    on_zhat = rstd * mean_ez
    on_z = -on_zhat * rstd
    flat = on_zhat * mean * rstd - rstd * mean_e

    def produce(block):
        masks = tail_masks()
        for level, cell, row, width, _ in tiles_of(block):
            at = slice(cell, cell + TILE)
            dz = (
                dy[at, :] * level_rows(level, on_dy, masks)
                + z[at, :] * level_rows(level, on_z, masks)
                + level_rows(level, flat, masks)
            )
            write_shifted(buf, row, width, dz, C, True)

    return produce, [jnp.sum(v, axis=0, keepdims=True) for v in (sum_dyz, sum_dy)]


def center(buf, cells, row, lanes):
    return buf[row : row + cells, lanes : 2 * lanes]


def shape(dims, dtype):
    return jax.ShapeDtypeStruct(dims, dtype)


def pack(vec):
    high = vec.astype(bf16).astype(f32)
    middle = (vec - high).astype(bf16).astype(f32)
    low = vec - high - middle
    return jnp.concatenate([high, middle, low, jnp.zeros_like(vec)], axis=0).astype(bf16)


def unpack(block):
    parts = block.astype(f32)
    return parts[0:8] + parts[8:16] + parts[16:24]


def bit_of(order, step):
    dp = lax.axis_index("dp")
    return jnp.where(lax.axis_index("tower") == 0, dp >> order[0][step], dp >> order[1][step]) & 1


def call(kernel, token, ins, in_specs, outs, out_specs, name, scratch=(), mib=16, alias=None):
    n_in, n_out = len(ins), len(outs)

    def ordered(*refs):
        kernel(*refs[:n_in], *refs[n_in + 1 : n_in + 1 + n_out], *refs[n_in + n_out + 2 :])

    *results, token = pl.pallas_call(
        ordered,
        out_shape=list(outs) + [shape((8, LANES), f32)],
        in_specs=list(in_specs) + [HBM],
        out_specs=list(out_specs) + [HBM],
        scratch_shapes=list(scratch),
        input_output_aliases=alias or {},
        compiler_params=params(mib),
        cost_estimate=pl.CostEstimate(flops=COSTS.get(name, COST), bytes_accessed=1, transcendentals=0),
        name=name,
    )(*ins, token)
    return results, token


def split_store(bit, tap, grad, keep, send):
    half = C // 2
    low, high = grad[:half], grad[half:]
    keep[tap * half : (tap + 1) * half, :] = jnp.where(bit == 1, high, low).astype(bf16)
    send[tap * half : (tap + 1) * half, :] = jnp.where(bit == 1, low, high).astype(bf16)


def halve_kernel(taps, rows, order, step, keep, got, vec, keep_out, send_out, vec_out):
    bit = bit_of(order, step)
    half = rows // 2

    def one(t, _):
        for out, side in ((keep_out, bit), (send_out, 1 - bit)):
            at = pl.ds(pl.multiple_of(t * rows + side * half, half), half)
            to = pl.ds(pl.multiple_of(t * half, half), half)
            out[to, :] = (keep[at, :].astype(f32) + got[at, :].astype(f32)).astype(bf16)
        return 0

    lax.fori_loop(0, taps, one, 0)
    total = vec[...] + unpack(got[taps * rows :, :])
    vec_out[...] = total
    send_out[taps * half :, :] = pack(total)


def add_kernel(taps, rows, keep, got, vec, sum_out, vec_out):
    def one(t, _):
        at = pl.ds(pl.multiple_of(t * rows, rows), rows)
        sum_out[at, :] = (keep[at, :].astype(f32) + got[at, :].astype(f32)).astype(bf16)
        return 0

    lax.fori_loop(0, taps, one, 0)
    total = vec[...] + unpack(got[taps * rows :, :])
    vec_out[...] = total
    sum_out[taps * rows :, :] = pack(total)


def join_kernel(taps, rows, order, step, own, got, out):
    bit = bit_of(order, step)

    def one(t, _):
        at = pl.ds(pl.multiple_of(t * rows, rows), rows)
        out[pl.ds(pl.multiple_of((2 * t + bit) * rows, rows), rows), :] = own[at, :]
        out[pl.ds(pl.multiple_of((2 * t + 1 - bit) * rows, rows), rows), :] = got[at, :]
        return 0

    lax.fori_loop(0, taps, one, 0)


def write_half(layer, side, half_rows, out, wide, sems):
    half = C // 2
    copies = []
    for t in range(9):
        rows = slice(t * half, (t + 1) * half)
        wide[rows, :] = half_rows[rows, :].astype(f32)
        to = pl.multiple_of((layer * 9 + t) * C + side * half, half)
        copies.append(pltpu.make_async_copy(wide.at[rows], out.at[pl.ds(to, half)], sems.at[t]))
        copies[-1].start()
    return copies


def write_own_kernel(layer, order, own, *refs):
    out, wide, sems = refs[-3:]
    for copy in write_half(layer, bit_of(order, 0), own, out, wide, sems):
        copy.wait()


def write_got_kernel(layer, order, extra, got, *refs):
    bit = bit_of(order, 0)
    out, wide, sems = refs[-3 - (1 if extra else 2 if not layer else 0) :][:1] + refs[-2:]
    copies = write_half(layer, 1 - bit, got, out, wide, sems)
    half = C // 2
    if extra:
        own, vec, _, _, rest, _, _ = refs
        for t in range(extra):
            rest[pl.ds(pl.multiple_of(t * C + bit * half, half), half), :] = own[(9 + t) * half : (10 + t) * half, :]
            rest[pl.ds(pl.multiple_of(t * C + (1 - bit) * half, half), half), :] = got[(9 + t) * half : (10 + t) * half, :]
        rest[extra * C :, :] = pack(vec[...])
    elif not layer:
        *vecs, _, _, gains_out, shifts_out, _, _ = refs
        gains_out[...] = jnp.concatenate([v[0:1, :] for v in vecs], axis=0)
        shifts_out[...] = jnp.concatenate([v[1:2, :] for v in vecs], axis=0)
    for copy in copies:
        copy.wait()


def heads_kernel(own, got, vec, dhead_out, bias_out, scale_out):
    for i in range(3):
        at = slice(i * C, (i + 1) * C)
        turned = (own[at, :].astype(f32) + got[at, :].astype(f32)).T
        for j in range(3):
            dhead_out[i, j] = turned[j * HEAD : (j + 1) * HEAD, :]
    both = vec[...] + unpack(got[3 * C :, :])
    bias_out[...] = both[2:3, 0:HEAD]
    lane = lax.broadcasted_iota(jnp.int32, (8, LANES), 1)
    row = lax.broadcasted_iota(jnp.int32, (8, LANES), 0)
    sums = jnp.sum(both[:, 0:LANES], axis=1, keepdims=True)
    line = jnp.sum(jnp.where((row >= 3) & (lane == row - 3), sums, 0.0), axis=0, keepdims=True)
    scale_out[...] = line[:, 0 : len(COUNTS)]


def features_kernel(keep, got, var, out):
    half = C // 2
    inverse = lax.rsqrt(jnp.where(lax.axis_index("tower") == 0, var[:, :half], var[:, half:]) + EPS)

    def scaled(cell, cells):
        return (keep[pl.ds(cell, cells), :].astype(f32) + got[pl.ds(cell, cells), :].astype(f32)) * inverse

    def one(t, _):
        at = pl.multiple_of(t * TILE, TILE)
        out[pl.ds(at, TILE), :] = scaled(at, TILE).astype(bf16)
        return 0

    lax.fori_loop(0, 1344 // TILE, one, 0)
    tail = scaled(1344, TILE)
    out[1344:PIX, :] = jnp.concatenate([tail[16:24], tail[32:40], tail[26:30]], axis=0).astype(bf16)


def gradients_out(bit, turned, buf, keep, send):
    for i in range(3):
        grad = kernel_grad(turned, buf, i)
        for j in range(3):
            split_store(bit, i * 3 + j, grad[:, j * C : (j + 1) * C], keep, send)


def vector_rows(rows):
    row = lax.broadcasted_iota(jnp.int32, (8, C), 0)
    out = jnp.zeros((8, C), f32)
    for at, value in enumerate(rows):
        out = jnp.where(row == at, value, out)
    return out


def spread_tail(tile, scratch):
    scratch[...] = jnp.zeros(scratch.shape, f32)
    scratch[16:24, :] = tile[0:8]
    scratch[32:40, :] = tile[8:16]
    scratch[26:30, :] = tile[16:20]


def prepare_kernel(head, cls, reg, pos, hw, hg, tail):
    box = reg[...].astype(f32) * pos[...].astype(f32)
    is_class = lax.axis_index("tower") == 0
    rows = jnp.concatenate(
        [
            jnp.where(is_class, cls[...].astype(f32), 0.0),
            jnp.where(is_class, 0.0, jnp.concatenate([box, jnp.zeros((3, PIX), f32)], axis=0)),
            jnp.zeros((LANES - CLASSES - 8, PIX), f32),
        ],
        axis=0,
    )
    rows = jnp.concatenate([rows, jnp.zeros((LANES, CELLS - PIX), f32)], axis=1)
    hg[...] = rows.T
    spread_tail(jnp.concatenate([hg[1344:PIX, :]] * 2, axis=1), tail)
    hg[1344:CELLS, :] = tail[:, 0:LANES]
    for i in range(3):
        three = jnp.concatenate([head[i, j].astype(f32) for j in range(3)] + [jnp.zeros((1, C), f32)], axis=0)
        hw[i * C : (i + 1) * C, :] = three.astype(bf16)


def first_kernel(
    order, scale, own, other, bn_mean, bn_var, w_hbm, gains, shifts, head, head_bias, hw, hg_in,
    w, z_out, a_out, stats_out, dy_out, sums_out, keep_out, send_out, vec_out,
    buf, z_last, a_last, dy, sums, hg, hbuf, u, turned, tail, scale_sums, sems,
):
    loads = [pltpu.make_async_copy(w_hbm.at[l], w.at[l], sems.at[l]) for l in range(LAYERS)]
    for load in loads:
        load.start()
    half = C // 2
    tower = lax.axis_index("tower")
    clear_gaps(buf)
    clear_gaps(hbuf)
    inverse = lax.rsqrt(bn_var[...] + EPS)
    mean0 = bn_mean[...]

    def halves(rows):
        left = jnp.where(tower == 0, own[rows, :].astype(f32), other[rows, :].astype(f32))
        right = jnp.where(tower == 0, other[rows, :].astype(f32), own[rows, :].astype(f32))
        return (jnp.concatenate([left, right], axis=1) - mean0) * inverse

    def base(level, cell, row, width, carry):
        if level < 3:
            tile = halves(pl.ds(cell, TILE))
        else:
            spread_tail(halves(slice(1344, PIX)), tail)
            tile = tail[...]
        write_shifted(buf, row, width, tile, C, False)
        return carry

    each_tile(base, jnp.int32(0))
    for cell, cells, row, width in PARTS:
        a_out[0, cell : cell + cells, :] = center(buf, cells, row, C)
    scale_rows = offset_rows = None
    for l in range(LAYERS):
        z = z_out.at[l] if l < LAYERS - 1 else z_last
        stats = Stats()
        loads[l].wait()

        def consume(block, l=l, z=z, stats=stats):
            out = conv_block(block, buf, w[l])
            z[block[0] : block[0] + block[1], :] = out
            stats.add(block, out)

        if l == 0:
            for block in BLOCKS:
                consume(block)
        else:
            keep = a_out.at[l] if l < LAYERS - 1 else a_last
            before = z_out.at[l - 1]
            produce = lambda block: act_tiles(block, before, scale_rows, offset_rows, buf, keep)
            pipelined(produce, consume)
        mean, rstd = stats.finish()
        if l < LAYERS - 1:
            stats_out[l, 0:8, :] = mean
            stats_out[l, 8:16, :] = rstd
        scale_rows = rstd * gains[l : l + 1]
        offset_rows = shifts[l : l + 1] - mean * scale_rows
    for block in BLOCKS:
        act_tiles(block, z_last, scale_rows, offset_rows, buf)

    lane = lax.broadcasted_iota(jnp.int32, (TILE, LANES), 1)
    row = lax.broadcasted_iota(jnp.int32, (TILE, LANES), 0)
    third = ((row >= 16) & (row < 24)) | ((row >= 32) & (row < 40))
    fourth = (row >= 26) & (row < 30)

    @pl.when(tower == 0)
    def _():
        hg[...] = hg_in[...]
        scale_sums[...] = jnp.zeros(scale_sums.shape, f32)

    @pl.when(tower == 1)
    def _():
        for cell, cells, first, width in PARTS:
            for at in range(0, cells, 256):
                size = min(256, cells - at)
                total = None
                for i in range(3):
                    from_row = first + at + (i - 1) * width
                    for j in range(3):
                        kernel = jnp.concatenate([head[i, j], jnp.zeros((LANES - HEAD, C), bf16)], axis=0)
                        term = lax.dot_general(
                            buf[from_row : from_row + size, j * C : (j + 1) * C],
                            kernel,
                            (((1,), (1,)), ((), ())),
                            preferred_element_type=f32,
                        )
                        total = term if total is None else total + term
                u[cell + at : cell + at + size, :] = total
        bias = jnp.concatenate([head_bias[...], jnp.zeros((1, LANES - HEAD), f32)], axis=1)
        dist_lane = (lane >= CLASSES) & (lane < CLASSES + 4)

        def boxes(level, cell, row, width, carry):
            raw = u[pl.ds(cell, TILE), :] + bias
            g = hg_in[pl.ds(cell, TILE), :]
            if level < 3:
                ls = scale[0:1, level : level + 1]
                use = dist_lane
            else:
                ls = jnp.where(third, scale[0:1, 3:4], scale[0:1, 4:5])
                use = dist_lane & (third | fourth)
            weighted = jnp.where(use, g * jnp.exp(ls * raw), 0.0)
            hg[pl.ds(cell, TILE), :] = jnp.where(dist_lane, weighted * ls, g)
            term = weighted * raw
            if level < 3:
                return carry + fold(term)
            return (fold(jnp.where(third, term, 0.0)), fold(jnp.where(fourth, term, 0.0)))

        r = each_tile(boxes, jnp.zeros((8, LANES), f32))
        scale_sums[...] = stack_rows([r[0], r[1], r[2], r[3][0], r[3][1]])

    scale_sum_rows = [scale_sums[k : k + 1, :] for k in range(len(COUNTS))]

    def head_rows(level, cell, row, width, carry):
        tile = hg[pl.ds(cell, TILE), :].astype(bf16).astype(f32)
        at = lax.broadcasted_iota(jnp.int32, tile.shape, 0) & (width - 1)
        after = jnp.where(at == 0, 0.0, pltpu.roll(tile, 1, 0))
        before = jnp.where(at == width - 1, 0.0, pltpu.roll(tile, TILE - 1, 0))
        middle = pltpu.roll(tile, HEAD, 1)
        after = pltpu.roll(after, 2 * HEAD - LANES, 1)
        rows = pl.ds(row, TILE)
        hbuf[rows, 0:LANES] = jnp.where(lane < HEAD, before, middle).astype(bf16)
        hbuf[rows, LANES : 2 * LANES] = jnp.where(lane < 2 * HEAD - LANES, middle, after).astype(bf16)
        return carry + fold(tile)

    r = each_tile(head_rows, jnp.zeros((8, LANES), f32))
    bias_row = jnp.sum(r[0] + r[1] + r[2] + r[3], axis=0, keepdims=True)

    bit = bit_of(order, 0)
    a4t = jnp.concatenate([center(buf, n, r, C).T for _, n, r, _ in PARTS], axis=1)
    for i in range(3):
        split_store(bit, 9 + i, kernel_grad(a4t, hbuf, i), keep_out, send_out)
    l = LAYERS - 1
    up = Upward(dy, z_last, mean, rstd, gains[l : l + 1], shifts[l : l + 1])
    for block in BLOCKS:
        _, cells, row, width, _ = block
        left = jnp.concatenate([hbuf[row - d * width : row - d * width + cells, :] for d in (-1, 0, 1)], axis=1)
        up.add(block, jnp.dot(left, hw[...], preferred_element_type=f32))
    up.finish(sums)
    produce, norm_sums = norm_back(dy, z_last, mean, rstd, gains[l : l + 1], sums, buf)
    wide = lambda v: jnp.concatenate([v, jnp.zeros_like(v)], axis=1)
    vec = vector_rows(norm_sums + [wide(bias_row)] + [wide(v) for v in scale_sum_rows])
    vec_out[...] = vec
    send_out[12 * half :, :] = pack(vec)
    turned[...] = a_last[...].T
    layer_down(l, produce, buf, lambda tap: w[l, tap * C : (tap + 1) * C, :], z_out, stats_out, gains, shifts, dy_out, sums_out)
    gradients_out(bit, turned, buf, keep_out, send_out)


def layer_down(l, produce, buf, weight, z, stats, gains, shifts, dy_out, sums_out):
    k = l - 1
    up = Upward(dy_out, z.at[k], stats[k, 0:8, :], stats[k, 8:16, :], gains[k : k + 1], shifts[k : k + 1])
    pipelined(produce, lambda block: up.add(block, conv_back_block(block, buf, weight)))
    up.finish(sums_out)


def middle_kernel(l, order, dy, sums, z, a, stats, gains, shifts, w, *refs):
    if l:
        dy_out, sums_out, keep_out, send_out, vec_out, buf, turned = refs
    else:
        keep_half, send_half, keep_out, send_out, vec_out, buf, turned = refs
    half = C // 2
    bit = bit_of(order, 0)
    clear_gaps(buf)
    produce, norm_sums = norm_back(
        dy, z.at[l], stats[l, 0:8, :], stats[l, 8:16, :], gains[l : l + 1], sums, buf
    )
    vec = vector_rows(norm_sums)
    vec_out[...] = vec
    send_out[9 * half :, :] = pack(vec)
    turned[...] = a[l].T
    weight = lambda tap: w[l, tap * C : (tap + 1) * C, :]
    if l:
        layer_down(l, produce, buf, weight, z, stats, gains, shifts, dy_out, sums_out)
    else:
        mine = lax.axis_index("tower")

        def consume(block):
            da = conv_back_block(block, buf, weight)
            at = slice(block[0], block[0] + block[1])
            keep_half[at, :] = jnp.where(mine == 0, da[:, :half], da[:, half:])
            send_half[at, :] = jnp.where(mine == 0, da[:, half:], da[:, :half]).astype(bf16)

        pipelined(produce, consume)
    gradients_out(bit, turned, buf, keep_out, send_out)


def run_prepare(token, head, cls, reg, pos):
    return call(
        prepare_kernel,
        token,
        (head, cls, reg, pos),
        [VMEM] * 4,
        [pltpu.VMEM((3 * C, C), bf16), pltpu.VMEM((CELLS, LANES), f32)],
        [VMEM] * 2,
        "prepare",
        [pltpu.VMEM((TILE, C), f32)],
        16,
    )


def run_first(order, token, scale, own, other, mean, var, w, gains, shifts, head, bias, hw, hg):
    half = C // 2
    return call(
        functools.partial(first_kernel, order),
        token,
        (scale, own, other, mean, var, w, gains, shifts, head, bias, hw, hg),
        [VMEM] * 5 + [HBM] + [VMEM] * 6,
        [
            pltpu.VMEM((LAYERS, 9 * C, C), bf16),
            pltpu.VMEM((LAYERS - 1, CELLS, C), f32),
            pltpu.VMEM((LAYERS - 1, CELLS, C), bf16),
            pltpu.VMEM((LAYERS - 1, 16, C), f32),
            pltpu.VMEM((CELLS, C), f32),
            pltpu.VMEM((16, C), f32),
            pltpu.VMEM((12 * half, C), bf16),
            pltpu.VMEM((12 * half + VEC, C), bf16),
            pltpu.VMEM((8, C), f32),
        ],
        [VMEM] * 9,
        "forward_and_heads",
        [
            pltpu.VMEM((PADDED, 3 * C), bf16),
            pltpu.VMEM((CELLS, C), f32),
            pltpu.VMEM((CELLS, C), bf16),
            pltpu.VMEM((CELLS, C), f32),
            pltpu.VMEM((16, C), f32),
            pltpu.VMEM((CELLS, LANES), f32),
            pltpu.VMEM((PADDED, 2 * LANES), bf16),
            pltpu.VMEM((CELLS, LANES), f32),
            pltpu.VMEM((C, CELLS), bf16),
            pltpu.VMEM((TILE, C), f32),
            pltpu.VMEM((8, LANES), f32),
            pltpu.SemaphoreType.DMA((LAYERS,)),
        ],
        FIRST_MIB,
    )


def run_middle(l, order, token, dy, sums, z, a, stats, gains, shifts, w):
    half = C // 2
    outs = [shape((CELLS, C), f32), shape((16, C), f32)] if l else [shape((CELLS, half), f32), shape((CELLS, half), bf16)]
    outs += [shape((9 * half, C), bf16), shape((9 * half + VEC, C), bf16), shape((8, C), f32)]
    scratch = [
        pltpu.VMEM((PADDED, 3 * C), bf16),
        pltpu.VMEM((C, CELLS), bf16),
    ]
    return call(
        functools.partial(middle_kernel, l, order),
        token,
        (dy, sums, z, a, stats, gains, shifts, w),
        [VMEM] * 8,
        outs,
        [VMEM] * len(outs),
        f"layer_gradients_{l}",
        scratch,
        MIDDLE_MIB,
    )


class Sum:
    def __init__(self, layer, taps, order, bits, keep, send, vec):
        self.layer, self.taps, self.order, self.bits = layer, taps, order, bits
        self.keep, self.vec = keep, vec
        self.splits = min(SPLITS, bits)
        self.rows = C // 2
        self.steps = bits + self.splits - 1
        self.got = self.partner(send, 0)

    def partner(self, value, step):
        pairs = []
        for d in range(1 << self.bits):
            for t in range(2):
                pairs.append((2 * d + t, 2 * (d ^ (1 << self.order[t][step])) + t))
        return lax.ppermute(value, ("dp", "tower"), pairs)

    def advance(self, step, token):
        taps, rows = self.taps, self.rows
        vec = shape((8, C), f32)
        if step < self.splits:
            half = rows // 2
            (self.keep, send, self.vec), token = call(
                functools.partial(halve_kernel, taps, rows, self.order, step),
                token, (self.keep, self.got, self.vec), [VMEM] * 3,
                [shape((taps * half, C), bf16), shape((taps * half + VEC, C), bf16), vec], [VMEM] * 3,
                f"halve_{self.layer}_{step}",
            )
            self.rows = half
            bit = step
        elif step <= self.bits:
            (send, self.vec), token = call(
                functools.partial(add_kernel, taps, rows),
                token, (self.keep, self.got, self.vec), [VMEM] * 3,
                [shape((taps * rows + VEC, C), bf16), vec], [VMEM] * 2,
                f"add_{self.layer}_{step}",
            )
            self.keep = send
            bit = step if step < self.bits else self.splits - 1
        else:
            bit = self.steps - step
            (send,), token = call(
                functools.partial(join_kernel, taps, rows, self.order, bit + 1),
                token, (self.keep, self.got), [VMEM] * 2,
                [shape((taps * 2 * rows, C), bf16)], [VMEM],
                f"join_{self.layer}_{step}",
            )
            self.keep = send
            self.rows = 2 * rows
        self.got = self.partner(send, bit)
        return token

    def finish(self, token, out, own, vecs):
        extra = 0 if own else self.taps - 9
        outs, out_specs = [shape((LAYERS * 9 * C, C), f32)], [HBM]
        ins, specs = [self.keep if own else self.got], [VMEM]
        if extra:
            ins, specs = ins + [self.keep, self.vec], specs + [VMEM] * 2
            outs.append(shape((extra * C + VEC, C), bf16))
            out_specs.append(VMEM)
        elif not own and not self.layer:
            ins, specs = ins + vecs, specs + [VMEM] * LAYERS
            outs += [shape((LAYERS, C), f32)] * 2
            out_specs += [VMEM] * 2
        alias = {}
        if out is not None:
            alias = {len(ins): 0}
            ins, specs = ins + [out], specs + [HBM]
        if own:
            kernel = functools.partial(write_own_kernel, self.layer, self.order)
        else:
            kernel = functools.partial(write_got_kernel, self.layer, self.order, extra)
        return call(
            kernel, token, ins, specs, outs, out_specs, f"write_{self.layer}_{'own' if own else 'got'}",
            [pltpu.VMEM((9 * C // 2, C), f32), pltpu.SemaphoreType.DMA((9,))], 16, alias,
        )


TIMELINE = (
    (2, 0), (1, 0), (3, 1), (0, 0), (3, 2), (1, 1), (2, 1), (3, 3), (1, 2), (0, 1), (1, 3), (2, 2),
    (3, 4), (0, 2), (1, 4), (2, 3), (0, 3), (3, 5), (0, 4), (1, 5), (2, 4), (8, 0), (3, 6), (0, 5),
    (1, 6), (2, 5), (0, 6), (3, 7), (2, 6), (0, 7), (1, 7), (3, 8), (2, 7), (9, 0), (1, 8), (0, 8),
    (2, 8),
)
ORDERS = (
    ((1, 2, 0, 3), (0, 1, 2, 3)),
    ((2, 0, 1, 3), (1, 2, 0, 3)),
    ((0, 1, 2, 3), (2, 0, 1, 3)),
    ((0, 1, 2, 3), (2, 0, 1, 3)),
)


def orders(bits):
    if bits == 4:
        return ORDERS
    line = tuple(range(bits))
    return (((line, line[1:] + line[:1]),) * LAYERS)


def timeline(bits, steps):
    if bits == 4:
        return TIMELINE
    late = [(l, step) for step in range(1, steps + 3) for l in (3, 2, 1, 0)]
    return [(2, 0), (1, 0), (0, 0)] + late + [(FEATURES, 0), (HEADS, 0)]


def body(
    features, bn_mean, bn_var, tower_weight, norm_gain, norm_bias, head_weight, head_bias, level_scale,
    cls_cot, reg_cot, positive, *, dp,
):
    bits = dp.bit_length() - 1
    assert dp == 1 << bits and bits >= 1
    order = orders(bits)
    in_hbm = lambda v: pltpu.with_memory_space_constraint(v, pltpu.HBM)
    own = features[0]
    swap = [(0, 1), (1, 0)]
    other = lax.ppermute(own, "tower", swap)
    w = in_hbm(tower_weight[0].reshape(LAYERS, 9 * C, C))
    gains, shifts = in_hbm(norm_gain[0]), in_hbm(norm_bias[0])
    mean, var = in_hbm(bn_mean[None]), in_hbm(bn_var[None])
    head = in_hbm(jnp.swapaxes(head_weight, 2, 3))
    (hw, hg), token = run_prepare(
        mean, head, in_hbm(jnp.swapaxes(cls_cot[0], 0, 1)), in_hbm(jnp.swapaxes(reg_cot[0], 0, 1)), in_hbm(positive)
    )
    (w, z, a, stats, dy, dy_sums, keep, send, vec), token = run_first(
        order[3], token, in_hbm(level_scale[None]), in_hbm(own), other, mean, var, w, gains, shifts, head,
        in_hbm(head_bias[None]), hw, hg,
    )
    sums = [None] * LAYERS
    sums[3] = Sum(3, 12, order[3], bits, keep, send, vec)
    out = None
    for l, step in timeline(bits, sums[3].steps):
        if l == FEATURES:
            (feature_grad,), token = call(
                features_kernel, token, (keep_half, got_half, var), [VMEM] * 3,
                [shape((PIX, C // 2), bf16)], [VMEM], "feature_gradient",
            )
        elif l == HEADS:
            (dhead, dbias, dscale), token = call(
                heads_kernel, token, (heads, got_heads, sums[3].vec), [VMEM] * 3,
                [shape((3, 3, HEAD, C), f32), shape((1, HEAD), f32), shape((1, len(COUNTS)), f32)], [VMEM] * 3,
                "head_gradients",
            )
        elif step == 0:
            (*grads, keep, send, vec), token = run_middle(l, order[l], token, dy, dy_sums, z, a, stats, gains, shifts, w)
            sums[l] = Sum(l, 9, order[l], bits, keep, send, vec)
            if l:
                dy, dy_sums = grads
            else:
                keep_half, send_half = grads
                got_half = lax.ppermute(send_half, "tower", swap)
        elif step <= sums[l].steps:
            token = sums[l].advance(step, token)
        elif step == sums[l].steps + 1:
            (out,), token = sums[l].finish(token, out, True, None)
        else:
            (out, *more), token = sums[l].finish(token, out, False, [one.vec for one in sums])
            if l == 3:
                (heads,) = more
                got_heads = lax.ppermute(heads, "tower", swap)
            elif l == 0:
                dgain, dshift = more
    return (
        feature_grad[None],
        out.reshape(1, LAYERS, 3, 3, C, C),
        dgain[None],
        dshift[None],
        jnp.swapaxes(dhead, 2, 3),
        dbias[0],
        dscale[0],
    )


def solution(mesh):
    return jax.shard_map(
        functools.partial(body, dp=mesh.shape["dp"]),
        mesh=mesh,
        in_specs=(
            P("dp", None, "tower"),
            P(),
            P(),
            P("tower", None, None, None, None, None),
            P("tower", None, None),
            P("tower", None, None),
            P(),
            P(),
            P(),
            P("dp", None, None),
            P("dp", None, None),
            P("dp", None),
        ),
        out_specs=(
            P("dp", None, "tower"),
            P("tower", None, None, None, None, None),
            P("tower", None, None),
            P("tower", None, None),
            P(),
            P(),
            P(),
        ),
        check_vma=False,
    )
```

time: 181 us -> 135 us (0.75)
  waiting for transfers between devices: 60.4 us -> 38.7 us
  Pallas kernels: 72.2 us -> 53.6 us
  local copies, waits for them, and re-layouts: 10.3 us -> 0 us
  starting transfers between devices: 35.5 us -> 41.2 us
    ppermute x28, waiting for transfers between devices: 59.5 us -> 38 us  [partner(): return lax.ppermute(value, ('dp', 'tower'), pairs)]
    pallas_call x34 -> x39, Pallas kernels: 72.2 us -> 53.6 us  [call(): pl.pallas_call(ordered, out_shape=list(outs) + [shape((8, LANES), f32)],...]
    unnamed x24 -> x0, local copies, waits for them, and re-layouts: 9.76 us -> none
    ppermute x28, starting transfers between devices: 34.4 us -> 40.6 us  [partner(): return lax.ppermute(value, ('dp', 'tower'), pairs)]
  transfers between devices with their start and end apart: 31 -> 31, of which waited for: 17 -> 17; matrix products, arithmetic and copies ran while one was open for 1% -> 0% of each run, Pallas kernels for 23% -> 22%
where the time goes in v3:
time: 135 us
  Pallas kernels  53.6 us (40%)
  starting transfers between devices  41.2 us (31%)
  waiting for transfers between devices  38.7 us (29%)
    pallas_call x39, Pallas kernels, call(): pl.pallas_call(ordered, out_shape=list(outs) + [shape((8, LANES), f32)],...  53.6 us
    ppermute x28, starting transfers between devices, partner(): return lax.ppermute(value, ('dp', 'tower'), pairs)  40.6 us
    ppermute x28, waiting for transfers between devices, partner(): return lax.ppermute(value, ('dp', 'tower'), pairs)  38 us
  transfers between devices with their start and end apart: 31, of which 17 were waited for; matrix products, arithmetic and copies ran while one was open for 0% of the time, Pallas kernels for 22%

profile of v3, /device:TPU:0, one launch (start us, length us, event | category | flops | bytes accessed | tf_op | source)
XLA Modules:
  0.0 134.6 jit_solution(2577521279435420234)
XLA Ops:
  0.6 0.5 collective-permute-start
  1.2 1.4 %prepare.1 = (bf16[768,256]{1,0:T(8,128)(2,1)S(1)}, f32[1408,128]{1,0:T(8,128)S(1)}, f32[8,128]{1,0:T(8,128)S(1)}) custom-call(bf16[3,3,85,256]{3,2,1,0:T(8,128)(2,1)} %bitcast.24, bf16[80,1364]{1,0:T(8,128)(2,1)} %bitcast.43, bf16[5,1364]{1,0:T(8,128)(2,1)} %bitcast.44, s32[1,1364]{1,0:T(1,128)} %refs_3_.1, f32[1,256]{1,0:T(1,128)} %bitcast.36), custom_call_target="tpu_custom_call" | custom-call | flops 300000000 | bytes 1 | tf_op jit(solution)/shard_map/prepare/pallas_call | solution.py:333
  2.6 22.2 %forward_and_heads.1 = (bf16[4,2304,256]{2,1,0:T(8,128)(2,1)S(1)}, f32[3,1408,256]{2,1,0:T(8,128)S(1)}, bf16[3,1408,256]{2,1,0:T(8,128)(2,1)S(1)}, f32[3,16,256]...) custom-call(f32[1,5]{1,0:T(1,128)} %bitcast.40, ...), custom_call_target="tpu_custom_call" | custom-call | flops 300000000 | bytes 1 | tf_op jit(solution)/shard_map/forward_and_heads/pallas_call | solution.py:333
  24.9 2.9 %collective-permute-start.1 = (bf16[1568,256]{1,0:T(8,128)(2,1)S(1)}, bf16[1568,256]{1,0:T(8,128)(2,1)S(1)}, u32[]{:S(2)}, u32[]{:S(2)}) collective-permute-start(bf16[1568,256]{1,0:T(8,128)(2,1)S(1)} %get-tuple-element.150), channel_id=1, source_target_pairs={{0,2},{1,9},{2,0},{3,11},{4,6},{5,13},{6,4},{7,15},{8,10},{9,1},{1... | collective-permute-start | bytes 2408456 | tf_op jit(solution)/shard_map/ppermute | solution.py:779
  27.8 5.0 %layer_gradients_2.1 = (f32[1408,256]{1,0:T(8,128)S(1)}, f32[16,256]{1,0:T(8,128)S(1)}, bf16[1152,256]{1,0:T(8,128)(2,1)S(1)}, bf16[1184,256]{1,0:T(8,128)(2,1)S...) custom-call(f32[1408,256]{1,0:T(8,128)S(1)} %get-tuple-element.137.refs_0_, f32[16,256]{1,0:T(8,128)S(1)} %get-tuple-element.138.refs_1_, ...), custom_call_target="tpu_custom_call" | custom-call | flops 1000000 | bytes 1 | tf_op jit(solution)/shard_map/layer_gradients_2/pallas_call | solution.py:333
  32.8 5.3 %layer_gradients_1.1 = (f32[1408,256]{1,0:T(8,128)S(1)}, f32[16,256]{1,0:T(8,128)S(1)}, bf16[1152,256]{1,0:T(8,128)(2,1)S(1)}, bf16[1184,256]{1,0:T(8,128)(2,1)S...) custom-call(f32[1408,256]{1,0:T(8,128)S(1)} %get-tuple-element.144.refs_0_, f32[16,256]{1,0:T(8,128)S(1)} %get-tuple-element.145.refs_1_, ...), custom_call_target="tpu_custom_call" | custom-call | flops 1000000 | bytes 1 | tf_op jit(solution)/shard_map/layer_gradients_1/pallas_call | solution.py:333
  38.1 0.3 halve_3_1.1
  38.4 1.9 %collective-permute-start.5 = (bf16[800,256]{1,0:T(8,128)(2,1)S(1)}, bf16[800,256]{1,0:T(8,128)(2,1)S(1)}, u32[]{:S(2)}, u32[]{:S(2)}) collective-permute-start(bf16[800,256]{1,0:T(8,128)(2,1)S(1)} %get-tuple-element.163), channel_id=1, source_target_pairs={{0,4},{1,3},{2,6},{3,1},{4,0},{5,7},{6,2},{7,5},{8,12},{9,11},{10,... | collective-permute-start | bytes 1228808 | tf_op jit(solution)/shard_map/ppermute | solution.py:779
  40.3 1.6 %collective-permute-start.4 = (bf16[1184,256]{1,0:T(8,128)(2,1)S(1)}, bf16[1184,256]{1,0:T(8,128)(2,1)S(1)}, u32[]{:S(2)}, u32[]{:S(2)}) collective-permute-start(bf16[1184,256]{1,0:T(8,128)(2,1)S(1)} %get-tuple-element.160), channel_id=1, source_target_pairs={{0,8},{1,5},{2,10},{3,7},{4,12},{5,1},{6,14},{7,3},{8,0},{9,13},{1... | collective-permute-start | bytes 1818632 | tf_op jit(solution)/shard_map/ppermute | solution.py:779
  41.9 1.5 %collective-permute-start.3 = (bf16[1184,256]{1,0:T(8,128)(2,1)S(1)}, bf16[1184,256]{1,0:T(8,128)(2,1)S(1)}, u32[]{:S(2)}, u32[]{:S(2)}) collective-permute-start(bf16[1184,256]{1,0:T(8,128)(2,1)S(1)} %get-tuple-element.157), channel_id=1, source_target_pairs={{0,2},{1,9},{2,0},{3,11},{4,6},{5,13},{6,4},{7,15},{8,10},{9,1},{1... | collective-permute-start | bytes 1818632 | tf_op jit(solution)/shard_map/ppermute | solution.py:779
  43.4 4.9 %layer_gradients_0.1 = (f32[1408,128]{1,0:T(8,128)S(1)}, bf16[1408,128]{1,0:T(8,128)(2,1)S(1)}, bf16[1152,256]{1,0:T(8,128)(2,1)S(1)}, bf16[1184,256]{1,0:T(8,12...) custom-call(f32[1408,256]{1,0:T(8,128)S(1)} %get-tuple-element.147.refs_0_, ...), custom_call_target="tpu_custom_call" | custom-call | flops 100000000 | bytes 1 | tf_op jit(solution)/shard_map/layer_gradients_0/pallas_call | solution.py:333
  48.3 0.2 halve_3_2.1
  48.5 2.3 %collective-permute-start.8 = (bf16[416,256]{1,0:T(8,128)(2,1)S(1)}, bf16[416,256]{1,0:T(8,128)(2,1)S(1)}, u32[]{:S(2)}, u32[]{:S(2)}) collective-permute-start(bf16[416,256]{1,0:T(8,128)(2,1)S(1)} %get-tuple-element.175), channel_id=1, source_target_pairs={{0,8},{1,5},{2,10},{3,7},{4,12},{5,1},{6,14},{7,3},{8,0},{9,13},{1... | collective-permute-start | bytes 638984 | tf_op jit(solution)/shard_map/ppermute | solution.py:779
  50.8 1.6 %collective-permute-start.10 = (bf16[1184,256]{1,0:T(8,128)(2,1)S(1)}, bf16[1184,256]{1,0:T(8,128)(2,1)S(1)}, u32[]{:S(2)}, u32[]{:S(2)}) collective-permute-start(bf16[1184,256]{1,0:T(8,128)(2,1)S(1)} %get-tuple-element.183), channel_id=1, source_target_pairs={{0,4},{1,3},{2,6},{3,1},{4,0},{5,7},{6,2},{7,5},{8,12},{9,11},{10,... | collective-permute-start | bytes 1818632 | tf_op jit(solution)/shard_map/ppermute | solution.py:779
  52.3 2.0 %collective-permute-done.4.refs_1_ = bf16[1184,256]{1,0:T(8,128)(2,1)S(1)} collective-permute-done((bf16[1184,256]{1,0:T(8,128)(2,1)S(1)}, bf16[1184,256]{1,0:T(8,128)(2,1)S(1)}, u32[]{:S(2)}, u32[]{:S(2)}) %collective-permute-start.4) | collective-permute-done | bytes 606240 | tf_op jit(solution)/shard_map/ppermute | solution.py:779
  54.3 0.2 halve_1_1.1
  54.5 2.5 %collective-permute-start.7 = (bf16[608,256]{1,0:T(8,128)(2,1)S(1)}, bf16[608,256]{1,0:T(8,128)(2,1)S(1)}, u32[]{:S(2)}, u32[]{:S(2)}) collective-permute-start(bf16[608,256]{1,0:T(8,128)(2,1)S(1)} %get-tuple-element.172), channel_id=1, source_target_pairs={{0,2},{1,9},{2,0},{3,11},{4,6},{5,13},{6,4},{7,15},{8,10},{9,1},{1... | collective-permute-start | bytes 933896 | tf_op jit(solution)/shard_map/ppermute | solution.py:779
  57.1 0.2 halve_2_1.1
  57.3 0.5 collective-permute-start.6
  57.8 1.1 collective-permute-done.8.refs_1_
  59.0 2.7 %collective-permute-start.14 = (bf16[416,256]{1,0:T(8,128)(2,1)S(1)}, bf16[416,256]{1,0:T(8,128)(2,1)S(1)}, u32[]{:S(2)}, u32[]{:S(2)}) collective-permute-start(bf16[416,256]{1,0:T(8,128)(2,1)S(1)} %get-tuple-element.196.refs_0_), channel_id=1, source_target_pairs={{0,16},{1,17},{2,18},{3,19},{4,20},{5,21},{6,22},{7,23},{8,24},{9,... | collective-permute-start | bytes 638984 | tf_op jit(solution)/shard_map/ppermute | solution.py:779
  61.6 3.7 %collective-permute-done.7.refs_1_ = bf16[608,256]{1,0:T(8,128)(2,1)S(1)} collective-permute-done((bf16[608,256]{1,0:T(8,128)(2,1)S(1)}, bf16[608,256]{1,0:T(8,128)(2,1)S(1)}, u32[]{:S(2)}, u32[]{:S(2)}) %collective-permute-start.7) | collective-permute-done | bytes 311328 | tf_op jit(solution)/shard_map/ppermute | solution.py:779
  65.3 0.1 halve_1_2.1
  65.5 0.5 collective-permute-start.9
  66.0 0.2 halve_0_1.1
  66.2 2.4 %collective-permute-start.13 = (bf16[608,256]{1,0:T(8,128)(2,1)S(1)}, bf16[608,256]{1,0:T(8,128)(2,1)S(1)}, u32[]{:S(2)}, u32[]{:S(2)}) collective-permute-start(bf16[608,256]{1,0:T(8,128)(2,1)S(1)} %get-tuple-element.194), channel_id=1, source_target_pairs={{0,8},{1,5},{2,10},{3,7},{4,12},{5,1},{6,14},{7,3},{8,0},{9,13},{1... | collective-permute-start | bytes 933896 | tf_op jit(solution)/shard_map/ppermute | solution.py:779
  68.6 3.7 %collective-permute-done.9.refs_1_ = bf16[320,256]{1,0:T(8,128)(2,1)S(1)} collective-permute-done((bf16[320,256]{1,0:T(8,128)(2,1)S(1)}, bf16[320,256]{1,0:T(8,128)(2,1)S(1)}, u32[]{:S(2)}, u32[]{:S(2)}) %collective-permute-start.9) | collective-permute-done | bytes 163872 | tf_op jit(solution)/shard_map/ppermute | solution.py:779
  72.4 2.6 %collective-permute-start.12 = (bf16[320,256]{1,0:T(8,128)(2,1)S(1)}, bf16[320,256]{1,0:T(8,128)(2,1)S(1)}, u32[]{:S(2)}, u32[]{:S(2)}) collective-permute-start(bf16[320,256]{1,0:T(8,128)(2,1)S(1)} %get-tuple-element.191.refs_0_), channel_id=1, source_target_pairs={{0,16},{1,17},{2,18},{3,19},{4,20},{5,21},{6,22},{7,23},{8,24},{9,... | collective-permute-start | bytes 491528 | tf_op jit(solution)/shard_map/ppermute | solution.py:779
  75.0 0.1 halve_2_2.1
  75.2 2.4 %collective-permute-start.11 = (bf16[320,256]{1,0:T(8,128)(2,1)S(1)}, bf16[320,256]{1,0:T(8,128)(2,1)S(1)}, u32[]{:S(2)}, u32[]{:S(2)}) collective-permute-start(bf16[320,256]{1,0:T(8,128)(2,1)S(1)} %get-tuple-element.189), channel_id=1, source_target_pairs={{0,8},{1,5},{2,10},{3,7},{4,12},{5,1},{6,14},{7,3},{8,0},{9,13},{1... | collective-permute-start | bytes 491528 | tf_op jit(solution)/shard_map/ppermute | solution.py:779
  77.8 0.1 halve_0_2.1
  77.9 2.1 %collective-permute-start.17 = (bf16[320,256]{1,0:T(8,128)(2,1)S(1)}, bf16[320,256]{1,0:T(8,128)(2,1)S(1)}, u32[]{:S(2)}, u32[]{:S(2)}) collective-permute-start(bf16[320,256]{1,0:T(8,128)(2,1)S(1)} %get-tuple-element.206), channel_id=1, source_target_pairs={{0,2},{1,9},{2,0},{3,11},{4,6},{5,13},{6,4},{7,15},{8,10},{9,1},{1... | collective-permute-start | bytes 491528 | tf_op jit(solution)/shard_map/ppermute | solution.py:779
  80.0 2.2 %collective-permute-done.12.refs_1_ = bf16[320,256]{1,0:T(8,128)(2,1)S(1)} collective-permute-done((bf16[320,256]{1,0:T(8,128)(2,1)S(1)}, bf16[320,256]{1,0:T(8,128)(2,1)S(1)}, u32[]{:S(2)}, u32[]{:S(2)}) %collective-permute-start.12) | collective-permute-done | bytes 163872 | tf_op jit(solution)/shard_map/ppermute | solution.py:779
  82.3 1.6 %collective-permute-done.11.refs_1_ = bf16[320,256]{1,0:T(8,128)(2,1)S(1)} collective-permute-done((bf16[320,256]{1,0:T(8,128)(2,1)S(1)}, bf16[320,256]{1,0:T(8,128)(2,1)S(1)}, u32[]{:S(2)}, u32[]{:S(2)}) %collective-permute-start.11) | collective-permute-done | bytes 163872 | tf_op jit(solution)/shard_map/ppermute | solution.py:779
  84.0 1.4 %collective-permute-start.18 = (bf16[320,256]{1,0:T(8,128)(2,1)S(1)}, bf16[320,256]{1,0:T(8,128)(2,1)S(1)}, u32[]{:S(2)}, u32[]{:S(2)}) collective-permute-start(bf16[320,256]{1,0:T(8,128)(2,1)S(1)} %get-tuple-element.209.refs_0_), channel_id=1, source_target_pairs={{0,16},{1,17},{2,18},{3,19},{4,20},{5,21},{6,22},{7,23},{8,24},{9,... | collective-permute-start | bytes 491528 | tf_op jit(solution)/shard_map/ppermute | solution.py:779
  85.4 2.7 %collective-permute-start.15 = (bf16[320,256]{1,0:T(8,128)(2,1)S(1)}, bf16[320,256]{1,0:T(8,128)(2,1)S(1)}, u32[]{:S(2)}, u32[]{:S(2)}) collective-permute-start(bf16[320,256]{1,0:T(8,128)(2,1)S(1)} %get-tuple-element.202.refs_0_), channel_id=1, source_target_pairs={{0,16},{1,17},{2,18},{3,19},{4,20},{5,21},{6,22},{7,23},{8,24},{9,... | collective-permute-start | bytes 491528 | tf_op jit(solution)/shard_map/ppermute | solution.py:779
  88.2 1.0 collective-permute-start.23
  89.2 9.9 %collective-permute-done.18.refs_1_ = bf16[320,256]{1,0:T(8,128)(2,1)S(1)} collective-permute-done((bf16[320,256]{1,0:T(8,128)(2,1)S(1)}, bf16[320,256]{1,0:T(8,128)(2,1)S(1)}, u32[]{:S(2)}, u32[]{:S(2)}) %collective-permute-start.18) | collective-permute-done | bytes 163872 | tf_op jit(solution)/shard_map/ppermute | solution.py:779
  99.2 1.6 %collective-permute-start.22 = (bf16[320,256]{1,0:T(8,128)(2,1)S(1)}, bf16[320,256]{1,0:T(8,128)(2,1)S(1)}, u32[]{:S(2)}, u32[]{:S(2)}) collective-permute-start(bf16[320,256]{1,0:T(8,128)(2,1)S(1)} %get-tuple-element.220.refs_0_), channel_id=1, source_target_pairs={{0,2},{1,9},{2,0},{3,11},{4,6},{5,13},{6,4},{7,15},{8,10},{9,1},{1... | collective-permute-start | bytes 491528 | tf_op jit(solution)/shard_map/ppermute | solution.py:779
  100.9 0.6 collective-permute-start.21
  101.6 0.5 collective-permute-start.20
  102.1 1.6 %feature_gradient.1 = (bf16[1364,128]{1,0:T(8,128)(2,1)}, f32[8,128]{1,0:T(8,128)S(1)}) custom-call(f32[1408,128]{1,0:T(8,128)S(1)} %get-tuple-element.154.refs_0_, bf16[1408,128]{1,0:T(8,128)(2,1)S(1)} %collective-permute-done.2.refs_1_, f32[1,256]{1,0:T(1,128)} %bitcast.39, f32[8,128]{1,0:T(8,128)S(1)} %get-tuple-element.216.refs_3_), custom_call_target="tpu_custom_call" | custom-call | flops 3000000000 | bytes 1 | tf_op jit(solution)/shard_map/feature_gradient/pallas_call | solution.py:333
  103.8 0.8 collective-permute-done.22.refs_1_
  104.7 0.9 collective-permute-start.25
  105.5 1.5 %collective-permute-start.29 = (bf16[1536,256]{1,0:T(8,128)(2,1)S(1)}, bf16[1536,256]{1,0:T(8,128)(2,1)S(1)}, u32[]{:S(2)}, u32[]{:S(2)}) collective-permute-start(bf16[1536,256]{1,0:T(8,128)(2,1)S(1)} %get-tuple-element.227.refs_0_.refs_1_), channel_id=1, source_target_pairs={{0,2},{1,9},{2,0},{3,11},{4,6},{5,13},{6,4},{7,15},{8,10},{9,1},{1... | collective-permute-start | bytes 2359304 | tf_op jit(solution)/shard_map/ppermute | solution.py:779
  107.0 0.8 collective-permute-done.21.refs_1_
  107.8 1.0 collective-permute-done.20.refs_1_
  108.9 0.7 collective-permute-start.24
  109.5 5.6 %collective-permute-done.25.refs_1_ = bf16[576,256]{1,0:T(8,128)(2,1)S(1)} collective-permute-done((bf16[576,256]{1,0:T(8,128)(2,1)S(1)}, bf16[576,256]{1,0:T(8,128)(2,1)S(1)}, u32[]{:S(2)}, u32[]{:S(2)}) %collective-permute-start.25) | collective-permute-done | bytes 294944 | tf_op jit(solution)/shard_map/ppermute | solution.py:779
  115.2 0.7 collective-permute-start.27
  115.9 1.1 write_3_own.1
  116.9 1.9 %collective-permute-done.24.refs_1_ = bf16[576,256]{1,0:T(8,128)(2,1)S(1)} collective-permute-done((bf16[576,256]{1,0:T(8,128)(2,1)S(1)}, bf16[576,256]{1,0:T(8,128)(2,1)S(1)}, u32[]{:S(2)}, u32[]{:S(2)}) %collective-permute-start.24) | collective-permute-done | bytes 294944 | tf_op jit(solution)/shard_map/ppermute | solution.py:779
  118.9 1.6 %collective-permute-start.26 = (bf16[1152,256]{1,0:T(8,128)(2,1)S(1)}, bf16[1152,256]{1,0:T(8,128)(2,1)S(1)}, u32[]{:S(2)}, u32[]{:S(2)}) collective-permute-start(bf16[1152,256]{1,0:T(8,128)(2,1)S(1)} %get-tuple-element.232.refs_0_), channel_id=1, source_target_pairs={{0,2},{1,9},{2,0},{3,11},{4,6},{5,13},{6,4},{7,15},{8,10},{9,1},{1... | collective-permute-start | bytes 1769480 | tf_op jit(solution)/shard_map/ppermute | solution.py:779
  120.5 1.1 write_0_own.1
  121.6 1.1 write_1_own.1
  122.7 2.1 %collective-permute-done.29.refs_0_ = bf16[1536,256]{1,0:T(8,128)(2,1)S(1)} collective-permute-done((bf16[1536,256]{1,0:T(8,128)(2,1)S(1)}, bf16[1536,256]{1,0:T(8,128)(2,1)S(1)}, u32[]{:S(2)}, u32[]{:S(2)}) %collective-permute-start.29) | collective-permute-done | bytes 786464 | tf_op jit(solution)/shard_map/ppermute | solution.py:779
  124.7 1.1 write_3_got.1
  125.9 1.1 write_2_own.1
  127.0 0.6 collective-permute-done.30.refs_1_
  127.6 1.2 head_gradients.1
  128.8 1.1 write_1_got.1
  130.0 1.7 %write_0_got.1 = (f32[9216,256]{1,0:T(8,128)}, f32[4,256]{1,0:T(4,128)}, f32[4,256]{1,0:T(4,128)}, f32[8,128]{1,0:T(8,128)S(1)}) custom-call(bf16[1152,256]{1,0:T(8,128)(2,1)S(1)} %collective-permute-done.27.refs_0_, f32[8,256]{1,0:T(8,128)S(1)} %get-tuple-element.234.refs_1_, ...), custom_call_target="tpu_custom_call", output_to_operand_aliasing={{0}: (5, {})} | custom-call | flops 300000000 | bytes 1 | tf_op jit(solution)/shard_map/write_0_got/pallas_call | solution.py:333
  131.7 1.7 %collective-permute-done.26.refs_0_ = bf16[1152,256]{1,0:T(8,128)(2,1)S(1)} collective-permute-done((bf16[1152,256]{1,0:T(8,128)(2,1)S(1)}, bf16[1152,256]{1,0:T(8,128)(2,1)S(1)}, u32[]{:S(2)}, u32[]{:S(2)}) %collective-permute-start.26) | collective-permute-done | bytes 589856 | tf_op jit(solution)/shard_map/ppermute | solution.py:779
  133.3 1.1 write_2_got.1
  (37 shorter events, 1.5 us)
Async XLA Ops:
  0.6 2.0 %collective-permute-start = (bf16[1364,128]{1,0:T(8,128)(2,1)}, bf16[1364,128]{1,0:T(8,128)(2,1)S(1)}, u32[]{:S(2)}, u32[]{:S(2)}) collective-permute-start(bf16[1364,128]{1,0:T(8,128)(2,1)} %bitcast.26), channel_id=1, source_target_pairs={{0,1},{1,0},{2,3},{3,2},{4,5},{5,4},{6,7},{7,6},{8,9},{9,8},{10,11... | collective-permute-start | bytes 1047560 | tf_op jit(solution)/shard_map/ppermute | solution.py:880
  24.9 13.3 %collective-permute-start.1 = (bf16[1568,256]{1,0:T(8,128)(2,1)S(1)}, bf16[1568,256]{1,0:T(8,128)(2,1)S(1)}, u32[]{:S(2)}, u32[]{:S(2)}) collective-permute-start(bf16[1568,256]{1,0:T(8,128)(2,1)S(1)} %get-tuple-element.150), channel_id=1, source_target_pairs={{0,2},{1,9},{2,0},{3,11},{4,6},{5,13},{6,4},{7,15},{8,10},{9,1},{1... | collective-permute-start | bytes 2408456 | tf_op jit(solution)/shard_map/ppermute | solution.py:779
  38.4 9.9 %collective-permute-start.5 = (bf16[800,256]{1,0:T(8,128)(2,1)S(1)}, bf16[800,256]{1,0:T(8,128)(2,1)S(1)}, u32[]{:S(2)}, u32[]{:S(2)}) collective-permute-start(bf16[800,256]{1,0:T(8,128)(2,1)S(1)} %get-tuple-element.163), channel_id=1, source_target_pairs={{0,4},{1,3},{2,6},{3,1},{4,0},{5,7},{6,2},{7,5},{8,12},{9,11},{10,... | collective-permute-start | bytes 1228808 | tf_op jit(solution)/shard_map/ppermute | solution.py:779
  40.3 14.0 %collective-permute-start.4 = (bf16[1184,256]{1,0:T(8,128)(2,1)S(1)}, bf16[1184,256]{1,0:T(8,128)(2,1)S(1)}, u32[]{:S(2)}, u32[]{:S(2)}) collective-permute-start(bf16[1184,256]{1,0:T(8,128)(2,1)S(1)} %get-tuple-element.160), channel_id=1, source_target_pairs={{0,8},{1,5},{2,10},{3,7},{4,12},{5,1},{6,14},{7,3},{8,0},{9,13},{1... | collective-permute-start | bytes 1818632 | tf_op jit(solution)/shard_map/ppermute | solution.py:779
  41.9 15.2 %collective-permute-start.3 = (bf16[1184,256]{1,0:T(8,128)(2,1)S(1)}, bf16[1184,256]{1,0:T(8,128)(2,1)S(1)}, u32[]{:S(2)}, u32[]{:S(2)}) collective-permute-start(bf16[1184,256]{1,0:T(8,128)(2,1)S(1)} %get-tuple-element.157), channel_id=1, source_target_pairs={{0,2},{1,9},{2,0},{3,11},{4,6},{5,13},{6,4},{7,15},{8,10},{9,1},{1... | collective-permute-start | bytes 1818632 | tf_op jit(solution)/shard_map/ppermute | solution.py:779
  48.5 10.4 %collective-permute-start.8 = (bf16[416,256]{1,0:T(8,128)(2,1)S(1)}, bf16[416,256]{1,0:T(8,128)(2,1)S(1)}, u32[]{:S(2)}, u32[]{:S(2)}) collective-permute-start(bf16[416,256]{1,0:T(8,128)(2,1)S(1)} %get-tuple-element.175), channel_id=1, source_target_pairs={{0,8},{1,5},{2,10},{3,7},{4,12},{5,1},{6,14},{7,3},{8,0},{9,13},{1... | collective-permute-start | bytes 638984 | tf_op jit(solution)/shard_map/ppermute | solution.py:779
  50.8 15.2 %collective-permute-start.10 = (bf16[1184,256]{1,0:T(8,128)(2,1)S(1)}, bf16[1184,256]{1,0:T(8,128)(2,1)S(1)}, u32[]{:S(2)}, u32[]{:S(2)}) collective-permute-start(bf16[1184,256]{1,0:T(8,128)(2,1)S(1)} %get-tuple-element.183), channel_id=1, source_target_pairs={{0,4},{1,3},{2,6},{3,1},{4,0},{5,7},{6,2},{7,5},{8,12},{9,11},{10,... | collective-permute-start | bytes 1818632 | tf_op jit(solution)/shard_map/ppermute | solution.py:779
  54.5 10.8 %collective-permute-start.7 = (bf16[608,256]{1,0:T(8,128)(2,1)S(1)}, bf16[608,256]{1,0:T(8,128)(2,1)S(1)}, u32[]{:S(2)}, u32[]{:S(2)}) collective-permute-start(bf16[608,256]{1,0:T(8,128)(2,1)S(1)} %get-tuple-element.172), channel_id=1, source_target_pairs={{0,2},{1,9},{2,0},{3,11},{4,6},{5,13},{6,4},{7,15},{8,10},{9,1},{1... | collective-permute-start | bytes 933896 | tf_op jit(solution)/shard_map/ppermute | solution.py:779
  57.3 17.8 %collective-permute-start.6 = (bf16[608,256]{1,0:T(8,128)(2,1)S(1)}, bf16[608,256]{1,0:T(8,128)(2,1)S(1)}, u32[]{:S(2)}, u32[]{:S(2)}) collective-permute-start(bf16[608,256]{1,0:T(8,128)(2,1)S(1)} %get-tuple-element.169), channel_id=1, source_target_pairs={{0,4},{1,3},{2,6},{3,1},{4,0},{5,7},{6,2},{7,5},{8,12},{9,11},{10,... | collective-permute-start | bytes 933896 | tf_op jit(solution)/shard_map/ppermute | solution.py:779
  59.0 18.6 %collective-permute-start.14 = (bf16[416,256]{1,0:T(8,128)(2,1)S(1)}, bf16[416,256]{1,0:T(8,128)(2,1)S(1)}, u32[]{:S(2)}, u32[]{:S(2)}) collective-permute-start(bf16[416,256]{1,0:T(8,128)(2,1)S(1)} %get-tuple-element.196.refs_0_), channel_id=1, source_target_pairs={{0,16},{1,17},{2,18},{3,19},{4,20},{5,21},{6,22},{7,23},{8,24},{9,... | collective-permute-start | bytes 638984 | tf_op jit(solution)/shard_map/ppermute | solution.py:779
  65.5 6.9 %collective-permute-start.9 = (bf16[320,256]{1,0:T(8,128)(2,1)S(1)}, bf16[320,256]{1,0:T(8,128)(2,1)S(1)}, u32[]{:S(2)}, u32[]{:S(2)}) collective-permute-start(bf16[320,256]{1,0:T(8,128)(2,1)S(1)} %get-tuple-element.180), channel_id=1, source_target_pairs={{0,4},{1,3},{2,6},{3,1},{4,0},{5,7},{6,2},{7,5},{8,12},{9,11},{10,... | collective-permute-start | bytes 491528 | tf_op jit(solution)/shard_map/ppermute | solution.py:779
  66.0 36.1 %collective-permute-start.2 = (bf16[1408,128]{1,0:T(8,128)(2,1)S(1)}, bf16[1408,128]{1,0:T(8,128)(2,1)S(1)}, u32[]{:S(2)}, u32[]{:S(2)}) collective-permute-start(bf16[1408,128]{1,0:T(8,128)(2,1)S(1)} %get-tuple-element.155), channel_id=1, source_target_pairs={{0,1},{1,0},{2,3},{3,2},{4,5},{5,4},{6,7},{7,6},{8,9},{9,8},{10,11... | collective-permute-start | bytes 1081352 | tf_op jit(solution)/shard_map/ppermute | solution.py:914
  66.2 11.6 %collective-permute-start.13 = (bf16[608,256]{1,0:T(8,128)(2,1)S(1)}, bf16[608,256]{1,0:T(8,128)(2,1)S(1)}, u32[]{:S(2)}, u32[]{:S(2)}) collective-permute-start(bf16[608,256]{1,0:T(8,128)(2,1)S(1)} %get-tuple-element.194), channel_id=1, source_target_pairs={{0,8},{1,5},{2,10},{3,7},{4,12},{5,1},{6,14},{7,3},{8,0},{9,13},{1... | collective-permute-start | bytes 933896 | tf_op jit(solution)/shard_map/ppermute | solution.py:779
  72.4 9.8 %collective-permute-start.12 = (bf16[320,256]{1,0:T(8,128)(2,1)S(1)}, bf16[320,256]{1,0:T(8,128)(2,1)S(1)}, u32[]{:S(2)}, u32[]{:S(2)}) collective-permute-start(bf16[320,256]{1,0:T(8,128)(2,1)S(1)} %get-tuple-element.191.refs_0_), channel_id=1, source_target_pairs={{0,16},{1,17},{2,18},{3,19},{4,20},{5,21},{6,22},{7,23},{8,24},{9,... | collective-permute-start | bytes 491528 | tf_op jit(solution)/shard_map/ppermute | solution.py:779
  75.2 8.7 %collective-permute-start.11 = (bf16[320,256]{1,0:T(8,128)(2,1)S(1)}, bf16[320,256]{1,0:T(8,128)(2,1)S(1)}, u32[]{:S(2)}, u32[]{:S(2)}) collective-permute-start(bf16[320,256]{1,0:T(8,128)(2,1)S(1)} %get-tuple-element.189), channel_id=1, source_target_pairs={{0,8},{1,5},{2,10},{3,7},{4,12},{5,1},{6,14},{7,3},{8,0},{9,13},{1... | collective-permute-start | bytes 491528 | tf_op jit(solution)/shard_map/ppermute | solution.py:779
  77.7 10.5 %collective-permute-start.19 = (bf16[416,256]{1,0:T(8,128)(2,1)S(1)}, bf16[416,256]{1,0:T(8,128)(2,1)S(1)}, u32[]{:S(2)}, u32[]{:S(2)}) collective-permute-start(bf16[416,256]{1,0:T(8,128)(2,1)S(1)} %get-tuple-element.211.refs_0_), channel_id=1, source_target_pairs={{0,8},{1,5},{2,10},{3,7},{4,12},{5,1},{6,14},{7,3},{8,0},{9,13},{1... | collective-permute-start | bytes 638984 | tf_op jit(solution)/shard_map/ppermute | solution.py:779
  77.9 6.0 %collective-permute-start.17 = (bf16[320,256]{1,0:T(8,128)(2,1)S(1)}, bf16[320,256]{1,0:T(8,128)(2,1)S(1)}, u32[]{:S(2)}, u32[]{:S(2)}) collective-permute-start(bf16[320,256]{1,0:T(8,128)(2,1)S(1)} %get-tuple-element.206), channel_id=1, source_target_pairs={{0,2},{1,9},{2,0},{3,11},{4,6},{5,13},{6,4},{7,15},{8,10},{9,1},{1... | collective-permute-start | bytes 491528 | tf_op jit(solution)/shard_map/ppermute | solution.py:779
  84.0 15.1 %collective-permute-start.18 = (bf16[320,256]{1,0:T(8,128)(2,1)S(1)}, bf16[320,256]{1,0:T(8,128)(2,1)S(1)}, u32[]{:S(2)}, u32[]{:S(2)}) collective-permute-start(bf16[320,256]{1,0:T(8,128)(2,1)S(1)} %get-tuple-element.209.refs_0_), channel_id=1, source_target_pairs={{0,16},{1,17},{2,18},{3,19},{4,20},{5,21},{6,22},{7,23},{8,24},{9,... | collective-permute-start | bytes 491528 | tf_op jit(solution)/shard_map/ppermute | solution.py:779
  85.4 15.4 %collective-permute-start.16 = (bf16[320,256]{1,0:T(8,128)(2,1)S(1)}, bf16[320,256]{1,0:T(8,128)(2,1)S(1)}, u32[]{:S(2)}, u32[]{:S(2)}) collective-permute-start(bf16[320,256]{1,0:T(8,128)(2,1)S(1)} %get-tuple-element.204.refs_0_), channel_id=1, source_target_pairs={{0,4},{1,3},{2,6},{3,1},{4,0},{5,7},{6,2},{7,5},{8,12},{9,11},{10,... | collective-permute-start | bytes 491528 | tf_op jit(solution)/shard_map/ppermute | solution.py:779
  85.4 16.1 %collective-permute-start.15 = (bf16[320,256]{1,0:T(8,128)(2,1)S(1)}, bf16[320,256]{1,0:T(8,128)(2,1)S(1)}, u32[]{:S(2)}, u32[]{:S(2)}) collective-permute-start(bf16[320,256]{1,0:T(8,128)(2,1)S(1)} %get-tuple-element.202.refs_0_), channel_id=1, source_target_pairs={{0,16},{1,17},{2,18},{3,19},{4,20},{5,21},{6,22},{7,23},{8,24},{9,... | collective-permute-start | bytes 491528 | tf_op jit(solution)/shard_map/ppermute | solution.py:779
  88.2 15.5 %collective-permute-start.23 = (bf16[768,256]{1,0:T(8,128)(2,1)S(1)}, bf16[768,256]{1,0:T(8,128)(2,1)S(1)}, u32[]{:S(2)}, u32[]{:S(2)}) collective-permute-start(bf16[768,256]{1,0:T(8,128)(2,1)S(1)} %get-tuple-element.221.refs_0_), channel_id=1, source_target_pairs={{0,4},{1,3},{2,6},{3,1},{4,0},{5,7},{6,2},{7,5},{8,12},{9,11},{10,... | collective-permute-start | bytes 1179656 | tf_op jit(solution)/shard_map/ppermute | solution.py:779
  99.2 5.4 %collective-permute-start.22 = (bf16[320,256]{1,0:T(8,128)(2,1)S(1)}, bf16[320,256]{1,0:T(8,128)(2,1)S(1)}, u32[]{:S(2)}, u32[]{:S(2)}) collective-permute-start(bf16[320,256]{1,0:T(8,128)(2,1)S(1)} %get-tuple-element.220.refs_0_), channel_id=1, source_target_pairs={{0,2},{1,9},{2,0},{3,11},{4,6},{5,13},{6,4},{7,15},{8,10},{9,1},{1... | collective-permute-start | bytes 491528 | tf_op jit(solution)/shard_map/ppermute | solution.py:779
  100.9 6.9 %collective-permute-start.21 = (bf16[576,256]{1,0:T(8,128)(2,1)S(1)}, bf16[576,256]{1,0:T(8,128)(2,1)S(1)}, u32[]{:S(2)}, u32[]{:S(2)}) collective-permute-start(bf16[576,256]{1,0:T(8,128)(2,1)S(1)} %get-tuple-element.219.refs_0_), channel_id=1, source_target_pairs={{0,2},{1,9},{2,0},{3,11},{4,6},{5,13},{6,4},{7,15},{8,10},{9,1},{1... | collective-permute-start | bytes 884744 | tf_op jit(solution)/shard_map/ppermute | solution.py:779
  101.6 7.2 %collective-permute-start.20 = (bf16[320,256]{1,0:T(8,128)(2,1)S(1)}, bf16[320,256]{1,0:T(8,128)(2,1)S(1)}, u32[]{:S(2)}, u32[]{:S(2)}) collective-permute-start(bf16[320,256]{1,0:T(8,128)(2,1)S(1)} %get-tuple-element.218.refs_0_), channel_id=1, source_target_pairs={{0,8},{1,5},{2,10},{3,7},{4,12},{5,1},{6,14},{7,3},{8,0},{9,13},{1... | collective-permute-start | bytes 491528 | tf_op jit(solution)/shard_map/ppermute | solution.py:779
  104.7 10.5 %collective-permute-start.25 = (bf16[576,256]{1,0:T(8,128)(2,1)S(1)}, bf16[576,256]{1,0:T(8,128)(2,1)S(1)}, u32[]{:S(2)}, u32[]{:S(2)}) collective-permute-start(bf16[576,256]{1,0:T(8,128)(2,1)S(1)} %get-tuple-element.228.refs_0_), channel_id=1, source_target_pairs={{0,8},{1,5},{2,10},{3,7},{4,12},{5,1},{6,14},{7,3},{8,0},{9,13},{1... | collective-permute-start | bytes 884744 | tf_op jit(solution)/shard_map/ppermute | solution.py:779
  105.5 19.2 %collective-permute-start.29 = (bf16[1536,256]{1,0:T(8,128)(2,1)S(1)}, bf16[1536,256]{1,0:T(8,128)(2,1)S(1)}, u32[]{:S(2)}, u32[]{:S(2)}) collective-permute-start(bf16[1536,256]{1,0:T(8,128)(2,1)S(1)} %get-tuple-element.227.refs_0_.refs_1_), channel_id=1, source_target_pairs={{0,2},{1,9},{2,0},{3,11},{4,6},{5,13},{6,4},{7,15},{8,10},{9,1},{1... | collective-permute-start | bytes 2359304 | tf_op jit(solution)/shard_map/ppermute | solution.py:779
  108.9 10.0 %collective-permute-start.24 = (bf16[576,256]{1,0:T(8,128)(2,1)S(1)}, bf16[576,256]{1,0:T(8,128)(2,1)S(1)}, u32[]{:S(2)}, u32[]{:S(2)}) collective-permute-start(bf16[576,256]{1,0:T(8,128)(2,1)S(1)} %get-tuple-element.226.refs_0_), channel_id=1, source_target_pairs={{0,4},{1,3},{2,6},{3,1},{4,0},{5,7},{6,2},{7,5},{8,12},{9,11},{10,... | collective-permute-start | bytes 884744 | tf_op jit(solution)/shard_map/ppermute | solution.py:779
  109.5 19.3 %collective-permute-start.28 = (bf16[1152,256]{1,0:T(8,128)(2,1)S(1)}, bf16[1152,256]{1,0:T(8,128)(2,1)S(1)}, u32[]{:S(2)}, u32[]{:S(2)}) collective-permute-start(bf16[1152,256]{1,0:T(8,128)(2,1)S(1)} %get-tuple-element.238.refs_0_), channel_id=1, source_target_pairs={{0,8},{1,5},{2,10},{3,7},{4,12},{5,1},{6,14},{7,3},{8,0},{9,13},{1... | collective-permute-start | bytes 1769480 | tf_op jit(solution)/shard_map/ppermute | solution.py:779
  115.2 14.8 %collective-permute-start.27 = (bf16[1152,256]{1,0:T(8,128)(2,1)S(1)}, bf16[1152,256]{1,0:T(8,128)(2,1)S(1)}, u32[]{:S(2)}, u32[]{:S(2)}) collective-permute-start(bf16[1152,256]{1,0:T(8,128)(2,1)S(1)} %get-tuple-element.233.refs_0_), channel_id=1, source_target_pairs={{0,4},{1,3},{2,6},{3,1},{4,0},{5,7},{6,2},{7,5},{8,12},{9,11},{10,... | collective-permute-start | bytes 1769480 | tf_op jit(solution)/shard_map/ppermute | solution.py:779
  118.9 14.4 %collective-permute-start.26 = (bf16[1152,256]{1,0:T(8,128)(2,1)S(1)}, bf16[1152,256]{1,0:T(8,128)(2,1)S(1)}, u32[]{:S(2)}, u32[]{:S(2)}) collective-permute-start(bf16[1152,256]{1,0:T(8,128)(2,1)S(1)} %get-tuple-element.232.refs_0_), channel_id=1, source_target_pairs={{0,2},{1,9},{2,0},{3,11},{4,6},{5,13},{6,4},{7,15},{8,10},{9,1},{1... | collective-permute-start | bytes 1769480 | tf_op jit(solution)/shard_map/ppermute | solution.py:779
  125.8 1.8 %collective-permute-start.30 = (bf16[800,256]{1,0:T(8,128)(2,1)S(1)}, bf16[800,256]{1,0:T(8,128)(2,1)S(1)}, u32[]{:S(2)}, u32[]{:S(2)}) collective-permute-start(bf16[800,256]{1,0:T(8,128)(2,1)S(1)} %get-tuple-element.248.refs_0_), channel_id=1, source_target_pairs={{0,1},{1,0},{2,3},{3,2},{4,5},{5,4},{6,7},{7,6},{8,9},{9,8},{10,11... | collective-permute-start | bytes 1228808 | tf_op jit(solution)/shard_map/ppermute | solution.py:923

commit v4 on v3

--- a/solution.py
+++ b/solution.py
@@ -31,35 +31,39 @@
 
 VEC = 32
 FEATURES, HEADS = 8, 9
-COST = 300000000
+COST = 1500000000
 COSTS = {
-    "add_3_3": 3000000000,
-    "join_0_5": 2000000000,
-    "add_3_4": 3000000000,
-    "halve_3_2": 1000000000,
-    "join_1_6": 300000000,
-    "add_2_4": 300000000,
-    "feature_gradient": 3000000000,
-    "join_2_5": 1000000000,
-    "write_1_got": 1000000,
-    "add_1_4": 2000000000,
-    "join_2_6": 1000000,
-    "write_3_got": 300000000,
-    "layer_gradients_1": 1000000,
-    "write_0_own": 3000000000,
-    "write_2_own": 1500000000,
-    "halve_2_1": 1000000,
-    "halve_1_2": 100000000,
-    "add_1_3": 100000000,
-    "head_gradients": 1000000,
-    "halve_0_2": 1000000,
-    "add_0_3": 100000000,
-    "write_1_own": 2000000000,
-    "layer_gradients_2": 1000000,
-    "join_3_6": 2000000000,
-    "join_3_5": 1000000000,
-    "halve_3_1": 5000000000,
-    "layer_gradients_0": 100000000,
+    "write_3_own": 100000000,
+    "layer_gradients_2": 3000000000,
+    "join_1_6": 1000000000,
+    "halve_1_1": 2000000000,
+    "add_1_3": 300000000,
+    "write_2_own": 3000000000,
+    "join_2_6": 3000000000,
+    "halve_0_1": 300000000,
+    "feature_gradient": 100000000,
+    "halve_3_1": 1500000000,
+    "halve_2_1": 2000000000,
+    "write_1_own": 100000000,
+    "add_0_4": 1000000000,
+    "head_gradients": 1500000000,
+    "layer_gradients_1": 5000000000,
+    "add_0_3": 5000000000,
+    "layer_gradients_0": 2000000000,
+    "write_0_got": 3000000000,
+    "write_3_got": 1000000,
+    "join_3_6": 1000000000,
+    "halve_0_2": 1500000000,
+    "write_1_got": 2000000000,
+    "join_0_5": 1000000,
+    "join_1_5": 1000000000,
+    "halve_2_2": 2000000000,
+    "join_0_6": 3000000000,
+    "add_3_4": 300000000,
+    "join_3_5": 3000000000,
+    "add_1_4": 100000000,
+    "halve_3_2": 2000000000,
+    "halve_1_2": 1500000000,
 }
 FIRST_MIB = 32
 MIDDLE_MIB = 24
@@ -110,28 +114,19 @@
     return out
 
 
-def each_tile(step, init):
-    results = []
-    for level, (tiles, cell, row, width) in enumerate(((16, 0, 64, 64), (4, 1024, 1152, 32), (1, 1280, 1440, 16))):
-        carry = init
-
-        def run(i, carry, level=level, cell=cell, row=row, width=width):
-            at = pl.multiple_of(i * TILE, TILE)
-            return step(level, cell + at, row + at, width, carry)
-
-        if tiles == 1:
-            carry = step(level, cell, row, width, carry)
-        else:
-            carry = lax.fori_loop(0, tiles, run, carry, unroll=2)
-        results.append(carry)
-    results.append(step(3, 1344, 1504, 16, init))
-    return results
+def moved(tile, width):
+    row = lax.broadcasted_iota(jnp.int32, (8, tile.shape[1]), 0)
+    before, after = pltpu.roll(tile, 1, 0), pltpu.roll(tile, TILE - 1, 0)
+    first, last = [], []
+    for at in range(0, TILE, 8):
+        one, two = before[at : at + 8], after[at : at + 8]
+        first.append(jnp.where(row == 0, 0.0, one) if at % width == 0 else one)
+        last.append(jnp.where(row == 7, 0.0, two) if (at + 8) % width == 0 else two)
+    return jnp.concatenate(first, axis=0), jnp.concatenate(last, axis=0)
 
 
 def write_shifted(buf, row, width, tile, lanes, flip):
-    at = lax.broadcasted_iota(jnp.int32, tile.shape, 0) & (width - 1)
-    before = jnp.where(at == 0, 0.0, pltpu.roll(tile, 1, 0))
-    after = jnp.where(at == width - 1, 0.0, pltpu.roll(tile, TILE - 1, 0))
+    before, after = moved(tile, width)
     if flip:
         before, after = after, before
     rows = pl.ds(row, TILE)
@@ -181,11 +176,13 @@
     return [(level if at == 0 or level < 2 else 3, cell + at, row + at, width, at) for at in range(0, cells, TILE)]
 
 
-def pipelined(produce, consume):
+def pipelined(produce, consume, ready=lambda: None):
     produce(BLOCKS[0])
     for i, block in enumerate(BLOCKS):
         if i + 1 < len(BLOCKS):
             produce(BLOCKS[i + 1])
+        if i == 0:
+            ready()
         consume(block)
 
 
@@ -240,8 +237,8 @@
 def act_tiles(block, z, scale, offset, buf, keep=None):
     masks = tail_masks()
     for level, cell, row, width, _ in tiles_of(block):
-        y = z[cell : cell + TILE, :] * level_rows(level, scale, masks) + level_rows(level, offset, masks)
-        a = y * (0.5 * jnp.tanh(0.5 * y) + 0.5)
+        h = z[cell : cell + TILE, :] * level_rows(level, scale, masks) + level_rows(level, offset, masks)
+        a = h * jnp.tanh(h) + h
         if level == 3:
             a = jnp.where(masks[0] | masks[1], a, 0.0)
         write_shifted(buf, row, width, a, C, False)
@@ -251,16 +248,16 @@
 
 class Upward:
     def __init__(self, dy_out, z, mean, rstd, gain, shift):
-        self.dy_out, self.z, self.rstd, self.neg, self.gain, self.shift = dy_out, z, rstd, -mean * rstd, gain, shift
+        self.dy_out, self.z, self.rstd, self.neg, self.gain, self.shift = dy_out, z, rstd, -mean * rstd, 0.5 * gain, 0.5 * shift
         self.sums = [[jnp.zeros((8, C), f32), jnp.zeros((8, C), f32)] for _ in COUNTS]
 
     def add(self, block, da):
         masks = tail_masks()
         for level, cell, _, _, at in tiles_of(block):
             zhat = self.z[cell : cell + TILE, :] * level_rows(level, self.rstd, masks) + level_rows(level, self.neg, masks)
-            y = zhat * self.gain + self.shift
-            s = 0.5 * jnp.tanh(0.5 * y) + 0.5
-            dy = da[at : at + TILE] * (s * (1.0 + y * (1.0 - s)))
+            h = zhat * self.gain + self.shift
+            t = jnp.tanh(h)
+            dy = da[at : at + TILE] * ((1.0 + t) * (1.0 + h * (1.0 - t)))
             self.dy_out[cell : cell + TILE, :] = dy
             dyz = dy * zhat
             if level < 3:
@@ -271,8 +268,8 @@
                 self.sums[to] = [self.sums[to][0] + fold(one), self.sums[to][1] + fold(two)]
 
     def finish(self, sums_out):
-        sums_out[0:8, :] = stack_rows([v[0] for v in self.sums])
-        sums_out[8:16, :] = stack_rows([v[1] for v in self.sums])
+        sums_out[0:8, :] = 0.5 * stack_rows([v[0] for v in self.sums])
+        sums_out[8:16, :] = 0.5 * stack_rows([v[1] for v in self.sums])
 
 
 def norm_back(dy, z, mean, rstd, gain, sums, buf):
@@ -280,7 +277,7 @@
     inv_counts = counts_column()
     mean_e = group_sum(sum_dy * gain) * inv_counts
     mean_ez = group_sum(sum_dyz * gain) * inv_counts
-    on_dy = rstd * gain
+    on_dy = 0.5 * rstd * gain
     on_zhat = rstd * mean_ez
     on_z = -on_zhat * rstd
     flat = on_zhat * mean * rstd - rstd * mean_e
@@ -405,14 +402,19 @@
 
 
 def write_own_kernel(layer, order, own, *refs):
-    out, wide, sems = refs[-3:]
-    for copy in write_half(layer, bit_of(order, 0), own, out, wide, sems):
+    out, wide, sems = refs[-3 - (2 if not layer else 0) :][:1] + refs[-2:]
+    copies = write_half(layer, bit_of(order, 0), own, out, wide, sems)
+    if not layer:
+        vecs, (gains_out, shifts_out) = refs[:LAYERS], refs[-4:-2]
+        gains_out[...] = jnp.concatenate([v[0:1, :] for v in vecs], axis=0)
+        shifts_out[...] = jnp.concatenate([v[1:2, :] for v in vecs], axis=0)
+    for copy in copies:
         copy.wait()
 
 
 def write_got_kernel(layer, order, extra, got, *refs):
     bit = bit_of(order, 0)
-    out, wide, sems = refs[-3 - (1 if extra else 2 if not layer else 0) :][:1] + refs[-2:]
+    out, wide, sems = refs[-3 - (1 if extra else 0) :][:1] + refs[-2:]
     copies = write_half(layer, 1 - bit, got, out, wide, sems)
     half = C // 2
     if extra:
@@ -421,10 +423,6 @@
             rest[pl.ds(pl.multiple_of(t * C + bit * half, half), half), :] = own[(9 + t) * half : (10 + t) * half, :]
             rest[pl.ds(pl.multiple_of(t * C + (1 - bit) * half, half), half), :] = got[(9 + t) * half : (10 + t) * half, :]
         rest[extra * C :, :] = pack(vec[...])
-    elif not layer:
-        *vecs, _, _, gains_out, shifts_out, _, _ = refs
-        gains_out[...] = jnp.concatenate([v[0:1, :] for v in vecs], axis=0)
-        shifts_out[...] = jnp.concatenate([v[1:2, :] for v in vecs], axis=0)
     for copy in copies:
         copy.wait()
 
@@ -483,7 +481,57 @@
     scratch[26:30, :] = tile[16:20]
 
 
-def prepare_kernel(head, cls, reg, pos, hw, hg, tail):
+class Heads:
+    def __init__(self, hg, hk, hbuf, bias, scale):
+        self.hg, self.hk, self.hbuf, self.scale = hg, hk, hbuf, scale
+        self.bias = jnp.concatenate([bias[...], jnp.zeros((1, LANES - HEAD), f32)], axis=1)
+        self.total = jnp.zeros((8, LANES), f32)
+        self.scales = [jnp.zeros((8, LANES), f32) for _ in COUNTS]
+
+    def add(self, block, buf):
+        _, cells, first, width, _ = block
+        raw_block = None
+        for i in range(3):
+            at = first + (i - 1) * width
+            for j in range(3):
+                tap = (i * 3 + j) * LANES
+                term = lax.dot_general(
+                    buf[at : at + cells, j * C : (j + 1) * C],
+                    self.hk[tap : tap + LANES, :],
+                    (((1,), (1,)), ((), ())),
+                    preferred_element_type=f32,
+                )
+                raw_block = term if raw_block is None else raw_block + term
+        lane = lax.broadcasted_iota(jnp.int32, (TILE, LANES), 1)
+        dist = (lane >= CLASSES) & (lane < CLASSES + 4) & (lax.axis_index("tower") == 1)
+        third, fourth = (m[:, :LANES] for m in tail_masks())
+        for level, cell, row, width, at in tiles_of(block):
+            raw = raw_block[at : at + TILE] + self.bias
+            g = self.hg[cell : cell + TILE, :]
+            if level < 3:
+                ls, use = self.scale[0:1, level : level + 1], dist
+            else:
+                ls = jnp.where(third, self.scale[0:1, 3:4], self.scale[0:1, 4:5])
+                use = dist & (third | fourth)
+            weighted = jnp.where(use, g * jnp.exp(ls * raw), 0.0)
+            term = weighted * raw
+            parts = [(level, term)] if level < 3 else [(3, jnp.where(third, term, 0.0)), (4, jnp.where(fourth, term, 0.0))]
+            for to, value in parts:
+                self.scales[to] = self.scales[to] + fold(value)
+            tile = jnp.where(dist, weighted * ls, g).astype(bf16).astype(f32)
+            self.total = self.total + fold(tile)
+            after, before = moved(tile, width)
+            middle = pltpu.roll(tile, HEAD, 1)
+            after = pltpu.roll(after, 2 * HEAD - LANES, 1)
+            rows = slice(row, row + TILE)
+            self.hbuf[rows, 0:LANES] = jnp.where(lane < HEAD, before, middle).astype(bf16)
+            self.hbuf[rows, LANES : 2 * LANES] = jnp.where(lane < 2 * HEAD - LANES, middle, after).astype(bf16)
+
+    def rows(self):
+        return [jnp.sum(v, axis=0, keepdims=True) for v in [self.total] + self.scales]
+
+
+def prepare_kernel(head, cls, reg, pos, hw, hk, hg, tail):
     box = reg[...].astype(f32) * pos[...].astype(f32)
     is_class = lax.axis_index("tower") == 0
     rows = jnp.concatenate(
@@ -501,12 +549,15 @@
     for i in range(3):
         three = jnp.concatenate([head[i, j].astype(f32) for j in range(3)] + [jnp.zeros((1, C), f32)], axis=0)
         hw[i * C : (i + 1) * C, :] = three.astype(bf16)
+        for j in range(3):
+            one = jnp.concatenate([head[i, j].astype(f32), jnp.zeros((LANES - HEAD, C), f32)], axis=0)
+            hk[(i * 3 + j) * LANES : (i * 3 + j + 1) * LANES, :] = one.astype(bf16)
 
 
 def first_kernel(
-    order, scale, own, other, bn_mean, bn_var, w_hbm, gains, shifts, head, head_bias, hw, hg_in,
+    order, scale, own, other, bn_mean, bn_var, w_hbm, gains, shifts, head_bias, hw, hk, hg,
     w, z_out, a_out, stats_out, dy_out, sums_out, keep_out, send_out, vec_out,
-    buf, z_last, a_last, dy, sums, hg, hbuf, u, turned, tail, scale_sums, sems,
+    buf, z_last, a_last, dy, sums, hbuf, turned, tail, sems,
 ):
     loads = [pltpu.make_async_copy(w_hbm.at[l], w.at[l], sems.at[l]) for l in range(LAYERS)]
     for load in loads:
@@ -523,23 +574,20 @@
         right = jnp.where(tower == 0, other[rows, :].astype(f32), own[rows, :].astype(f32))
         return (jnp.concatenate([left, right], axis=1) - mean0) * inverse
 
-    def base(level, cell, row, width, carry):
-        if level < 3:
-            tile = halves(pl.ds(cell, TILE))
-        else:
-            spread_tail(halves(slice(1344, PIX)), tail)
-            tile = tail[...]
-        write_shifted(buf, row, width, tile, C, False)
-        return carry
-
-    each_tile(base, jnp.int32(0))
-    for cell, cells, row, width in PARTS:
-        a_out[0, cell : cell + cells, :] = center(buf, cells, row, C)
+    def base(block):
+        for level, cell, row, width, _ in tiles_of(block):
+            if level < 3:
+                tile = halves(slice(cell, cell + TILE))
+            else:
+                spread_tail(halves(slice(1344, PIX)), tail)
+                tile = tail[...]
+            write_shifted(buf, row, width, tile, C, False)
+            a_out[0, cell : cell + TILE, :] = tile.astype(bf16)
+
     scale_rows = offset_rows = None
     for l in range(LAYERS):
         z = z_out.at[l] if l < LAYERS - 1 else z_last
         stats = Stats()
-        loads[l].wait()
 
         def consume(block, l=l, z=z, stats=stats):
             out = conv_block(block, buf, w[l])
@@ -547,103 +595,38 @@
             stats.add(block, out)
 
         if l == 0:
-            for block in BLOCKS:
-                consume(block)
+            produce = base
         else:
             keep = a_out.at[l] if l < LAYERS - 1 else a_last
             before = z_out.at[l - 1]
             produce = lambda block: act_tiles(block, before, scale_rows, offset_rows, buf, keep)
-            pipelined(produce, consume)
+        pipelined(produce, consume, loads[l].wait)
         mean, rstd = stats.finish()
         if l < LAYERS - 1:
             stats_out[l, 0:8, :] = mean
             stats_out[l, 8:16, :] = rstd
-        scale_rows = rstd * gains[l : l + 1]
-        offset_rows = shifts[l : l + 1] - mean * scale_rows
-    for block in BLOCKS:
-        act_tiles(block, z_last, scale_rows, offset_rows, buf)
-
-    lane = lax.broadcasted_iota(jnp.int32, (TILE, LANES), 1)
-    row = lax.broadcasted_iota(jnp.int32, (TILE, LANES), 0)
-    third = ((row >= 16) & (row < 24)) | ((row >= 32) & (row < 40))
-    fourth = (row >= 26) & (row < 30)
-
-    @pl.when(tower == 0)
-    def _():
-        hg[...] = hg_in[...]
-        scale_sums[...] = jnp.zeros(scale_sums.shape, f32)
-
-    @pl.when(tower == 1)
-    def _():
-        for cell, cells, first, width in PARTS:
-            for at in range(0, cells, 256):
-                size = min(256, cells - at)
-                total = None
-                for i in range(3):
-                    from_row = first + at + (i - 1) * width
-                    for j in range(3):
-                        kernel = jnp.concatenate([head[i, j], jnp.zeros((LANES - HEAD, C), bf16)], axis=0)
-                        term = lax.dot_general(
-                            buf[from_row : from_row + size, j * C : (j + 1) * C],
-                            kernel,
-                            (((1,), (1,)), ((), ())),
-                            preferred_element_type=f32,
-                        )
-                        total = term if total is None else total + term
-                u[cell + at : cell + at + size, :] = total
-        bias = jnp.concatenate([head_bias[...], jnp.zeros((1, LANES - HEAD), f32)], axis=1)
-        dist_lane = (lane >= CLASSES) & (lane < CLASSES + 4)
-
-        def boxes(level, cell, row, width, carry):
-            raw = u[pl.ds(cell, TILE), :] + bias
-            g = hg_in[pl.ds(cell, TILE), :]
-            if level < 3:
-                ls = scale[0:1, level : level + 1]
-                use = dist_lane
-            else:
-                ls = jnp.where(third, scale[0:1, 3:4], scale[0:1, 4:5])
-                use = dist_lane & (third | fourth)
-            weighted = jnp.where(use, g * jnp.exp(ls * raw), 0.0)
-            hg[pl.ds(cell, TILE), :] = jnp.where(dist_lane, weighted * ls, g)
-            term = weighted * raw
-            if level < 3:
-                return carry + fold(term)
-            return (fold(jnp.where(third, term, 0.0)), fold(jnp.where(fourth, term, 0.0)))
-
-        r = each_tile(boxes, jnp.zeros((8, LANES), f32))
-        scale_sums[...] = stack_rows([r[0], r[1], r[2], r[3][0], r[3][1]])
-
-    scale_sum_rows = [scale_sums[k : k + 1, :] for k in range(len(COUNTS))]
-
-    def head_rows(level, cell, row, width, carry):
-        tile = hg[pl.ds(cell, TILE), :].astype(bf16).astype(f32)
-        at = lax.broadcasted_iota(jnp.int32, tile.shape, 0) & (width - 1)
-        after = jnp.where(at == 0, 0.0, pltpu.roll(tile, 1, 0))
-        before = jnp.where(at == width - 1, 0.0, pltpu.roll(tile, TILE - 1, 0))
-        middle = pltpu.roll(tile, HEAD, 1)
-        after = pltpu.roll(after, 2 * HEAD - LANES, 1)
-        rows = pl.ds(row, TILE)
-        hbuf[rows, 0:LANES] = jnp.where(lane < HEAD, before, middle).astype(bf16)
-        hbuf[rows, LANES : 2 * LANES] = jnp.where(lane < 2 * HEAD - LANES, middle, after).astype(bf16)
-        return carry + fold(tile)
-
-    r = each_tile(head_rows, jnp.zeros((8, LANES), f32))
-    bias_row = jnp.sum(r[0] + r[1] + r[2] + r[3], axis=0, keepdims=True)
-
+        scale_rows = 0.5 * rstd * gains[l : l + 1]
+        offset_rows = 0.5 * shifts[l : l + 1] - mean * scale_rows
+    l = LAYERS - 1
+    heads = Heads(hg, hk, hbuf, head_bias, scale)
+    up = Upward(dy, z_last, mean, rstd, gains[l : l + 1], shifts[l : l + 1])
+    for i in range(len(BLOCKS) + 2):
+        if i < len(BLOCKS):
+            act_tiles(BLOCKS[i], z_last, scale_rows, offset_rows, buf)
+        if 1 <= i <= len(BLOCKS):
+            heads.add(BLOCKS[i - 1], buf)
+        if i >= 2:
+            _, cells, row, width, _ = BLOCKS[i - 2]
+            left = jnp.concatenate([hbuf[row - d * width : row - d * width + cells, :] for d in (-1, 0, 1)], axis=1)
+            up.add(BLOCKS[i - 2], jnp.dot(left, hw[...], preferred_element_type=f32))
+    up.finish(sums)
     bit = bit_of(order, 0)
     a4t = jnp.concatenate([center(buf, n, r, C).T for _, n, r, _ in PARTS], axis=1)
     for i in range(3):
         split_store(bit, 9 + i, kernel_grad(a4t, hbuf, i), keep_out, send_out)
-    l = LAYERS - 1
-    up = Upward(dy, z_last, mean, rstd, gains[l : l + 1], shifts[l : l + 1])
-    for block in BLOCKS:
-        _, cells, row, width, _ = block
-        left = jnp.concatenate([hbuf[row - d * width : row - d * width + cells, :] for d in (-1, 0, 1)], axis=1)
-        up.add(block, jnp.dot(left, hw[...], preferred_element_type=f32))
-    up.finish(sums)
     produce, norm_sums = norm_back(dy, z_last, mean, rstd, gains[l : l + 1], sums, buf)
     wide = lambda v: jnp.concatenate([v, jnp.zeros_like(v)], axis=1)
-    vec = vector_rows(norm_sums + [wide(bias_row)] + [wide(v) for v in scale_sum_rows])
+    vec = vector_rows(norm_sums + [wide(row) for row in heads.rows()])
     vec_out[...] = vec
     send_out[12 * half :, :] = pack(vec)
     turned[...] = a_last[...].T
@@ -695,20 +678,20 @@
         token,
         (head, cls, reg, pos),
         [VMEM] * 4,
-        [pltpu.VMEM((3 * C, C), bf16), pltpu.VMEM((CELLS, LANES), f32)],
-        [VMEM] * 2,
+        [pltpu.VMEM((3 * C, C), bf16), pltpu.VMEM((9 * LANES, C), bf16), pltpu.VMEM((CELLS, LANES), f32)],
+        [VMEM] * 3,
         "prepare",
         [pltpu.VMEM((TILE, C), f32)],
         16,
     )
 
 
-def run_first(order, token, scale, own, other, mean, var, w, gains, shifts, head, bias, hw, hg):
+def run_first(order, token, scale, own, other, mean, var, w, gains, shifts, bias, hw, hk, hg):
     half = C // 2
     return call(
         functools.partial(first_kernel, order),
         token,
-        (scale, own, other, mean, var, w, gains, shifts, head, bias, hw, hg),
+        (scale, own, other, mean, var, w, gains, shifts, bias, hw, hk, hg),
         [VMEM] * 5 + [HBM] + [VMEM] * 6,
         [
             pltpu.VMEM((LAYERS, 9 * C, C), bf16),
@@ -729,12 +712,9 @@
             pltpu.VMEM((CELLS, C), bf16),
             pltpu.VMEM((CELLS, C), f32),
             pltpu.VMEM((16, C), f32),
-            pltpu.VMEM((CELLS, LANES), f32),
             pltpu.VMEM((PADDED, 2 * LANES), bf16),
-            pltpu.VMEM((CELLS, LANES), f32),
             pltpu.VMEM((C, CELLS), bf16),
             pltpu.VMEM((TILE, C), f32),
-            pltpu.VMEM((8, LANES), f32),
             pltpu.SemaphoreType.DMA((LAYERS,)),
         ],
         FIRST_MIB,
@@ -780,6 +760,7 @@
 
     def advance(self, step, token):
         taps, rows = self.taps, self.rows
+        self.done = step
         vec = shape((8, C), f32)
         if step < self.splits:
             half = rows // 2
@@ -821,7 +802,7 @@
             ins, specs = ins + [self.keep, self.vec], specs + [VMEM] * 2
             outs.append(shape((extra * C + VEC, C), bf16))
             out_specs.append(VMEM)
-        elif not own and not self.layer:
+        elif own and not self.layer:
             ins, specs = ins + vecs, specs + [VMEM] * LAYERS
             outs += [shape((LAYERS, C), f32)] * 2
             out_specs += [VMEM] * 2
@@ -840,16 +821,16 @@
 
 
 TIMELINE = (
-    (2, 0), (1, 0), (3, 1), (0, 0), (3, 2), (1, 1), (2, 1), (3, 3), (1, 2), (0, 1), (1, 3), (2, 2),
-    (3, 4), (0, 2), (1, 4), (2, 3), (0, 3), (3, 5), (0, 4), (1, 5), (2, 4), (8, 0), (3, 6), (0, 5),
-    (1, 6), (2, 5), (0, 6), (3, 7), (2, 6), (0, 7), (1, 7), (3, 8), (2, 7), (9, 0), (1, 8), (0, 8),
-    (2, 8),
+    (2, 0), (1, 0), (3, 1), (0, 0), (2, 1), (3, 2), (2, 2), (3, 3), (1, 1), (0, 1), (3, 4), (2, 3),
+    (1, 2), (3, 5), (0, 2), (2, 4), (1, 3), (0, 3), (3, 6), (1, 4), (2, 5), (0, 4), (1, 5), (3, 7),
+    (0, 5), (2, 6), (3, 8), (1, 6), (8, 0), (0, 6), (9, 0), (0, 7), (1, 7), (2, 7), (2, 8), (1, 8),
+    (0, 8),
 )
 ORDERS = (
-    ((1, 2, 0, 3), (0, 1, 2, 3)),
-    ((2, 0, 1, 3), (1, 2, 0, 3)),
-    ((0, 1, 2, 3), (2, 0, 1, 3)),
-    ((0, 1, 2, 3), (2, 0, 1, 3)),
+    ((2, 0, 1, 3), (0, 1, 2, 3)),
+    ((0, 2, 1, 3), (1, 0, 2, 3)),
+    ((1, 2, 0, 3), (2, 0, 1, 3)),
+    ((0, 2, 1, 3), (1, 0, 2, 3)),
 )
 
 
@@ -882,12 +863,12 @@
     gains, shifts = in_hbm(norm_gain[0]), in_hbm(norm_bias[0])
     mean, var = in_hbm(bn_mean[None]), in_hbm(bn_var[None])
     head = in_hbm(jnp.swapaxes(head_weight, 2, 3))
-    (hw, hg), token = run_prepare(
+    (hw, hk, hg), token = run_prepare(
         mean, head, in_hbm(jnp.swapaxes(cls_cot[0], 0, 1)), in_hbm(jnp.swapaxes(reg_cot[0], 0, 1)), in_hbm(positive)
     )
     (w, z, a, stats, dy, dy_sums, keep, send, vec), token = run_first(
-        order[3], token, in_hbm(level_scale[None]), in_hbm(own), other, mean, var, w, gains, shifts, head,
-        in_hbm(head_bias[None]), hw, hg,
+        order[3], token, in_hbm(level_scale[None]), in_hbm(own), other, mean, var, w, gains, shifts,
+        in_hbm(head_bias[None]), hw, hk, hg,
     )
     sums = [None] * LAYERS
     sums[3] = Sum(3, 12, order[3], bits, keep, send, vec)
@@ -915,14 +896,15 @@
         elif step <= sums[l].steps:
             token = sums[l].advance(step, token)
         elif step == sums[l].steps + 1:
-            (out,), token = sums[l].finish(token, out, True, None)
+            assert l or all(one.done >= bits for one in sums)
+            (out, *more), token = sums[l].finish(token, out, True, [one.vec for one in sums])
+            if l == 0:
+                dgain, dshift = more
         else:
-            (out, *more), token = sums[l].finish(token, out, False, [one.vec for one in sums])
+            (out, *more), token = sums[l].finish(token, out, False, None)
             if l == 3:
                 (heads,) = more
                 got_heads = lax.ppermute(heads, "tower", swap)
-            elif l == 0:
-                dgain, dshift = more
     return (
         feature_grad[None],
         out.reshape(1, LAYERS, 3, 3, C, C),

time: 135 us -> 127 us (0.941)
  waiting for transfers between devices: 38.7 us -> 34.2 us
  starting transfers between devices: 41.2 us -> 37.1 us
    ppermute x28, starting transfers between devices: 40.6 us -> 36.5 us  [partner(): return lax.ppermute(value, ('dp', 'tower'), pairs)]
    ppermute x28, waiting for transfers between devices: 38 us -> 34.2 us  [partner(): return lax.ppermute(value, ('dp', 'tower'), pairs)]
  transfers between devices with their start and end apart: 31 -> 31, of which waited for: 17 -> 13; matrix products, arithmetic and copies ran while one was open for 0% -> 0% of each run, Pallas kernels for 22% -> 24%
where the time goes in v4:
time: 127 us
  Pallas kernels  54.4 us (43%)
  starting transfers between devices  37.1 us (29%)
  waiting for transfers between devices  34.2 us (27%)
    pallas_call x39, Pallas kernels, call(): pl.pallas_call(ordered, out_shape=list(outs) + [shape((8, LANES), f32)],...  54.4 us
    ppermute x28, starting transfers between devices, partner(): return lax.ppermute(value, ('dp', 'tower'), pairs)  36.5 us
    ppermute x28, waiting for transfers between devices, partner(): return lax.ppermute(value, ('dp', 'tower'), pairs)  34.2 us
  transfers between devices with their start and end apart: 31, of which 13 were waited for; matrix products, arithmetic and copies ran while one was open for 0% of the time, Pallas kernels for 24%

profile of v4, /device:TPU:0, one launch (start us, length us, event | category | flops | bytes accessed | tf_op | source)
XLA Modules:
  0.0 126.9 jit_solution(2245475168207985935)
XLA Ops:
  0.6 0.5 collective-permute-start
  1.2 1.5 %prepare.1 = (bf16[768,256]{1,0:T(8,128)(2,1)S(1)}, bf16[1152,256]{1,0:T(8,128)(2,1)S(1)}, f32[1408,128]{1,0:T(8,128)S(1)}, f32[8,128]{1,0:T(8,128)S(1)}) custom-call(bf16[3,3,85,256]{3,2,1,0:T(8,128)(2,1)} %bitcast.40, bf16[80,1364]{1,0:T(8,128)(2,1)} %bitcast.42, bf16[5,1364]{1,0:T(8,128)(2,1)} %bitcast.43, s32[1,1364]{1,0:T(1,128)} %refs_3_.1, ...), custom_call_target="tpu_custom_call" | custom-call | flops 1500000000 | bytes 1 | tf_op jit(solution)/shard_map/prepare/pallas_call | solution.py:330
  2.7 23.0 %forward_and_heads.1 = (bf16[4,2304,256]{2,1,0:T(8,128)(2,1)S(1)}, f32[3,1408,256]{2,1,0:T(8,128)S(1)}, bf16[3,1408,256]{2,1,0:T(8,128)(2,1)S(1)}, f32[3,16,256]...) custom-call(f32[1,5]{1,0:T(1,128)} %bitcast.38, ...), custom_call_target="tpu_custom_call" | custom-call | flops 1500000000 | bytes 1 | tf_op jit(solution)/shard_map/forward_and_heads/pallas_call | solution.py:330
  25.6 2.9 %collective-permute-start.1 = (bf16[1568,256]{1,0:T(8,128)(2,1)S(1)}, bf16[1568,256]{1,0:T(8,128)(2,1)S(1)}, u32[]{:S(2)}, u32[]{:S(2)}) collective-permute-start(bf16[1568,256]{1,0:T(8,128)(2,1)S(1)} %get-tuple-element.152), channel_id=1, source_target_pairs={{0,2},{1,5},{2,0},{3,7},{4,6},{5,1},{6,4},{7,3},{8,10},{9,13},{10,... | collective-permute-start | bytes 2408456 | tf_op jit(solution)/shard_map/ppermute | solution.py:759
  28.5 5.0 %layer_gradients_2.1 = (f32[1408,256]{1,0:T(8,128)S(1)}, f32[16,256]{1,0:T(8,128)S(1)}, bf16[1152,256]{1,0:T(8,128)(2,1)S(1)}, bf16[1184,256]{1,0:T(8,128)(2,1)S...) custom-call(f32[1408,256]{1,0:T(8,128)S(1)} %get-tuple-element.139.refs_0_, f32[16,256]{1,0:T(8,128)S(1)} %get-tuple-element.140.refs_1_, ...), custom_call_target="tpu_custom_call" | custom-call | flops 3000000000 | bytes 1 | tf_op jit(solution)/shard_map/layer_gradients_2/pallas_call | solution.py:330
  33.6 1.6 %collective-permute-start.5 = (bf16[1184,256]{1,0:T(8,128)(2,1)S(1)}, bf16[1184,256]{1,0:T(8,128)(2,1)S(1)}, u32[]{:S(2)}, u32[]{:S(2)}) collective-permute-start(bf16[1184,256]{1,0:T(8,128)(2,1)S(1)} %get-tuple-element.165), channel_id=1, source_target_pairs={{0,4},{1,9},{2,6},{3,11},{4,0},{5,13},{6,2},{7,15},{8,12},{9,1},{1... | collective-permute-start | bytes 1818632 | tf_op jit(solution)/shard_map/ppermute | solution.py:759
  35.2 5.0 %layer_gradients_1.1 = (f32[1408,256]{1,0:T(8,128)S(1)}, f32[16,256]{1,0:T(8,128)S(1)}, bf16[1152,256]{1,0:T(8,128)(2,1)S(1)}, bf16[1184,256]{1,0:T(8,128)(2,1)S...) custom-call(f32[1408,256]{1,0:T(8,128)S(1)} %get-tuple-element.146.refs_0_, f32[16,256]{1,0:T(8,128)S(1)} %get-tuple-element.147.refs_1_, ...), custom_call_target="tpu_custom_call" | custom-call | flops 5000000000 | bytes 1 | tf_op jit(solution)/shard_map/layer_gradients_1/pallas_call | solution.py:330
  40.2 0.5 halve_3_1.1
  40.7 1.6 %collective-permute-start.4 = (bf16[800,256]{1,0:T(8,128)(2,1)S(1)}, bf16[800,256]{1,0:T(8,128)(2,1)S(1)}, u32[]{:S(2)}, u32[]{:S(2)}) collective-permute-start(bf16[800,256]{1,0:T(8,128)(2,1)S(1)} %get-tuple-element.162), channel_id=1, source_target_pairs={{0,8},{1,3},{2,10},{3,1},{4,12},{5,7},{6,14},{7,5},{8,0},{9,11},{1... | collective-permute-start | bytes 1228808 | tf_op jit(solution)/shard_map/ppermute | solution.py:759
  42.4 4.9 %layer_gradients_0.1 = (f32[1408,128]{1,0:T(8,128)S(1)}, bf16[1408,128]{1,0:T(8,128)(2,1)S(1)}, bf16[1152,256]{1,0:T(8,128)(2,1)S(1)}, bf16[1184,256]{1,0:T(8,12...) custom-call(f32[1408,256]{1,0:T(8,128)S(1)} %get-tuple-element.149.refs_0_, ...), custom_call_target="tpu_custom_call" | custom-call | flops 2000000000 | bytes 1 | tf_op jit(solution)/shard_map/layer_gradients_0/pallas_call | solution.py:330
  47.3 0.2 halve_2_1.1
  47.5 0.5 collective-permute-start.7
  48.0 0.5 collective-permute-start.3
  48.6 0.2 collective-permute-done.4.refs_1_
  48.8 0.2 halve_3_2.1
  48.9 1.1 collective-permute-start.6
  50.0 1.6 %collective-permute-start.11 = (bf16[1184,256]{1,0:T(8,128)(2,1)S(1)}, bf16[1184,256]{1,0:T(8,128)(2,1)S(1)}, u32[]{:S(2)}, u32[]{:S(2)}) collective-permute-start(bf16[1184,256]{1,0:T(8,128)(2,1)S(1)} %get-tuple-element.187), channel_id=1, source_target_pairs={{0,8},{1,3},{2,10},{3,1},{4,12},{5,7},{6,14},{7,5},{8,0},{9,11},{1... | collective-permute-start | bytes 1818632 | tf_op jit(solution)/shard_map/ppermute | solution.py:759
  51.6 5.2 %collective-permute-done.7.refs_1_ = bf16[608,256]{1,0:T(8,128)(2,1)S(1)} collective-permute-done((bf16[608,256]{1,0:T(8,128)(2,1)S(1)}, bf16[608,256]{1,0:T(8,128)(2,1)S(1)}, u32[]{:S(2)}, u32[]{:S(2)}) %collective-permute-start.7) | collective-permute-done | bytes 311328 | tf_op jit(solution)/shard_map/ppermute | solution.py:759
  56.8 0.1 halve_2_2.1
  56.9 0.3 collective-permute-done.6.refs_1_
  57.3 2.7 %collective-permute-start.10 = (bf16[416,256]{1,0:T(8,128)(2,1)S(1)}, bf16[416,256]{1,0:T(8,128)(2,1)S(1)}, u32[]{:S(2)}, u32[]{:S(2)}) collective-permute-start(bf16[416,256]{1,0:T(8,128)(2,1)S(1)} %get-tuple-element.184.refs_0_), channel_id=1, source_target_pairs={{0,16},{1,17},{2,18},{3,19},{4,20},{5,21},{6,22},{7,23},{8,24},{9,... | collective-permute-start | bytes 638984 | tf_op jit(solution)/shard_map/ppermute | solution.py:759
  60.0 4.7 %collective-permute-done.3.refs_1_ = bf16[1184,256]{1,0:T(8,128)(2,1)S(1)} collective-permute-done((bf16[1184,256]{1,0:T(8,128)(2,1)S(1)}, bf16[1184,256]{1,0:T(8,128)(2,1)S(1)}, u32[]{:S(2)}, u32[]{:S(2)}) %collective-permute-start.3) | collective-permute-done | bytes 606240 | tf_op jit(solution)/shard_map/ppermute | solution.py:759
  64.6 0.2 halve_1_1.1
  64.8 1.7 %collective-permute-start.8 = (bf16[608,256]{1,0:T(8,128)(2,1)S(1)}, bf16[608,256]{1,0:T(8,128)(2,1)S(1)}, u32[]{:S(2)}, u32[]{:S(2)}) collective-permute-start(bf16[608,256]{1,0:T(8,128)(2,1)S(1)} %get-tuple-element.179), channel_id=1, source_target_pairs={{0,8},{1,3},{2,10},{3,1},{4,12},{5,7},{6,14},{7,5},{8,0},{9,11},{1... | collective-permute-start | bytes 933896 | tf_op jit(solution)/shard_map/ppermute | solution.py:759
  66.5 0.5 collective-permute-start.9
  67.0 0.8 collective-permute-done.11.refs_1_
  67.8 0.2 halve_0_1.1
  68.0 0.8 collective-permute-start.14
  68.8 0.1 add_3_4.1
  68.9 1.9 %collective-permute-start.15 = (bf16[416,256]{1,0:T(8,128)(2,1)S(1)}, bf16[416,256]{1,0:T(8,128)(2,1)S(1)}, u32[]{:S(2)}, u32[]{:S(2)}) collective-permute-start(bf16[416,256]{1,0:T(8,128)(2,1)S(1)} %get-tuple-element.201.refs_0_), channel_id=1, source_target_pairs={{0,4},{1,9},{2,6},{3,11},{4,0},{5,13},{6,2},{7,15},{8,12},{9,1},{1... | collective-permute-start | bytes 638984 | tf_op jit(solution)/shard_map/ppermute | solution.py:759
  70.8 1.1 collective-permute-done.9.refs_1_
  71.9 2.7 %collective-permute-start.13 = (bf16[320,256]{1,0:T(8,128)(2,1)S(1)}, bf16[320,256]{1,0:T(8,128)(2,1)S(1)}, u32[]{:S(2)}, u32[]{:S(2)}) collective-permute-start(bf16[320,256]{1,0:T(8,128)(2,1)S(1)} %get-tuple-element.196.refs_0_), channel_id=1, source_target_pairs={{0,16},{1,17},{2,18},{3,19},{4,20},{5,21},{6,22},{7,23},{8,24},{9,... | collective-permute-start | bytes 491528 | tf_op jit(solution)/shard_map/ppermute | solution.py:759
  74.5 0.1 halve_1_2.1
  74.7 1.1 collective-permute-start.12
  75.9 0.1 halve_0_2.1
  76.0 1.1 collective-permute-start.18
  77.1 1.1 collective-permute-start.17
  78.2 3.3 %collective-permute-done.13.refs_1_ = bf16[320,256]{1,0:T(8,128)(2,1)S(1)} collective-permute-done((bf16[320,256]{1,0:T(8,128)(2,1)S(1)}, bf16[320,256]{1,0:T(8,128)(2,1)S(1)}, u32[]{:S(2)}, u32[]{:S(2)}) %collective-permute-start.13) | collective-permute-done | bytes 163872 | tf_op jit(solution)/shard_map/ppermute | solution.py:759
  81.6 0.7 collective-permute-start.21
  82.3 1.1 collective-permute-start.16
  83.4 0.1 collective-permute-done.18.refs_1_
  83.7 4.3 %collective-permute-done.17.refs_1_ = bf16[768,256]{1,0:T(8,128)(2,1)S(1)} collective-permute-done((bf16[768,256]{1,0:T(8,128)(2,1)S(1)}, bf16[768,256]{1,0:T(8,128)(2,1)S(1)}, u32[]{:S(2)}, u32[]{:S(2)}) %collective-permute-start.17) | collective-permute-done | bytes 393248 | tf_op jit(solution)/shard_map/ppermute | solution.py:759
  88.2 3.5 %collective-permute-start.20 = (bf16[320,256]{1,0:T(8,128)(2,1)S(1)}, bf16[320,256]{1,0:T(8,128)(2,1)S(1)}, u32[]{:S(2)}, u32[]{:S(2)}) collective-permute-start(bf16[320,256]{1,0:T(8,128)(2,1)S(1)} %get-tuple-element.216.refs_0_), channel_id=1, source_target_pairs={{0,16},{1,17},{2,18},{3,19},{4,20},{5,21},{6,22},{7,23},{8,24},{9,... | collective-permute-start | bytes 491528 | tf_op jit(solution)/shard_map/ppermute | solution.py:759
  91.9 1.2 collective-permute-start.24
  93.1 1.3 %collective-permute-start.19 = (bf16[320,256]{1,0:T(8,128)(2,1)S(1)}, bf16[320,256]{1,0:T(8,128)(2,1)S(1)}, u32[]{:S(2)}, u32[]{:S(2)}) collective-permute-start(bf16[320,256]{1,0:T(8,128)(2,1)S(1)} %get-tuple-element.215.refs_0_), channel_id=1, source_target_pairs={{0,4},{1,9},{2,6},{3,11},{4,0},{5,13},{6,2},{7,15},{8,12},{9,1},{1... | collective-permute-start | bytes 491528 | tf_op jit(solution)/shard_map/ppermute | solution.py:759
  94.4 4.2 %collective-permute-done.20.refs_1_ = bf16[320,256]{1,0:T(8,128)(2,1)S(1)} collective-permute-done((bf16[320,256]{1,0:T(8,128)(2,1)S(1)}, bf16[320,256]{1,0:T(8,128)(2,1)S(1)}, u32[]{:S(2)}, u32[]{:S(2)}) %collective-permute-start.20) | collective-permute-done | bytes 163872 | tf_op jit(solution)/shard_map/ppermute | solution.py:759
  98.7 1.2 collective-permute-start.25
  100.0 0.6 collective-permute-start.22
  100.6 1.1 write_3_own.1
  101.7 2.4 %collective-permute-done.25.refs_1_ = bf16[320,256]{1,0:T(8,128)(2,1)S(1)} collective-permute-done((bf16[320,256]{1,0:T(8,128)(2,1)S(1)}, bf16[320,256]{1,0:T(8,128)(2,1)S(1)}, u32[]{:S(2)}, u32[]{:S(2)}) %collective-permute-start.25) | collective-permute-done | bytes 163872 | tf_op jit(solution)/shard_map/ppermute | solution.py:759
  104.2 1.6 %collective-permute-start.26 = (bf16[576,256]{1,0:T(8,128)(2,1)S(1)}, bf16[576,256]{1,0:T(8,128)(2,1)S(1)}, u32[]{:S(2)}, u32[]{:S(2)}) collective-permute-start(bf16[576,256]{1,0:T(8,128)(2,1)S(1)} %get-tuple-element.235.refs_0_), channel_id=1, source_target_pairs={{0,2},{1,5},{2,0},{3,7},{4,6},{5,1},{6,4},{7,3},{8,10},{9,13},{10,... | collective-permute-start | bytes 884744 | tf_op jit(solution)/shard_map/ppermute | solution.py:759
  105.9 1.1 write_3_got.1
  107.0 1.1 collective-permute-start.29
  108.2 0.7 collective-permute-start.28
  109.0 1.6 %feature_gradient.1 = (bf16[1364,128]{1,0:T(8,128)(2,1)}, f32[8,128]{1,0:T(8,128)S(1)}) custom-call(f32[1408,128]{1,0:T(8,128)S(1)} %get-tuple-element.156.refs_0_, bf16[1408,128]{1,0:T(8,128)(2,1)S(1)} %collective-permute-done.2.refs_1_, f32[1,256]{1,0:T(1,128)} %bitcast.35, f32[8,128]{1,0:T(8,128)S(1)} %get-tuple-element.233.refs_3_), custom_call_target="tpu_custom_call" | custom-call | flops 100000000 | bytes 1 | tf_op jit(solution)/shard_map/feature_gradient/pallas_call | solution.py:330
  110.6 0.4 collective-permute-done.26.refs_1_
  111.1 1.2 head_gradients.1
  112.3 1.7 %write_0_own.1 = (f32[9216,256]{1,0:T(8,128)}, f32[4,256]{1,0:T(4,128)}, f32[4,256]{1,0:T(4,128)}, f32[8,128]{1,0:T(8,128)S(1)}) custom-call(bf16[1152,256]{1,0:T(8,128)(2,1)S(1)} %get-tuple-element.237.refs_0_, f32[8,256]{1,0:T(8,128)S(1)} %get-tuple-element.240.refs_1_, f32[8,256]{1,0:T(8,128)S(1)} %get-tuple-element.241.refs_2_, ...), custom_call_target="tpu_custom_call", output_to_operand_aliasing={{0}: (5, {})} | custom-call | flops 1500000000 | bytes 1 | tf_op jit(solution)/shard_map/write_0_own/pallas_call | solution.py:330
  114.0 1.1 write_1_own.1
  115.1 1.1 write_2_own.1
  116.2 7.2 %collective-permute-done.29.refs_0_ = bf16[1152,256]{1,0:T(8,128)(2,1)S(1)} collective-permute-done((bf16[1152,256]{1,0:T(8,128)(2,1)S(1)}, bf16[1152,256]{1,0:T(8,128)(2,1)S(1)}, u32[]{:S(2)}, u32[]{:S(2)}) %collective-permute-start.29) | collective-permute-done | bytes 589856 | tf_op jit(solution)/shard_map/ppermute | solution.py:759
  123.4 1.1 write_2_got.1
  124.5 1.1 write_1_got.1
  125.6 1.1 write_0_got.1
  (37 shorter events, 1.4 us)
Async XLA Ops:
  0.6 2.0 %collective-permute-start = (bf16[1364,128]{1,0:T(8,128)(2,1)}, bf16[1364,128]{1,0:T(8,128)(2,1)S(1)}, u32[]{:S(2)}, u32[]{:S(2)}) collective-permute-start(bf16[1364,128]{1,0:T(8,128)(2,1)} %bitcast.24), channel_id=1, source_target_pairs={{0,1},{1,0},{2,3},{3,2},{4,5},{5,4},{6,7},{7,6},{8,9},{9,8},{10,11... | collective-permute-start | bytes 1047560 | tf_op jit(solution)/shard_map/ppermute | solution.py:861
  25.6 14.6 %collective-permute-start.1 = (bf16[1568,256]{1,0:T(8,128)(2,1)S(1)}, bf16[1568,256]{1,0:T(8,128)(2,1)S(1)}, u32[]{:S(2)}, u32[]{:S(2)}) collective-permute-start(bf16[1568,256]{1,0:T(8,128)(2,1)S(1)} %get-tuple-element.152), channel_id=1, source_target_pairs={{0,2},{1,5},{2,0},{3,7},{4,6},{5,1},{6,4},{7,3},{8,10},{9,13},{10,... | collective-permute-start | bytes 2408456 | tf_op jit(solution)/shard_map/ppermute | solution.py:759
  33.6 13.7 %collective-permute-start.5 = (bf16[1184,256]{1,0:T(8,128)(2,1)S(1)}, bf16[1184,256]{1,0:T(8,128)(2,1)S(1)}, u32[]{:S(2)}, u32[]{:S(2)}) collective-permute-start(bf16[1184,256]{1,0:T(8,128)(2,1)S(1)} %get-tuple-element.165), channel_id=1, source_target_pairs={{0,4},{1,9},{2,6},{3,11},{4,0},{5,13},{6,2},{7,15},{8,12},{9,1},{1... | collective-permute-start | bytes 1818632 | tf_op jit(solution)/shard_map/ppermute | solution.py:759
  40.7 8.0 %collective-permute-start.4 = (bf16[800,256]{1,0:T(8,128)(2,1)S(1)}, bf16[800,256]{1,0:T(8,128)(2,1)S(1)}, u32[]{:S(2)}, u32[]{:S(2)}) collective-permute-start(bf16[800,256]{1,0:T(8,128)(2,1)S(1)} %get-tuple-element.162), channel_id=1, source_target_pairs={{0,8},{1,3},{2,10},{3,1},{4,12},{5,7},{6,14},{7,5},{8,0},{9,11},{1... | collective-permute-start | bytes 1228808 | tf_op jit(solution)/shard_map/ppermute | solution.py:759
  47.5 9.2 %collective-permute-start.7 = (bf16[608,256]{1,0:T(8,128)(2,1)S(1)}, bf16[608,256]{1,0:T(8,128)(2,1)S(1)}, u32[]{:S(2)}, u32[]{:S(2)}) collective-permute-start(bf16[608,256]{1,0:T(8,128)(2,1)S(1)} %get-tuple-element.173), channel_id=1, source_target_pairs={{0,8},{1,3},{2,10},{3,1},{4,12},{5,7},{6,14},{7,5},{8,0},{9,11},{1... | collective-permute-start | bytes 933896 | tf_op jit(solution)/shard_map/ppermute | solution.py:759
  48.0 16.6 %collective-permute-start.3 = (bf16[1184,256]{1,0:T(8,128)(2,1)S(1)}, bf16[1184,256]{1,0:T(8,128)(2,1)S(1)}, u32[]{:S(2)}, u32[]{:S(2)}) collective-permute-start(bf16[1184,256]{1,0:T(8,128)(2,1)S(1)} %get-tuple-element.159), channel_id=1, source_target_pairs={{0,2},{1,5},{2,0},{3,7},{4,6},{5,1},{6,4},{7,3},{8,10},{9,13},{10,... | collective-permute-start | bytes 1818632 | tf_op jit(solution)/shard_map/ppermute | solution.py:759
  48.9 8.3 %collective-permute-start.6 = (bf16[416,256]{1,0:T(8,128)(2,1)S(1)}, bf16[416,256]{1,0:T(8,128)(2,1)S(1)}, u32[]{:S(2)}, u32[]{:S(2)}) collective-permute-start(bf16[416,256]{1,0:T(8,128)(2,1)S(1)} %get-tuple-element.170), channel_id=1, source_target_pairs={{0,4},{1,9},{2,6},{3,11},{4,0},{5,13},{6,2},{7,15},{8,12},{9,1},{1... | collective-permute-start | bytes 638984 | tf_op jit(solution)/shard_map/ppermute | solution.py:759
  50.0 17.8 %collective-permute-start.11 = (bf16[1184,256]{1,0:T(8,128)(2,1)S(1)}, bf16[1184,256]{1,0:T(8,128)(2,1)S(1)}, u32[]{:S(2)}, u32[]{:S(2)}) collective-permute-start(bf16[1184,256]{1,0:T(8,128)(2,1)S(1)} %get-tuple-element.187), channel_id=1, source_target_pairs={{0,8},{1,3},{2,10},{3,1},{4,12},{5,7},{6,14},{7,5},{8,0},{9,11},{1... | collective-permute-start | bytes 1818632 | tf_op jit(solution)/shard_map/ppermute | solution.py:759
  57.3 11.5 %collective-permute-start.10 = (bf16[416,256]{1,0:T(8,128)(2,1)S(1)}, bf16[416,256]{1,0:T(8,128)(2,1)S(1)}, u32[]{:S(2)}, u32[]{:S(2)}) collective-permute-start(bf16[416,256]{1,0:T(8,128)(2,1)S(1)} %get-tuple-element.184.refs_0_), channel_id=1, source_target_pairs={{0,16},{1,17},{2,18},{3,19},{4,20},{5,21},{6,22},{7,23},{8,24},{9,... | collective-permute-start | bytes 638984 | tf_op jit(solution)/shard_map/ppermute | solution.py:759
  64.8 9.7 %collective-permute-start.8 = (bf16[608,256]{1,0:T(8,128)(2,1)S(1)}, bf16[608,256]{1,0:T(8,128)(2,1)S(1)}, u32[]{:S(2)}, u32[]{:S(2)}) collective-permute-start(bf16[608,256]{1,0:T(8,128)(2,1)S(1)} %get-tuple-element.179), channel_id=1, source_target_pairs={{0,8},{1,3},{2,10},{3,1},{4,12},{5,7},{6,14},{7,5},{8,0},{9,11},{1... | collective-permute-start | bytes 933896 | tf_op jit(solution)/shard_map/ppermute | solution.py:759
  66.5 5.3 %collective-permute-start.9 = (bf16[320,256]{1,0:T(8,128)(2,1)S(1)}, bf16[320,256]{1,0:T(8,128)(2,1)S(1)}, u32[]{:S(2)}, u32[]{:S(2)}) collective-permute-start(bf16[320,256]{1,0:T(8,128)(2,1)S(1)} %get-tuple-element.182), channel_id=1, source_target_pairs={{0,2},{1,5},{2,0},{3,7},{4,6},{5,1},{6,4},{7,3},{8,10},{9,13},{10,... | collective-permute-start | bytes 491528 | tf_op jit(solution)/shard_map/ppermute | solution.py:759
  68.0 7.8 %collective-permute-start.14 = (bf16[608,256]{1,0:T(8,128)(2,1)S(1)}, bf16[608,256]{1,0:T(8,128)(2,1)S(1)}, u32[]{:S(2)}, u32[]{:S(2)}) collective-permute-start(bf16[608,256]{1,0:T(8,128)(2,1)S(1)} %get-tuple-element.199), channel_id=1, source_target_pairs={{0,2},{1,5},{2,0},{3,7},{4,6},{5,1},{6,4},{7,3},{8,10},{9,13},{10,... | collective-permute-start | bytes 933896 | tf_op jit(solution)/shard_map/ppermute | solution.py:759
  68.9 6.9 %collective-permute-start.15 = (bf16[416,256]{1,0:T(8,128)(2,1)S(1)}, bf16[416,256]{1,0:T(8,128)(2,1)S(1)}, u32[]{:S(2)}, u32[]{:S(2)}) collective-permute-start(bf16[416,256]{1,0:T(8,128)(2,1)S(1)} %get-tuple-element.201.refs_0_), channel_id=1, source_target_pairs={{0,4},{1,9},{2,6},{3,11},{4,0},{5,13},{6,2},{7,15},{8,12},{9,1},{1... | collective-permute-start | bytes 638984 | tf_op jit(solution)/shard_map/ppermute | solution.py:759
  71.9 9.6 %collective-permute-start.13 = (bf16[320,256]{1,0:T(8,128)(2,1)S(1)}, bf16[320,256]{1,0:T(8,128)(2,1)S(1)}, u32[]{:S(2)}, u32[]{:S(2)}) collective-permute-start(bf16[320,256]{1,0:T(8,128)(2,1)S(1)} %get-tuple-element.196.refs_0_), channel_id=1, source_target_pairs={{0,16},{1,17},{2,18},{3,19},{4,20},{5,21},{6,22},{7,23},{8,24},{9,... | collective-permute-start | bytes 491528 | tf_op jit(solution)/shard_map/ppermute | solution.py:759
  74.7 7.6 %collective-permute-start.12 = (bf16[320,256]{1,0:T(8,128)(2,1)S(1)}, bf16[320,256]{1,0:T(8,128)(2,1)S(1)}, u32[]{:S(2)}, u32[]{:S(2)}) collective-permute-start(bf16[320,256]{1,0:T(8,128)(2,1)S(1)} %get-tuple-element.194), channel_id=1, source_target_pairs={{0,4},{1,9},{2,6},{3,11},{4,0},{5,13},{6,2},{7,15},{8,12},{9,1},{1... | collective-permute-start | bytes 491528 | tf_op jit(solution)/shard_map/ppermute | solution.py:759
  76.0 7.6 %collective-permute-start.18 = (bf16[320,256]{1,0:T(8,128)(2,1)S(1)}, bf16[320,256]{1,0:T(8,128)(2,1)S(1)}, u32[]{:S(2)}, u32[]{:S(2)}) collective-permute-start(bf16[320,256]{1,0:T(8,128)(2,1)S(1)} %get-tuple-element.210), channel_id=1, source_target_pairs={{0,4},{1,9},{2,6},{3,11},{4,0},{5,13},{6,2},{7,15},{8,12},{9,1},{1... | collective-permute-start | bytes 491528 | tf_op jit(solution)/shard_map/ppermute | solution.py:759
  77.1 10.9 %collective-permute-start.17 = (bf16[768,256]{1,0:T(8,128)(2,1)S(1)}, bf16[768,256]{1,0:T(8,128)(2,1)S(1)}, u32[]{:S(2)}, u32[]{:S(2)}) collective-permute-start(bf16[768,256]{1,0:T(8,128)(2,1)S(1)} %get-tuple-element.208.refs_0_), channel_id=1, source_target_pairs={{0,8},{1,3},{2,10},{3,1},{4,12},{5,7},{6,14},{7,5},{8,0},{9,11},{1... | collective-permute-start | bytes 1179656 | tf_op jit(solution)/shard_map/ppermute | solution.py:759
  81.6 10.2 %collective-permute-start.21 = (bf16[320,256]{1,0:T(8,128)(2,1)S(1)}, bf16[320,256]{1,0:T(8,128)(2,1)S(1)}, u32[]{:S(2)}, u32[]{:S(2)}) collective-permute-start(bf16[320,256]{1,0:T(8,128)(2,1)S(1)} %get-tuple-element.218.refs_0_), channel_id=1, source_target_pairs={{0,2},{1,5},{2,0},{3,7},{4,6},{5,1},{6,4},{7,3},{8,10},{9,13},{10,... | collective-permute-start | bytes 491528 | tf_op jit(solution)/shard_map/ppermute | solution.py:759
  82.3 9.4 %collective-permute-start.16 = (bf16[320,256]{1,0:T(8,128)(2,1)S(1)}, bf16[320,256]{1,0:T(8,128)(2,1)S(1)}, u32[]{:S(2)}, u32[]{:S(2)}) collective-permute-start(bf16[320,256]{1,0:T(8,128)(2,1)S(1)} %get-tuple-element.206.refs_0_), channel_id=1, source_target_pairs={{0,16},{1,17},{2,18},{3,19},{4,20},{5,21},{6,22},{7,23},{8,24},{9,... | collective-permute-start | bytes 491528 | tf_op jit(solution)/shard_map/ppermute | solution.py:759
  88.1 17.8 %collective-permute-start.23 = (bf16[1536,256]{1,0:T(8,128)(2,1)S(1)}, bf16[1536,256]{1,0:T(8,128)(2,1)S(1)}, u32[]{:S(2)}, u32[]{:S(2)}) collective-permute-start(bf16[1536,256]{1,0:T(8,128)(2,1)S(1)} %get-tuple-element.223.refs_0_.refs_1_), channel_id=1, source_target_pairs={{0,2},{1,5},{2,0},{3,7},{4,6},{5,1},{6,4},{7,3},{8,10},{9,13},{10,... | collective-permute-start | bytes 2359304 | tf_op jit(solution)/shard_map/ppermute | solution.py:759
  88.2 10.5 %collective-permute-start.20 = (bf16[320,256]{1,0:T(8,128)(2,1)S(1)}, bf16[320,256]{1,0:T(8,128)(2,1)S(1)}, u32[]{:S(2)}, u32[]{:S(2)}) collective-permute-start(bf16[320,256]{1,0:T(8,128)(2,1)S(1)} %get-tuple-element.216.refs_0_), channel_id=1, source_target_pairs={{0,16},{1,17},{2,18},{3,19},{4,20},{5,21},{6,22},{7,23},{8,24},{9,... | collective-permute-start | bytes 491528 | tf_op jit(solution)/shard_map/ppermute | solution.py:759
  91.9 13.9 %collective-permute-start.24 = (bf16[576,256]{1,0:T(8,128)(2,1)S(1)}, bf16[576,256]{1,0:T(8,128)(2,1)S(1)}, u32[]{:S(2)}, u32[]{:S(2)}) collective-permute-start(bf16[576,256]{1,0:T(8,128)(2,1)S(1)} %get-tuple-element.227.refs_0_), channel_id=1, source_target_pairs={{0,8},{1,3},{2,10},{3,1},{4,12},{5,7},{6,14},{7,5},{8,0},{9,11},{1... | collective-permute-start | bytes 884744 | tf_op jit(solution)/shard_map/ppermute | solution.py:759
  93.1 6.9 %collective-permute-start.19 = (bf16[320,256]{1,0:T(8,128)(2,1)S(1)}, bf16[320,256]{1,0:T(8,128)(2,1)S(1)}, u32[]{:S(2)}, u32[]{:S(2)}) collective-permute-start(bf16[320,256]{1,0:T(8,128)(2,1)S(1)} %get-tuple-element.215.refs_0_), channel_id=1, source_target_pairs={{0,4},{1,9},{2,6},{3,11},{4,0},{5,13},{6,2},{7,15},{8,12},{9,1},{1... | collective-permute-start | bytes 491528 | tf_op jit(solution)/shard_map/ppermute | solution.py:759
  98.7 5.4 %collective-permute-start.25 = (bf16[320,256]{1,0:T(8,128)(2,1)S(1)}, bf16[320,256]{1,0:T(8,128)(2,1)S(1)}, u32[]{:S(2)}, u32[]{:S(2)}) collective-permute-start(bf16[320,256]{1,0:T(8,128)(2,1)S(1)} %get-tuple-element.228.refs_0_), channel_id=1, source_target_pairs={{0,4},{1,9},{2,6},{3,11},{4,0},{5,13},{6,2},{7,15},{8,12},{9,1},{1... | collective-permute-start | bytes 491528 | tf_op jit(solution)/shard_map/ppermute | solution.py:759
  100.0 9.0 %collective-permute-start.2 = (bf16[1408,128]{1,0:T(8,128)(2,1)S(1)}, bf16[1408,128]{1,0:T(8,128)(2,1)S(1)}, u32[]{:S(2)}, u32[]{:S(2)}) collective-permute-start(bf16[1408,128]{1,0:T(8,128)(2,1)S(1)} %get-tuple-element.157), channel_id=1, source_target_pairs={{0,1},{1,0},{2,3},{3,2},{4,5},{5,4},{6,7},{7,6},{8,9},{9,8},{10,11... | collective-permute-start | bytes 1081352 | tf_op jit(solution)/shard_map/ppermute | solution.py:895
  100.0 8.1 %collective-permute-start.22 = (bf16[576,256]{1,0:T(8,128)(2,1)S(1)}, bf16[576,256]{1,0:T(8,128)(2,1)S(1)}, u32[]{:S(2)}, u32[]{:S(2)}) collective-permute-start(bf16[576,256]{1,0:T(8,128)(2,1)S(1)} %get-tuple-element.222.refs_0_), channel_id=1, source_target_pairs={{0,8},{1,3},{2,10},{3,1},{4,12},{5,7},{6,14},{7,5},{8,0},{9,11},{1... | collective-permute-start | bytes 884744 | tf_op jit(solution)/shard_map/ppermute | solution.py:759
  104.2 6.8 %collective-permute-start.26 = (bf16[576,256]{1,0:T(8,128)(2,1)S(1)}, bf16[576,256]{1,0:T(8,128)(2,1)S(1)}, u32[]{:S(2)}, u32[]{:S(2)}) collective-permute-start(bf16[576,256]{1,0:T(8,128)(2,1)S(1)} %get-tuple-element.235.refs_0_), channel_id=1, source_target_pairs={{0,2},{1,5},{2,0},{3,7},{4,6},{5,1},{6,4},{7,3},{8,10},{9,13},{10,... | collective-permute-start | bytes 884744 | tf_op jit(solution)/shard_map/ppermute | solution.py:759
  107.0 4.1 %collective-permute-start.30 = (bf16[800,256]{1,0:T(8,128)(2,1)S(1)}, bf16[800,256]{1,0:T(8,128)(2,1)S(1)}, u32[]{:S(2)}, u32[]{:S(2)}) collective-permute-start(bf16[800,256]{1,0:T(8,128)(2,1)S(1)} %get-tuple-element.244.refs_0_), channel_id=1, source_target_pairs={{0,1},{1,0},{2,3},{3,2},{4,5},{5,4},{6,7},{7,6},{8,9},{9,8},{10,11... | collective-permute-start | bytes 1228808 | tf_op jit(solution)/shard_map/ppermute | solution.py:907
  107.0 16.3 %collective-permute-start.29 = (bf16[1152,256]{1,0:T(8,128)(2,1)S(1)}, bf16[1152,256]{1,0:T(8,128)(2,1)S(1)}, u32[]{:S(2)}, u32[]{:S(2)}) collective-permute-start(bf16[1152,256]{1,0:T(8,128)(2,1)S(1)} %get-tuple-element.239.refs_0_), channel_id=1, source_target_pairs={{0,4},{1,9},{2,6},{3,11},{4,0},{5,13},{6,2},{7,15},{8,12},{9,1},{1... | collective-permute-start | bytes 1769480 | tf_op jit(solution)/shard_map/ppermute | solution.py:759
  108.2 16.2 %collective-permute-start.28 = (bf16[1152,256]{1,0:T(8,128)(2,1)S(1)}, bf16[1152,256]{1,0:T(8,128)(2,1)S(1)}, u32[]{:S(2)}, u32[]{:S(2)}) collective-permute-start(bf16[1152,256]{1,0:T(8,128)(2,1)S(1)} %get-tuple-element.238.refs_0_), channel_id=1, source_target_pairs={{0,2},{1,5},{2,0},{3,7},{4,6},{5,1},{6,4},{7,3},{8,10},{9,13},{10,... | collective-permute-start | bytes 1769480 | tf_op jit(solution)/shard_map/ppermute | solution.py:759
  111.0 14.6 %collective-permute-start.27 = (bf16[1152,256]{1,0:T(8,128)(2,1)S(1)}, bf16[1152,256]{1,0:T(8,128)(2,1)S(1)}, u32[]{:S(2)}, u32[]{:S(2)}) collective-permute-start(bf16[1152,256]{1,0:T(8,128)(2,1)S(1)} %get-tuple-element.237.refs_0_), channel_id=1, source_target_pairs={{0,8},{1,3},{2,10},{3,1},{4,12},{5,7},{6,14},{7,5},{8,0},{9,11},{1... | collective-permute-start | bytes 1769480 | tf_op jit(solution)/shard_map/ppermute | solution.py:759

commit v5 on v4

--- a/solution.py
+++ b/solution.py
@@ -37,11 +37,10 @@
     "layer_gradients_2": 3000000000,
     "join_1_6": 1000000000,
     "halve_1_1": 2000000000,
-    "add_1_3": 300000000,
     "write_2_own": 3000000000,
     "join_2_6": 3000000000,
     "halve_0_1": 300000000,
-    "feature_gradient": 100000000,
+    "feature_gradient": 1000000000,
     "halve_3_1": 1500000000,
     "halve_2_1": 2000000000,
     "write_1_own": 100000000,
@@ -56,7 +55,7 @@
     "halve_0_2": 1500000000,
     "write_1_got": 2000000000,
     "join_0_5": 1000000,
-    "join_1_5": 1000000000,
+    "join_1_5": 2000000000,
     "halve_2_2": 2000000000,
     "join_0_6": 3000000000,
     "add_3_4": 300000000,

time: 127 us -> 125 us (0.984)
  waiting for transfers between devices: 34.2 us -> 32.1 us
    ppermute x28, waiting for transfers between devices: 34.2 us -> 32.1 us  [partner(): return lax.ppermute(value, ('dp', 'tower'), pairs)]
  transfers between devices with their start and end apart: 31 -> 31, of which waited for: 13 -> 14; matrix products, arithmetic and copies ran while one was open for 0% -> 0% of each run, Pallas kernels for 24% -> 24%
where the time goes in v5:
time: 125 us; the launch traced here: 124 us
  Pallas kernels  54.3 us (43%)
  starting transfers between devices  36.8 us (29%)
  waiting for transfers between devices  32.1 us (26%)
    pallas_call x39, Pallas kernels, call(): pl.pallas_call(ordered, out_shape=list(outs) + [shape((8, LANES), f32)],...  54.3 us
    ppermute x28, starting transfers between devices, partner(): return lax.ppermute(value, ('dp', 'tower'), pairs)  36.2 us
    ppermute x28, waiting for transfers between devices, partner(): return lax.ppermute(value, ('dp', 'tower'), pairs)  32.1 us
  transfers between devices with their start and end apart: 31, of which 14 were waited for; matrix products, arithmetic and copies ran while one was open for 0% of the time, Pallas kernels for 24%

profile of v5, /device:TPU:0, one launch (start us, length us, event | category | flops | bytes accessed | tf_op | source)
XLA Modules:
  0.0 124.4 jit_solution(16899791456479965937)
XLA Ops:
  0.6 0.5 collective-permute-start
  1.2 1.5 %prepare.1 = (bf16[768,256]{1,0:T(8,128)(2,1)S(1)}, bf16[1152,256]{1,0:T(8,128)(2,1)S(1)}, f32[1408,128]{1,0:T(8,128)S(1)}, f32[8,128]{1,0:T(8,128)S(1)}) custom-call(bf16[3,3,85,256]{3,2,1,0:T(8,128)(2,1)} %bitcast.40, bf16[80,1364]{1,0:T(8,128)(2,1)} %bitcast.41, bf16[5,1364]{1,0:T(8,128)(2,1)} %bitcast.42, s32[1,1364]{1,0:T(1,128)} %refs_3_.1, ...), custom_call_target="tpu_custom_call" | custom-call | flops 1500000000 | bytes 1 | tf_op jit(solution)/shard_map/prepare/pallas_call | solution.py:329
  2.7 23.0 %forward_and_heads.1 = (bf16[4,2304,256]{2,1,0:T(8,128)(2,1)S(1)}, f32[3,1408,256]{2,1,0:T(8,128)S(1)}, bf16[3,1408,256]{2,1,0:T(8,128)(2,1)S(1)}, f32[3,16,256]...) custom-call(f32[1,5]{1,0:T(1,128)} %bitcast.38, ...), custom_call_target="tpu_custom_call" | custom-call | flops 1500000000 | bytes 1 | tf_op jit(solution)/shard_map/forward_and_heads/pallas_call | solution.py:329
  25.6 2.9 %collective-permute-start.1 = (bf16[1568,256]{1,0:T(8,128)(2,1)S(1)}, bf16[1568,256]{1,0:T(8,128)(2,1)S(1)}, u32[]{:S(2)}, u32[]{:S(2)}) collective-permute-start(bf16[1568,256]{1,0:T(8,128)(2,1)S(1)} %get-tuple-element.152), channel_id=1, source_target_pairs={{0,2},{1,5},{2,0},{3,7},{4,6},{5,1},{6,4},{7,3},{8,10},{9,13},{10,... | collective-permute-start | bytes 2408456 | tf_op jit(solution)/shard_map/ppermute | solution.py:758
  28.5 5.0 %layer_gradients_2.1 = (f32[1408,256]{1,0:T(8,128)S(1)}, f32[16,256]{1,0:T(8,128)S(1)}, bf16[1152,256]{1,0:T(8,128)(2,1)S(1)}, bf16[1184,256]{1,0:T(8,128)(2,1)S...) custom-call(f32[1408,256]{1,0:T(8,128)S(1)} %get-tuple-element.139.refs_0_, f32[16,256]{1,0:T(8,128)S(1)} %get-tuple-element.140.refs_1_, ...), custom_call_target="tpu_custom_call" | custom-call | flops 3000000000 | bytes 1 | tf_op jit(solution)/shard_map/layer_gradients_2/pallas_call | solution.py:329
  33.6 1.6 %collective-permute-start.5 = (bf16[1184,256]{1,0:T(8,128)(2,1)S(1)}, bf16[1184,256]{1,0:T(8,128)(2,1)S(1)}, u32[]{:S(2)}, u32[]{:S(2)}) collective-permute-start(bf16[1184,256]{1,0:T(8,128)(2,1)S(1)} %get-tuple-element.165), channel_id=1, source_target_pairs={{0,4},{1,9},{2,6},{3,11},{4,0},{5,13},{6,2},{7,15},{8,12},{9,1},{1... | collective-permute-start | bytes 1818632 | tf_op jit(solution)/shard_map/ppermute | solution.py:758
  35.2 5.0 %layer_gradients_1.1 = (f32[1408,256]{1,0:T(8,128)S(1)}, f32[16,256]{1,0:T(8,128)S(1)}, bf16[1152,256]{1,0:T(8,128)(2,1)S(1)}, bf16[1184,256]{1,0:T(8,128)(2,1)S...) custom-call(f32[1408,256]{1,0:T(8,128)S(1)} %get-tuple-element.146.refs_0_, f32[16,256]{1,0:T(8,128)S(1)} %get-tuple-element.147.refs_1_, ...), custom_call_target="tpu_custom_call" | custom-call | flops 5000000000 | bytes 1 | tf_op jit(solution)/shard_map/layer_gradients_1/pallas_call | solution.py:329
  40.2 0.5 halve_3_1.1
  40.7 1.6 %collective-permute-start.4 = (bf16[800,256]{1,0:T(8,128)(2,1)S(1)}, bf16[800,256]{1,0:T(8,128)(2,1)S(1)}, u32[]{:S(2)}, u32[]{:S(2)}) collective-permute-start(bf16[800,256]{1,0:T(8,128)(2,1)S(1)} %get-tuple-element.162), channel_id=1, source_target_pairs={{0,8},{1,3},{2,10},{3,1},{4,12},{5,7},{6,14},{7,5},{8,0},{9,11},{1... | collective-permute-start | bytes 1228808 | tf_op jit(solution)/shard_map/ppermute | solution.py:758
  42.4 4.9 %layer_gradients_0.1 = (f32[1408,128]{1,0:T(8,128)S(1)}, bf16[1408,128]{1,0:T(8,128)(2,1)S(1)}, bf16[1152,256]{1,0:T(8,128)(2,1)S(1)}, bf16[1184,256]{1,0:T(8,12...) custom-call(f32[1408,256]{1,0:T(8,128)S(1)} %get-tuple-element.149.refs_0_, ...), custom_call_target="tpu_custom_call" | custom-call | flops 2000000000 | bytes 1 | tf_op jit(solution)/shard_map/layer_gradients_0/pallas_call | solution.py:329
  47.3 0.2 halve_2_1.1
  47.5 0.5 collective-permute-start.7
  48.0 0.5 collective-permute-start.3
  48.6 0.2 collective-permute-done.4.refs_1_
  48.8 0.2 halve_3_2.1
  48.9 1.1 collective-permute-start.6
  50.0 1.6 %collective-permute-start.11 = (bf16[1184,256]{1,0:T(8,128)(2,1)S(1)}, bf16[1184,256]{1,0:T(8,128)(2,1)S(1)}, u32[]{:S(2)}, u32[]{:S(2)}) collective-permute-start(bf16[1184,256]{1,0:T(8,128)(2,1)S(1)} %get-tuple-element.187), channel_id=1, source_target_pairs={{0,8},{1,3},{2,10},{3,1},{4,12},{5,7},{6,14},{7,5},{8,0},{9,11},{1... | collective-permute-start | bytes 1818632 | tf_op jit(solution)/shard_map/ppermute | solution.py:758
  51.6 5.2 %collective-permute-done.7.refs_1_ = bf16[608,256]{1,0:T(8,128)(2,1)S(1)} collective-permute-done((bf16[608,256]{1,0:T(8,128)(2,1)S(1)}, bf16[608,256]{1,0:T(8,128)(2,1)S(1)}, u32[]{:S(2)}, u32[]{:S(2)}) %collective-permute-start.7) | collective-permute-done | bytes 311328 | tf_op jit(solution)/shard_map/ppermute | solution.py:758
  56.8 0.1 halve_2_2.1
  56.9 0.3 collective-permute-done.6.refs_1_
  57.3 2.7 %collective-permute-start.10 = (bf16[416,256]{1,0:T(8,128)(2,1)S(1)}, bf16[416,256]{1,0:T(8,128)(2,1)S(1)}, u32[]{:S(2)}, u32[]{:S(2)}) collective-permute-start(bf16[416,256]{1,0:T(8,128)(2,1)S(1)} %get-tuple-element.184.refs_0_), channel_id=1, source_target_pairs={{0,16},{1,17},{2,18},{3,19},{4,20},{5,21},{6,22},{7,23},{8,24},{9,... | collective-permute-start | bytes 638984 | tf_op jit(solution)/shard_map/ppermute | solution.py:758
  60.0 4.7 %collective-permute-done.3.refs_1_ = bf16[1184,256]{1,0:T(8,128)(2,1)S(1)} collective-permute-done((bf16[1184,256]{1,0:T(8,128)(2,1)S(1)}, bf16[1184,256]{1,0:T(8,128)(2,1)S(1)}, u32[]{:S(2)}, u32[]{:S(2)}) %collective-permute-start.3) | collective-permute-done | bytes 606240 | tf_op jit(solution)/shard_map/ppermute | solution.py:758
  64.6 0.2 halve_1_1.1
  64.8 1.7 %collective-permute-start.8 = (bf16[608,256]{1,0:T(8,128)(2,1)S(1)}, bf16[608,256]{1,0:T(8,128)(2,1)S(1)}, u32[]{:S(2)}, u32[]{:S(2)}) collective-permute-start(bf16[608,256]{1,0:T(8,128)(2,1)S(1)} %get-tuple-element.179), channel_id=1, source_target_pairs={{0,8},{1,3},{2,10},{3,1},{4,12},{5,7},{6,14},{7,5},{8,0},{9,11},{1... | collective-permute-start | bytes 933896 | tf_op jit(solution)/shard_map/ppermute | solution.py:758
  66.5 0.5 collective-permute-start.9
  67.0 0.8 collective-permute-done.11.refs_1_
  67.8 0.2 halve_0_1.1
  68.0 0.8 collective-permute-start.14
  68.9 1.9 %collective-permute-start.15 = (bf16[416,256]{1,0:T(8,128)(2,1)S(1)}, bf16[416,256]{1,0:T(8,128)(2,1)S(1)}, u32[]{:S(2)}, u32[]{:S(2)}) collective-permute-start(bf16[416,256]{1,0:T(8,128)(2,1)S(1)} %get-tuple-element.201.refs_0_), channel_id=1, source_target_pairs={{0,4},{1,9},{2,6},{3,11},{4,0},{5,13},{6,2},{7,15},{8,12},{9,1},{1... | collective-permute-start | bytes 638984 | tf_op jit(solution)/shard_map/ppermute | solution.py:758
  70.8 1.1 collective-permute-done.9.refs_1_
  71.9 2.7 %collective-permute-start.13 = (bf16[320,256]{1,0:T(8,128)(2,1)S(1)}, bf16[320,256]{1,0:T(8,128)(2,1)S(1)}, u32[]{:S(2)}, u32[]{:S(2)}) collective-permute-start(bf16[320,256]{1,0:T(8,128)(2,1)S(1)} %get-tuple-element.196.refs_0_), channel_id=1, source_target_pairs={{0,16},{1,17},{2,18},{3,19},{4,20},{5,21},{6,22},{7,23},{8,24},{9,... | collective-permute-start | bytes 491528 | tf_op jit(solution)/shard_map/ppermute | solution.py:758
  74.5 0.1 halve_1_2.1
  74.7 1.1 collective-permute-start.12
  75.9 0.1 halve_0_2.1
  76.0 1.1 collective-permute-start.18
  77.1 1.1 collective-permute-start.17
  78.2 3.3 %collective-permute-done.13.refs_1_ = bf16[320,256]{1,0:T(8,128)(2,1)S(1)} collective-permute-done((bf16[320,256]{1,0:T(8,128)(2,1)S(1)}, bf16[320,256]{1,0:T(8,128)(2,1)S(1)}, u32[]{:S(2)}, u32[]{:S(2)}) %collective-permute-start.13) | collective-permute-done | bytes 163872 | tf_op jit(solution)/shard_map/ppermute | solution.py:758
  81.6 0.7 collective-permute-start.21
  82.3 1.1 collective-permute-start.16
  83.4 0.1 collective-permute-done.18.refs_1_
  83.7 4.3 %collective-permute-done.17.refs_1_ = bf16[768,256]{1,0:T(8,128)(2,1)S(1)} collective-permute-done((bf16[768,256]{1,0:T(8,128)(2,1)S(1)}, bf16[768,256]{1,0:T(8,128)(2,1)S(1)}, u32[]{:S(2)}, u32[]{:S(2)}) %collective-permute-start.17) | collective-permute-done | bytes 393248 | tf_op jit(solution)/shard_map/ppermute | solution.py:758
  88.2 3.5 %collective-permute-start.20 = (bf16[320,256]{1,0:T(8,128)(2,1)S(1)}, bf16[320,256]{1,0:T(8,128)(2,1)S(1)}, u32[]{:S(2)}, u32[]{:S(2)}) collective-permute-start(bf16[320,256]{1,0:T(8,128)(2,1)S(1)} %get-tuple-element.216.refs_0_), channel_id=1, source_target_pairs={{0,16},{1,17},{2,18},{3,19},{4,20},{5,21},{6,22},{7,23},{8,24},{9,... | collective-permute-start | bytes 491528 | tf_op jit(solution)/shard_map/ppermute | solution.py:758
  91.8 1.2 collective-permute-start.19
  93.1 1.3 %collective-permute-start.24 = (bf16[576,256]{1,0:T(8,128)(2,1)S(1)}, bf16[576,256]{1,0:T(8,128)(2,1)S(1)}, u32[]{:S(2)}, u32[]{:S(2)}) collective-permute-start(bf16[576,256]{1,0:T(8,128)(2,1)S(1)} %get-tuple-element.227.refs_0_), channel_id=1, source_target_pairs={{0,8},{1,3},{2,10},{3,1},{4,12},{5,7},{6,14},{7,5},{8,0},{9,11},{1... | collective-permute-start | bytes 884744 | tf_op jit(solution)/shard_map/ppermute | solution.py:758
  94.4 4.2 %collective-permute-done.20.refs_1_ = bf16[320,256]{1,0:T(8,128)(2,1)S(1)} collective-permute-done((bf16[320,256]{1,0:T(8,128)(2,1)S(1)}, bf16[320,256]{1,0:T(8,128)(2,1)S(1)}, u32[]{:S(2)}, u32[]{:S(2)}) %collective-permute-start.20) | collective-permute-done | bytes 163872 | tf_op jit(solution)/shard_map/ppermute | solution.py:758
  98.7 1.3 %collective-permute-start.25 = (bf16[320,256]{1,0:T(8,128)(2,1)S(1)}, bf16[320,256]{1,0:T(8,128)(2,1)S(1)}, u32[]{:S(2)}, u32[]{:S(2)}) collective-permute-start(bf16[320,256]{1,0:T(8,128)(2,1)S(1)} %get-tuple-element.228.refs_0_), channel_id=1, source_target_pairs={{0,4},{1,9},{2,6},{3,11},{4,0},{5,13},{6,2},{7,15},{8,12},{9,1},{1... | collective-permute-start | bytes 491528 | tf_op jit(solution)/shard_map/ppermute | solution.py:758
  100.0 0.2 collective-permute-start.22
  100.2 1.1 write_3_own.1
  101.3 2.8 %collective-permute-done.25.refs_1_ = bf16[320,256]{1,0:T(8,128)(2,1)S(1)} collective-permute-done((bf16[320,256]{1,0:T(8,128)(2,1)S(1)}, bf16[320,256]{1,0:T(8,128)(2,1)S(1)}, u32[]{:S(2)}, u32[]{:S(2)}) %collective-permute-start.25) | collective-permute-done | bytes 163872 | tf_op jit(solution)/shard_map/ppermute | solution.py:758
  104.1 1.7 %collective-permute-start.26 = (bf16[576,256]{1,0:T(8,128)(2,1)S(1)}, bf16[576,256]{1,0:T(8,128)(2,1)S(1)}, u32[]{:S(2)}, u32[]{:S(2)}) collective-permute-start(bf16[576,256]{1,0:T(8,128)(2,1)S(1)} %get-tuple-element.235.refs_0_), channel_id=1, source_target_pairs={{0,2},{1,5},{2,0},{3,7},{4,6},{5,1},{6,4},{7,3},{8,10},{9,13},{10,... | collective-permute-start | bytes 884744 | tf_op jit(solution)/shard_map/ppermute | solution.py:758
  105.9 0.9 collective-permute-start.29
  106.7 1.1 write_3_got.1
  108.0 0.9 collective-permute-start.28
  108.9 1.6 %feature_gradient.1 = (bf16[1364,128]{1,0:T(8,128)(2,1)}, f32[8,128]{1,0:T(8,128)S(1)}) custom-call(f32[1408,128]{1,0:T(8,128)S(1)} %get-tuple-element.156.refs_0_, bf16[1408,128]{1,0:T(8,128)(2,1)S(1)} %collective-permute-done.2.refs_1_, f32[1,256]{1,0:T(1,128)} %bitcast.37, f32[8,128]{1,0:T(8,128)S(1)} %get-tuple-element.233.refs_3_), custom_call_target="tpu_custom_call" | custom-call | flops 1000000000 | bytes 1 | tf_op jit(solution)/shard_map/feature_gradient/pallas_call | solution.py:329
  110.5 0.4 collective-permute-done.26.refs_1_
  111.1 1.2 head_gradients.1
  112.3 1.7 %write_0_own.1 = (f32[9216,256]{1,0:T(8,128)}, f32[4,256]{1,0:T(4,128)}, f32[4,256]{1,0:T(4,128)}, f32[8,128]{1,0:T(8,128)S(1)}) custom-call(bf16[1152,256]{1,0:T(8,128)(2,1)S(1)} %get-tuple-element.237.refs_0_, f32[8,256]{1,0:T(8,128)S(1)} %get-tuple-element.240.refs_1_, f32[8,256]{1,0:T(8,128)S(1)} %get-tuple-element.241.refs_2_, ...), custom_call_target="tpu_custom_call", output_to_operand_aliasing={{0}: (5, {})} | custom-call | flops 1500000000 | bytes 1 | tf_op jit(solution)/shard_map/write_0_own/pallas_call | solution.py:329
  113.9 1.1 write_1_own.1
  115.0 1.1 write_2_own.1
  116.1 4.3 %collective-permute-done.29.refs_0_ = bf16[1152,256]{1,0:T(8,128)(2,1)S(1)} collective-permute-done((bf16[1152,256]{1,0:T(8,128)(2,1)S(1)}, bf16[1152,256]{1,0:T(8,128)(2,1)S(1)}, u32[]{:S(2)}, u32[]{:S(2)}) %collective-permute-start.29) | collective-permute-done | bytes 589856 | tf_op jit(solution)/shard_map/ppermute | solution.py:758
  120.4 1.1 write_2_got.1
  121.5 0.5 collective-permute-done.28.refs_0_
  122.0 1.1 write_1_got.1
  123.1 1.1 write_0_got.1
  (37 shorter events, 1.5 us)
Async XLA Ops:
  0.6 2.0 %collective-permute-start = (bf16[1364,128]{1,0:T(8,128)(2,1)}, bf16[1364,128]{1,0:T(8,128)(2,1)S(1)}, u32[]{:S(2)}, u32[]{:S(2)}) collective-permute-start(bf16[1364,128]{1,0:T(8,128)(2,1)} %bitcast.24), channel_id=1, source_target_pairs={{0,1},{1,0},{2,3},{3,2},{4,5},{5,4},{6,7},{7,6},{8,9},{9,8},{10,11... | collective-permute-start | bytes 1047560 | tf_op jit(solution)/shard_map/ppermute | solution.py:860
  25.6 14.6 %collective-permute-start.1 = (bf16[1568,256]{1,0:T(8,128)(2,1)S(1)}, bf16[1568,256]{1,0:T(8,128)(2,1)S(1)}, u32[]{:S(2)}, u32[]{:S(2)}) collective-permute-start(bf16[1568,256]{1,0:T(8,128)(2,1)S(1)} %get-tuple-element.152), channel_id=1, source_target_pairs={{0,2},{1,5},{2,0},{3,7},{4,6},{5,1},{6,4},{7,3},{8,10},{9,13},{10,... | collective-permute-start | bytes 2408456 | tf_op jit(solution)/shard_map/ppermute | solution.py:758
  33.6 13.7 %collective-permute-start.5 = (bf16[1184,256]{1,0:T(8,128)(2,1)S(1)}, bf16[1184,256]{1,0:T(8,128)(2,1)S(1)}, u32[]{:S(2)}, u32[]{:S(2)}) collective-permute-start(bf16[1184,256]{1,0:T(8,128)(2,1)S(1)} %get-tuple-element.165), channel_id=1, source_target_pairs={{0,4},{1,9},{2,6},{3,11},{4,0},{5,13},{6,2},{7,15},{8,12},{9,1},{1... | collective-permute-start | bytes 1818632 | tf_op jit(solution)/shard_map/ppermute | solution.py:758
  40.7 8.0 %collective-permute-start.4 = (bf16[800,256]{1,0:T(8,128)(2,1)S(1)}, bf16[800,256]{1,0:T(8,128)(2,1)S(1)}, u32[]{:S(2)}, u32[]{:S(2)}) collective-permute-start(bf16[800,256]{1,0:T(8,128)(2,1)S(1)} %get-tuple-element.162), channel_id=1, source_target_pairs={{0,8},{1,3},{2,10},{3,1},{4,12},{5,7},{6,14},{7,5},{8,0},{9,11},{1... | collective-permute-start | bytes 1228808 | tf_op jit(solution)/shard_map/ppermute | solution.py:758
  47.5 9.2 %collective-permute-start.7 = (bf16[608,256]{1,0:T(8,128)(2,1)S(1)}, bf16[608,256]{1,0:T(8,128)(2,1)S(1)}, u32[]{:S(2)}, u32[]{:S(2)}) collective-permute-start(bf16[608,256]{1,0:T(8,128)(2,1)S(1)} %get-tuple-element.173), channel_id=1, source_target_pairs={{0,8},{1,3},{2,10},{3,1},{4,12},{5,7},{6,14},{7,5},{8,0},{9,11},{1... | collective-permute-start | bytes 933896 | tf_op jit(solution)/shard_map/ppermute | solution.py:758
  48.0 16.6 %collective-permute-start.3 = (bf16[1184,256]{1,0:T(8,128)(2,1)S(1)}, bf16[1184,256]{1,0:T(8,128)(2,1)S(1)}, u32[]{:S(2)}, u32[]{:S(2)}) collective-permute-start(bf16[1184,256]{1,0:T(8,128)(2,1)S(1)} %get-tuple-element.159), channel_id=1, source_target_pairs={{0,2},{1,5},{2,0},{3,7},{4,6},{5,1},{6,4},{7,3},{8,10},{9,13},{10,... | collective-permute-start | bytes 1818632 | tf_op jit(solution)/shard_map/ppermute | solution.py:758
  48.9 8.3 %collective-permute-start.6 = (bf16[416,256]{1,0:T(8,128)(2,1)S(1)}, bf16[416,256]{1,0:T(8,128)(2,1)S(1)}, u32[]{:S(2)}, u32[]{:S(2)}) collective-permute-start(bf16[416,256]{1,0:T(8,128)(2,1)S(1)} %get-tuple-element.170), channel_id=1, source_target_pairs={{0,4},{1,9},{2,6},{3,11},{4,0},{5,13},{6,2},{7,15},{8,12},{9,1},{1... | collective-permute-start | bytes 638984 | tf_op jit(solution)/shard_map/ppermute | solution.py:758
  50.0 17.8 %collective-permute-start.11 = (bf16[1184,256]{1,0:T(8,128)(2,1)S(1)}, bf16[1184,256]{1,0:T(8,128)(2,1)S(1)}, u32[]{:S(2)}, u32[]{:S(2)}) collective-permute-start(bf16[1184,256]{1,0:T(8,128)(2,1)S(1)} %get-tuple-element.187), channel_id=1, source_target_pairs={{0,8},{1,3},{2,10},{3,1},{4,12},{5,7},{6,14},{7,5},{8,0},{9,11},{1... | collective-permute-start | bytes 1818632 | tf_op jit(solution)/shard_map/ppermute | solution.py:758
  57.3 11.5 %collective-permute-start.10 = (bf16[416,256]{1,0:T(8,128)(2,1)S(1)}, bf16[416,256]{1,0:T(8,128)(2,1)S(1)}, u32[]{:S(2)}, u32[]{:S(2)}) collective-permute-start(bf16[416,256]{1,0:T(8,128)(2,1)S(1)} %get-tuple-element.184.refs_0_), channel_id=1, source_target_pairs={{0,16},{1,17},{2,18},{3,19},{4,20},{5,21},{6,22},{7,23},{8,24},{9,... | collective-permute-start | bytes 638984 | tf_op jit(solution)/shard_map/ppermute | solution.py:758
  64.8 9.7 %collective-permute-start.8 = (bf16[608,256]{1,0:T(8,128)(2,1)S(1)}, bf16[608,256]{1,0:T(8,128)(2,1)S(1)}, u32[]{:S(2)}, u32[]{:S(2)}) collective-permute-start(bf16[608,256]{1,0:T(8,128)(2,1)S(1)} %get-tuple-element.179), channel_id=1, source_target_pairs={{0,8},{1,3},{2,10},{3,1},{4,12},{5,7},{6,14},{7,5},{8,0},{9,11},{1... | collective-permute-start | bytes 933896 | tf_op jit(solution)/shard_map/ppermute | solution.py:758
  66.5 5.3 %collective-permute-start.9 = (bf16[320,256]{1,0:T(8,128)(2,1)S(1)}, bf16[320,256]{1,0:T(8,128)(2,1)S(1)}, u32[]{:S(2)}, u32[]{:S(2)}) collective-permute-start(bf16[320,256]{1,0:T(8,128)(2,1)S(1)} %get-tuple-element.182), channel_id=1, source_target_pairs={{0,2},{1,5},{2,0},{3,7},{4,6},{5,1},{6,4},{7,3},{8,10},{9,13},{10,... | collective-permute-start | bytes 491528 | tf_op jit(solution)/shard_map/ppermute | solution.py:758
  68.0 7.8 %collective-permute-start.14 = (bf16[608,256]{1,0:T(8,128)(2,1)S(1)}, bf16[608,256]{1,0:T(8,128)(2,1)S(1)}, u32[]{:S(2)}, u32[]{:S(2)}) collective-permute-start(bf16[608,256]{1,0:T(8,128)(2,1)S(1)} %get-tuple-element.199), channel_id=1, source_target_pairs={{0,2},{1,5},{2,0},{3,7},{4,6},{5,1},{6,4},{7,3},{8,10},{9,13},{10,... | collective-permute-start | bytes 933896 | tf_op jit(solution)/shard_map/ppermute | solution.py:758
  68.9 6.9 %collective-permute-start.15 = (bf16[416,256]{1,0:T(8,128)(2,1)S(1)}, bf16[416,256]{1,0:T(8,128)(2,1)S(1)}, u32[]{:S(2)}, u32[]{:S(2)}) collective-permute-start(bf16[416,256]{1,0:T(8,128)(2,1)S(1)} %get-tuple-element.201.refs_0_), channel_id=1, source_target_pairs={{0,4},{1,9},{2,6},{3,11},{4,0},{5,13},{6,2},{7,15},{8,12},{9,1},{1... | collective-permute-start | bytes 638984 | tf_op jit(solution)/shard_map/ppermute | solution.py:758
  71.9 9.6 %collective-permute-start.13 = (bf16[320,256]{1,0:T(8,128)(2,1)S(1)}, bf16[320,256]{1,0:T(8,128)(2,1)S(1)}, u32[]{:S(2)}, u32[]{:S(2)}) collective-permute-start(bf16[320,256]{1,0:T(8,128)(2,1)S(1)} %get-tuple-element.196.refs_0_), channel_id=1, source_target_pairs={{0,16},{1,17},{2,18},{3,19},{4,20},{5,21},{6,22},{7,23},{8,24},{9,... | collective-permute-start | bytes 491528 | tf_op jit(solution)/shard_map/ppermute | solution.py:758
  74.7 7.6 %collective-permute-start.12 = (bf16[320,256]{1,0:T(8,128)(2,1)S(1)}, bf16[320,256]{1,0:T(8,128)(2,1)S(1)}, u32[]{:S(2)}, u32[]{:S(2)}) collective-permute-start(bf16[320,256]{1,0:T(8,128)(2,1)S(1)} %get-tuple-element.194), channel_id=1, source_target_pairs={{0,4},{1,9},{2,6},{3,11},{4,0},{5,13},{6,2},{7,15},{8,12},{9,1},{1... | collective-permute-start | bytes 491528 | tf_op jit(solution)/shard_map/ppermute | solution.py:758
  76.0 7.6 %collective-permute-start.18 = (bf16[320,256]{1,0:T(8,128)(2,1)S(1)}, bf16[320,256]{1,0:T(8,128)(2,1)S(1)}, u32[]{:S(2)}, u32[]{:S(2)}) collective-permute-start(bf16[320,256]{1,0:T(8,128)(2,1)S(1)} %get-tuple-element.210), channel_id=1, source_target_pairs={{0,4},{1,9},{2,6},{3,11},{4,0},{5,13},{6,2},{7,15},{8,12},{9,1},{1... | collective-permute-start | bytes 491528 | tf_op jit(solution)/shard_map/ppermute | solution.py:758
  77.1 10.9 %collective-permute-start.17 = (bf16[768,256]{1,0:T(8,128)(2,1)S(1)}, bf16[768,256]{1,0:T(8,128)(2,1)S(1)}, u32[]{:S(2)}, u32[]{:S(2)}) collective-permute-start(bf16[768,256]{1,0:T(8,128)(2,1)S(1)} %get-tuple-element.208.refs_0_), channel_id=1, source_target_pairs={{0,8},{1,3},{2,10},{3,1},{4,12},{5,7},{6,14},{7,5},{8,0},{9,11},{1... | collective-permute-start | bytes 1179656 | tf_op jit(solution)/shard_map/ppermute | solution.py:758
  81.6 11.4 %collective-permute-start.21 = (bf16[320,256]{1,0:T(8,128)(2,1)S(1)}, bf16[320,256]{1,0:T(8,128)(2,1)S(1)}, u32[]{:S(2)}, u32[]{:S(2)}) collective-permute-start(bf16[320,256]{1,0:T(8,128)(2,1)S(1)} %get-tuple-element.218.refs_0_), channel_id=1, source_target_pairs={{0,2},{1,5},{2,0},{3,7},{4,6},{5,1},{6,4},{7,3},{8,10},{9,13},{10,... | collective-permute-start | bytes 491528 | tf_op jit(solution)/shard_map/ppermute | solution.py:758
  82.3 9.4 %collective-permute-start.16 = (bf16[320,256]{1,0:T(8,128)(2,1)S(1)}, bf16[320,256]{1,0:T(8,128)(2,1)S(1)}, u32[]{:S(2)}, u32[]{:S(2)}) collective-permute-start(bf16[320,256]{1,0:T(8,128)(2,1)S(1)} %get-tuple-element.206.refs_0_), channel_id=1, source_target_pairs={{0,16},{1,17},{2,18},{3,19},{4,20},{5,21},{6,22},{7,23},{8,24},{9,... | collective-permute-start | bytes 491528 | tf_op jit(solution)/shard_map/ppermute | solution.py:758
  88.1 18.6 %collective-permute-start.23 = (bf16[1536,256]{1,0:T(8,128)(2,1)S(1)}, bf16[1536,256]{1,0:T(8,128)(2,1)S(1)}, u32[]{:S(2)}, u32[]{:S(2)}) collective-permute-start(bf16[1536,256]{1,0:T(8,128)(2,1)S(1)} %get-tuple-element.223.refs_0_.refs_1_), channel_id=1, source_target_pairs={{0,2},{1,5},{2,0},{3,7},{4,6},{5,1},{6,4},{7,3},{8,10},{9,13},{10,... | collective-permute-start | bytes 2359304 | tf_op jit(solution)/shard_map/ppermute | solution.py:758
  88.2 10.4 %collective-permute-start.20 = (bf16[320,256]{1,0:T(8,128)(2,1)S(1)}, bf16[320,256]{1,0:T(8,128)(2,1)S(1)}, u32[]{:S(2)}, u32[]{:S(2)}) collective-permute-start(bf16[320,256]{1,0:T(8,128)(2,1)S(1)} %get-tuple-element.216.refs_0_), channel_id=1, source_target_pairs={{0,16},{1,17},{2,18},{3,19},{4,20},{5,21},{6,22},{7,23},{8,24},{9,... | collective-permute-start | bytes 491528 | tf_op jit(solution)/shard_map/ppermute | solution.py:758
  91.8 8.2 %collective-permute-start.19 = (bf16[320,256]{1,0:T(8,128)(2,1)S(1)}, bf16[320,256]{1,0:T(8,128)(2,1)S(1)}, u32[]{:S(2)}, u32[]{:S(2)}) collective-permute-start(bf16[320,256]{1,0:T(8,128)(2,1)S(1)} %get-tuple-element.215.refs_0_), channel_id=1, source_target_pairs={{0,4},{1,9},{2,6},{3,11},{4,0},{5,13},{6,2},{7,15},{8,12},{9,1},{1... | collective-permute-start | bytes 491528 | tf_op jit(solution)/shard_map/ppermute | solution.py:758
  93.1 12.7 %collective-permute-start.24 = (bf16[576,256]{1,0:T(8,128)(2,1)S(1)}, bf16[576,256]{1,0:T(8,128)(2,1)S(1)}, u32[]{:S(2)}, u32[]{:S(2)}) collective-permute-start(bf16[576,256]{1,0:T(8,128)(2,1)S(1)} %get-tuple-element.227.refs_0_), channel_id=1, source_target_pairs={{0,8},{1,3},{2,10},{3,1},{4,12},{5,7},{6,14},{7,5},{8,0},{9,11},{1... | collective-permute-start | bytes 884744 | tf_op jit(solution)/shard_map/ppermute | solution.py:758
  98.7 5.4 %collective-permute-start.25 = (bf16[320,256]{1,0:T(8,128)(2,1)S(1)}, bf16[320,256]{1,0:T(8,128)(2,1)S(1)}, u32[]{:S(2)}, u32[]{:S(2)}) collective-permute-start(bf16[320,256]{1,0:T(8,128)(2,1)S(1)} %get-tuple-element.228.refs_0_), channel_id=1, source_target_pairs={{0,4},{1,9},{2,6},{3,11},{4,0},{5,13},{6,2},{7,15},{8,12},{9,1},{1... | collective-permute-start | bytes 491528 | tf_op jit(solution)/shard_map/ppermute | solution.py:758
  100.0 7.9 %collective-permute-start.22 = (bf16[576,256]{1,0:T(8,128)(2,1)S(1)}, bf16[576,256]{1,0:T(8,128)(2,1)S(1)}, u32[]{:S(2)}, u32[]{:S(2)}) collective-permute-start(bf16[576,256]{1,0:T(8,128)(2,1)S(1)} %get-tuple-element.222.refs_0_), channel_id=1, source_target_pairs={{0,8},{1,3},{2,10},{3,1},{4,12},{5,7},{6,14},{7,5},{8,0},{9,11},{1... | collective-permute-start | bytes 884744 | tf_op jit(solution)/shard_map/ppermute | solution.py:758
  100.2 8.7 %collective-permute-start.2 = (bf16[1408,128]{1,0:T(8,128)(2,1)S(1)}, bf16[1408,128]{1,0:T(8,128)(2,1)S(1)}, u32[]{:S(2)}, u32[]{:S(2)}) collective-permute-start(bf16[1408,128]{1,0:T(8,128)(2,1)S(1)} %get-tuple-element.157), channel_id=1, source_target_pairs={{0,1},{1,0},{2,3},{3,2},{4,5},{5,4},{6,7},{7,6},{8,9},{9,8},{10,11... | collective-permute-start | bytes 1081352 | tf_op jit(solution)/shard_map/ppermute | solution.py:894
  104.1 6.8 %collective-permute-start.26 = (bf16[576,256]{1,0:T(8,128)(2,1)S(1)}, bf16[576,256]{1,0:T(8,128)(2,1)S(1)}, u32[]{:S(2)}, u32[]{:S(2)}) collective-permute-start(bf16[576,256]{1,0:T(8,128)(2,1)S(1)} %get-tuple-element.235.refs_0_), channel_id=1, source_target_pairs={{0,2},{1,5},{2,0},{3,7},{4,6},{5,1},{6,4},{7,3},{8,10},{9,13},{10,... | collective-permute-start | bytes 884744 | tf_op jit(solution)/shard_map/ppermute | solution.py:758
  105.9 14.6 %collective-permute-start.29 = (bf16[1152,256]{1,0:T(8,128)(2,1)S(1)}, bf16[1152,256]{1,0:T(8,128)(2,1)S(1)}, u32[]{:S(2)}, u32[]{:S(2)}) collective-permute-start(bf16[1152,256]{1,0:T(8,128)(2,1)S(1)} %get-tuple-element.239.refs_0_), channel_id=1, source_target_pairs={{0,4},{1,9},{2,6},{3,11},{4,0},{5,13},{6,2},{7,15},{8,12},{9,1},{1... | collective-permute-start | bytes 1769480 | tf_op jit(solution)/shard_map/ppermute | solution.py:758
  107.8 3.2 %collective-permute-start.30 = (bf16[800,256]{1,0:T(8,128)(2,1)S(1)}, bf16[800,256]{1,0:T(8,128)(2,1)S(1)}, u32[]{:S(2)}, u32[]{:S(2)}) collective-permute-start(bf16[800,256]{1,0:T(8,128)(2,1)S(1)} %get-tuple-element.244.refs_0_), channel_id=1, source_target_pairs={{0,1},{1,0},{2,3},{3,2},{4,5},{5,4},{6,7},{7,6},{8,9},{9,8},{10,11... | collective-permute-start | bytes 1228808 | tf_op jit(solution)/shard_map/ppermute | solution.py:906
  108.0 14.0 %collective-permute-start.28 = (bf16[1152,256]{1,0:T(8,128)(2,1)S(1)}, bf16[1152,256]{1,0:T(8,128)(2,1)S(1)}, u32[]{:S(2)}, u32[]{:S(2)}) collective-permute-start(bf16[1152,256]{1,0:T(8,128)(2,1)S(1)} %get-tuple-element.238.refs_0_), channel_id=1, source_target_pairs={{0,2},{1,5},{2,0},{3,7},{4,6},{5,1},{6,4},{7,3},{8,10},{9,13},{10,... | collective-permute-start | bytes 1769480 | tf_op jit(solution)/shard_map/ppermute | solution.py:758
  111.0 12.1 %collective-permute-start.27 = (bf16[1152,256]{1,0:T(8,128)(2,1)S(1)}, bf16[1152,256]{1,0:T(8,128)(2,1)S(1)}, u32[]{:S(2)}, u32[]{:S(2)}) collective-permute-start(bf16[1152,256]{1,0:T(8,128)(2,1)S(1)} %get-tuple-element.237.refs_0_), channel_id=1, source_target_pairs={{0,8},{1,3},{2,10},{3,1},{4,12},{5,7},{6,14},{7,5},{8,0},{9,11},{1... | collective-permute-start | bytes 1769480 | tf_op jit(solution)/shard_map/ppermute | solution.py:758

commit v6 on v5

--- a/solution.py
+++ b/solution.py
@@ -422,6 +422,16 @@
             rest[pl.ds(pl.multiple_of(t * C + bit * half, half), half), :] = own[(9 + t) * half : (10 + t) * half, :]
             rest[pl.ds(pl.multiple_of(t * C + (1 - bit) * half, half), half), :] = got[(9 + t) * half : (10 + t) * half, :]
         rest[extra * C :, :] = pack(vec[...])
+    for copy in copies:
+        copy.wait()
+
+
+def write_last_kernel(layers, orders, *refs):
+    n = len(layers)
+    out, wides, sems = refs[n + 1], refs[n + 2 : 2 * n + 2], refs[-1]
+    copies = []
+    for k, layer in enumerate(layers):
+        copies += write_half(layer, 1 - bit_of(orders[k], 0), refs[k], out, wides[k], sems.at[k])
     for copy in copies:
         copy.wait()
 
@@ -899,11 +909,16 @@
             (out, *more), token = sums[l].finish(token, out, True, [one.vec for one in sums])
             if l == 0:
                 dgain, dshift = more
-        else:
-            (out, *more), token = sums[l].finish(token, out, False, None)
-            if l == 3:
-                (heads,) = more
-                got_heads = lax.ppermute(heads, "tower", swap)
+        elif l == 3:
+            (out, heads), token = sums[l].finish(token, out, False, None)
+            got_heads = lax.ppermute(heads, "tower", swap)
+        elif l == 0:
+            last = (2, 1, 0)
+            (out,), token = call(
+                functools.partial(write_last_kernel, last, [order[k] for k in last]), token,
+                [sums[k].got for k in last] + [out], [VMEM] * 3 + [HBM], [shape((LAYERS * 9 * C, C), f32)], [HBM],
+                "write_0_got", [pltpu.VMEM((9 * C // 2, C), f32)] * 3 + [pltpu.SemaphoreType.DMA((3, 9))], 24, {3: 0},
+            )
     return (
         feature_grad[None],
         out.reshape(1, LAYERS, 3, 3, C, C),

time: 125 us -> 128 us (1.024)
  waiting for transfers between devices: 32.1 us -> 36.2 us
    ppermute x28, waiting for transfers between devices: 32.1 us -> 36.2 us  [partner(): return lax.ppermute(value, ('dp', 'tower'), pairs)]
    pallas_call x39 -> x37, Pallas kernels: 54.3 us -> 53.1 us  [call(): pl.pallas_call(ordered, out_shape=list(outs) + [shape((8, LANES), f32)],...]
  transfers between devices with their start and end apart: 31 -> 31, of which waited for: 14 -> 14; matrix products, arithmetic and copies ran while one was open for 0% -> 0% of each run, Pallas kernels for 24% -> 22%
where the time goes in v6:
time: 128 us
  Pallas kernels  53.1 us (41%)
  starting transfers between devices  37.5 us (29%)
  waiting for transfers between devices  36.2 us (28%)
    pallas_call x37, Pallas kernels, call(): pl.pallas_call(ordered, out_shape=list(outs) + [shape((8, LANES), f32)],...  53.1 us
    ppermute x28, starting transfers between devices, partner(): return lax.ppermute(value, ('dp', 'tower'), pairs)  36.9 us
    ppermute x28, waiting for transfers between devices, partner(): return lax.ppermute(value, ('dp', 'tower'), pairs)  36.2 us
  transfers between devices with their start and end apart: 31, of which 14 were waited for; matrix products, arithmetic and copies ran while one was open for 0% of the time, Pallas kernels for 22%

profile of v6, /device:TPU:0, one launch (start us, length us, event | category | flops | bytes accessed | tf_op | source)
XLA Modules:
  0.0 128.0 jit_solution(521276922900141450)
XLA Ops:
  0.6 0.5 collective-permute-start
  1.2 1.5 %prepare.1 = (bf16[768,256]{1,0:T(8,128)(2,1)S(1)}, bf16[1152,256]{1,0:T(8,128)(2,1)S(1)}, f32[1408,128]{1,0:T(8,128)S(1)}, f32[8,128]{1,0:T(8,128)S(1)}) custom-call(bf16[3,3,85,256]{3,2,1,0:T(8,128)(2,1)} %bitcast.40, bf16[80,1364]{1,0:T(8,128)(2,1)} %bitcast.41, bf16[5,1364]{1,0:T(8,128)(2,1)} %bitcast.42, s32[1,1364]{1,0:T(1,128)} %refs_3_.1, ...), custom_call_target="tpu_custom_call" | custom-call | flops 1500000000 | bytes 1 | tf_op jit(solution)/shard_map/prepare/pallas_call | solution.py:329
  2.7 23.0 %forward_and_heads.1 = (bf16[4,2304,256]{2,1,0:T(8,128)(2,1)S(1)}, f32[3,1408,256]{2,1,0:T(8,128)S(1)}, bf16[3,1408,256]{2,1,0:T(8,128)(2,1)S(1)}, f32[3,16,256]...) custom-call(f32[1,5]{1,0:T(1,128)} %bitcast.38, ...), custom_call_target="tpu_custom_call" | custom-call | flops 1500000000 | bytes 1 | tf_op jit(solution)/shard_map/forward_and_heads/pallas_call | solution.py:329
  25.6 2.9 %collective-permute-start.1 = (bf16[1568,256]{1,0:T(8,128)(2,1)S(1)}, bf16[1568,256]{1,0:T(8,128)(2,1)S(1)}, u32[]{:S(2)}, u32[]{:S(2)}) collective-permute-start(bf16[1568,256]{1,0:T(8,128)(2,1)S(1)} %get-tuple-element.148), channel_id=1, source_target_pairs={{0,2},{1,5},{2,0},{3,7},{4,6},{5,1},{6,4},{7,3},{8,10},{9,13},{10,... | collective-permute-start | bytes 2408456 | tf_op jit(solution)/shard_map/ppermute | solution.py:768
  28.5 5.0 %layer_gradients_2.1 = (f32[1408,256]{1,0:T(8,128)S(1)}, f32[16,256]{1,0:T(8,128)S(1)}, bf16[1152,256]{1,0:T(8,128)(2,1)S(1)}, bf16[1184,256]{1,0:T(8,128)(2,1)S...) custom-call(f32[1408,256]{1,0:T(8,128)S(1)} %get-tuple-element.135.refs_0_, f32[16,256]{1,0:T(8,128)S(1)} %get-tuple-element.136.refs_1_, ...), custom_call_target="tpu_custom_call" | custom-call | flops 3000000000 | bytes 1 | tf_op jit(solution)/shard_map/layer_gradients_2/pallas_call | solution.py:329
  33.6 1.6 %collective-permute-start.5 = (bf16[1184,256]{1,0:T(8,128)(2,1)S(1)}, bf16[1184,256]{1,0:T(8,128)(2,1)S(1)}, u32[]{:S(2)}, u32[]{:S(2)}) collective-permute-start(bf16[1184,256]{1,0:T(8,128)(2,1)S(1)} %get-tuple-element.161), channel_id=1, source_target_pairs={{0,4},{1,9},{2,6},{3,11},{4,0},{5,13},{6,2},{7,15},{8,12},{9,1},{1... | collective-permute-start | bytes 1818632 | tf_op jit(solution)/shard_map/ppermute | solution.py:768
  35.2 5.0 %layer_gradients_1.1 = (f32[1408,256]{1,0:T(8,128)S(1)}, f32[16,256]{1,0:T(8,128)S(1)}, bf16[1152,256]{1,0:T(8,128)(2,1)S(1)}, bf16[1184,256]{1,0:T(8,128)(2,1)S...) custom-call(f32[1408,256]{1,0:T(8,128)S(1)} %get-tuple-element.142.refs_0_, f32[16,256]{1,0:T(8,128)S(1)} %get-tuple-element.143.refs_1_, ...), custom_call_target="tpu_custom_call" | custom-call | flops 5000000000 | bytes 1 | tf_op jit(solution)/shard_map/layer_gradients_1/pallas_call | solution.py:329
  40.2 0.5 halve_3_1.1
  40.7 1.6 %collective-permute-start.4 = (bf16[800,256]{1,0:T(8,128)(2,1)S(1)}, bf16[800,256]{1,0:T(8,128)(2,1)S(1)}, u32[]{:S(2)}, u32[]{:S(2)}) collective-permute-start(bf16[800,256]{1,0:T(8,128)(2,1)S(1)} %get-tuple-element.158), channel_id=1, source_target_pairs={{0,8},{1,3},{2,10},{3,1},{4,12},{5,7},{6,14},{7,5},{8,0},{9,11},{1... | collective-permute-start | bytes 1228808 | tf_op jit(solution)/shard_map/ppermute | solution.py:768
  42.4 4.9 %layer_gradients_0.1 = (f32[1408,128]{1,0:T(8,128)S(1)}, bf16[1408,128]{1,0:T(8,128)(2,1)S(1)}, bf16[1152,256]{1,0:T(8,128)(2,1)S(1)}, bf16[1184,256]{1,0:T(8,12...) custom-call(f32[1408,256]{1,0:T(8,128)S(1)} %get-tuple-element.145.refs_0_, ...), custom_call_target="tpu_custom_call" | custom-call | flops 2000000000 | bytes 1 | tf_op jit(solution)/shard_map/layer_gradients_0/pallas_call | solution.py:329
  47.3 0.2 halve_2_1.1
  47.5 0.5 collective-permute-start.7
  48.0 0.5 collective-permute-start.3
  48.6 0.2 collective-permute-done.4.refs_1_
  48.8 0.2 halve_3_2.1
  48.9 1.1 collective-permute-start.6
  50.0 1.6 %collective-permute-start.11 = (bf16[1184,256]{1,0:T(8,128)(2,1)S(1)}, bf16[1184,256]{1,0:T(8,128)(2,1)S(1)}, u32[]{:S(2)}, u32[]{:S(2)}) collective-permute-start(bf16[1184,256]{1,0:T(8,128)(2,1)S(1)} %get-tuple-element.183), channel_id=1, source_target_pairs={{0,8},{1,3},{2,10},{3,1},{4,12},{5,7},{6,14},{7,5},{8,0},{9,11},{1... | collective-permute-start | bytes 1818632 | tf_op jit(solution)/shard_map/ppermute | solution.py:768
  51.6 5.2 %collective-permute-done.7.refs_1_ = bf16[608,256]{1,0:T(8,128)(2,1)S(1)} collective-permute-done((bf16[608,256]{1,0:T(8,128)(2,1)S(1)}, bf16[608,256]{1,0:T(8,128)(2,1)S(1)}, u32[]{:S(2)}, u32[]{:S(2)}) %collective-permute-start.7) | collective-permute-done | bytes 311328 | tf_op jit(solution)/shard_map/ppermute | solution.py:768
  56.8 0.1 halve_2_2.1
  56.9 0.3 collective-permute-done.6.refs_1_
  57.2 0.1 add_3_3.1
  57.3 2.7 %collective-permute-start.10 = (bf16[416,256]{1,0:T(8,128)(2,1)S(1)}, bf16[416,256]{1,0:T(8,128)(2,1)S(1)}, u32[]{:S(2)}, u32[]{:S(2)}) collective-permute-start(bf16[416,256]{1,0:T(8,128)(2,1)S(1)} %get-tuple-element.180.refs_0_), channel_id=1, source_target_pairs={{0,16},{1,17},{2,18},{3,19},{4,20},{5,21},{6,22},{7,23},{8,24},{9,... | collective-permute-start | bytes 638984 | tf_op jit(solution)/shard_map/ppermute | solution.py:768
  60.0 4.7 %collective-permute-done.3.refs_1_ = bf16[1184,256]{1,0:T(8,128)(2,1)S(1)} collective-permute-done((bf16[1184,256]{1,0:T(8,128)(2,1)S(1)}, bf16[1184,256]{1,0:T(8,128)(2,1)S(1)}, u32[]{:S(2)}, u32[]{:S(2)}) %collective-permute-start.3) | collective-permute-done | bytes 606240 | tf_op jit(solution)/shard_map/ppermute | solution.py:768
  64.6 0.2 halve_1_1.1
  64.8 1.7 %collective-permute-start.8 = (bf16[608,256]{1,0:T(8,128)(2,1)S(1)}, bf16[608,256]{1,0:T(8,128)(2,1)S(1)}, u32[]{:S(2)}, u32[]{:S(2)}) collective-permute-start(bf16[608,256]{1,0:T(8,128)(2,1)S(1)} %get-tuple-element.175), channel_id=1, source_target_pairs={{0,8},{1,3},{2,10},{3,1},{4,12},{5,7},{6,14},{7,5},{8,0},{9,11},{1... | collective-permute-start | bytes 933896 | tf_op jit(solution)/shard_map/ppermute | solution.py:768
  66.5 0.5 collective-permute-start.9
  67.0 0.8 collective-permute-done.11.refs_1_
  67.8 0.2 halve_0_1.1
  68.0 0.8 collective-permute-start.14
  68.8 0.1 add_3_4.1
  68.9 1.9 %collective-permute-start.15 = (bf16[416,256]{1,0:T(8,128)(2,1)S(1)}, bf16[416,256]{1,0:T(8,128)(2,1)S(1)}, u32[]{:S(2)}, u32[]{:S(2)}) collective-permute-start(bf16[416,256]{1,0:T(8,128)(2,1)S(1)} %get-tuple-element.197.refs_0_), channel_id=1, source_target_pairs={{0,4},{1,9},{2,6},{3,11},{4,0},{5,13},{6,2},{7,15},{8,12},{9,1},{1... | collective-permute-start | bytes 638984 | tf_op jit(solution)/shard_map/ppermute | solution.py:768
  70.8 1.1 collective-permute-done.9.refs_1_
  71.9 2.7 %collective-permute-start.13 = (bf16[320,256]{1,0:T(8,128)(2,1)S(1)}, bf16[320,256]{1,0:T(8,128)(2,1)S(1)}, u32[]{:S(2)}, u32[]{:S(2)}) collective-permute-start(bf16[320,256]{1,0:T(8,128)(2,1)S(1)} %get-tuple-element.192.refs_0_), channel_id=1, source_target_pairs={{0,16},{1,17},{2,18},{3,19},{4,20},{5,21},{6,22},{7,23},{8,24},{9,... | collective-permute-start | bytes 491528 | tf_op jit(solution)/shard_map/ppermute | solution.py:768
  74.5 0.1 halve_1_2.1
  74.7 1.1 collective-permute-start.12
  75.9 0.1 halve_0_2.1
  76.0 1.1 collective-permute-start.18
  77.1 1.1 collective-permute-start.17
  78.2 3.3 %collective-permute-done.13.refs_1_ = bf16[320,256]{1,0:T(8,128)(2,1)S(1)} collective-permute-done((bf16[320,256]{1,0:T(8,128)(2,1)S(1)}, bf16[320,256]{1,0:T(8,128)(2,1)S(1)}, u32[]{:S(2)}, u32[]{:S(2)}) %collective-permute-start.13) | collective-permute-done | bytes 163872 | tf_op jit(solution)/shard_map/ppermute | solution.py:768
  81.6 0.7 collective-permute-start.21
  82.3 1.1 collective-permute-start.16
  83.4 0.1 collective-permute-done.18.refs_1_
  83.7 4.3 %collective-permute-done.17.refs_1_ = bf16[768,256]{1,0:T(8,128)(2,1)S(1)} collective-permute-done((bf16[768,256]{1,0:T(8,128)(2,1)S(1)}, bf16[768,256]{1,0:T(8,128)(2,1)S(1)}, u32[]{:S(2)}, u32[]{:S(2)}) %collective-permute-start.17) | collective-permute-done | bytes 393248 | tf_op jit(solution)/shard_map/ppermute | solution.py:768
  88.2 3.5 %collective-permute-start.20 = (bf16[320,256]{1,0:T(8,128)(2,1)S(1)}, bf16[320,256]{1,0:T(8,128)(2,1)S(1)}, u32[]{:S(2)}, u32[]{:S(2)}) collective-permute-start(bf16[320,256]{1,0:T(8,128)(2,1)S(1)} %get-tuple-element.212.refs_0_), channel_id=1, source_target_pairs={{0,16},{1,17},{2,18},{3,19},{4,20},{5,21},{6,22},{7,23},{8,24},{9,... | collective-permute-start | bytes 491528 | tf_op jit(solution)/shard_map/ppermute | solution.py:768
  91.8 1.2 collective-permute-start.19
  93.1 1.3 %collective-permute-start.24 = (bf16[576,256]{1,0:T(8,128)(2,1)S(1)}, bf16[576,256]{1,0:T(8,128)(2,1)S(1)}, u32[]{:S(2)}, u32[]{:S(2)}) collective-permute-start(bf16[576,256]{1,0:T(8,128)(2,1)S(1)} %get-tuple-element.223.refs_0_), channel_id=1, source_target_pairs={{0,8},{1,3},{2,10},{3,1},{4,12},{5,7},{6,14},{7,5},{8,0},{9,11},{1... | collective-permute-start | bytes 884744 | tf_op jit(solution)/shard_map/ppermute | solution.py:768
  94.4 4.2 %collective-permute-done.20.refs_1_ = bf16[320,256]{1,0:T(8,128)(2,1)S(1)} collective-permute-done((bf16[320,256]{1,0:T(8,128)(2,1)S(1)}, bf16[320,256]{1,0:T(8,128)(2,1)S(1)}, u32[]{:S(2)}, u32[]{:S(2)}) %collective-permute-start.20) | collective-permute-done | bytes 163872 | tf_op jit(solution)/shard_map/ppermute | solution.py:768
  98.7 1.3 %collective-permute-start.25 = (bf16[320,256]{1,0:T(8,128)(2,1)S(1)}, bf16[320,256]{1,0:T(8,128)(2,1)S(1)}, u32[]{:S(2)}, u32[]{:S(2)}) collective-permute-start(bf16[320,256]{1,0:T(8,128)(2,1)S(1)} %get-tuple-element.224.refs_0_), channel_id=1, source_target_pairs={{0,4},{1,9},{2,6},{3,11},{4,0},{5,13},{6,2},{7,15},{8,12},{9,1},{1... | collective-permute-start | bytes 491528 | tf_op jit(solution)/shard_map/ppermute | solution.py:768
  100.0 0.2 collective-permute-start.22
  100.2 1.1 write_3_own.1
  101.3 2.8 %collective-permute-done.25.refs_1_ = bf16[320,256]{1,0:T(8,128)(2,1)S(1)} collective-permute-done((bf16[320,256]{1,0:T(8,128)(2,1)S(1)}, bf16[320,256]{1,0:T(8,128)(2,1)S(1)}, u32[]{:S(2)}, u32[]{:S(2)}) %collective-permute-start.25) | collective-permute-done | bytes 163872 | tf_op jit(solution)/shard_map/ppermute | solution.py:768
  104.1 1.7 %collective-permute-start.28 = (bf16[576,256]{1,0:T(8,128)(2,1)S(1)}, bf16[576,256]{1,0:T(8,128)(2,1)S(1)}, u32[]{:S(2)}, u32[]{:S(2)}) collective-permute-start(bf16[576,256]{1,0:T(8,128)(2,1)S(1)} %get-tuple-element.233.refs_0_), channel_id=1, source_target_pairs={{0,2},{1,5},{2,0},{3,7},{4,6},{5,1},{6,4},{7,3},{8,10},{9,13},{10,... | collective-permute-start | bytes 884744 | tf_op jit(solution)/shard_map/ppermute | solution.py:768
  105.9 0.9 collective-permute-start.26
  106.7 1.1 write_3_got.1
  108.0 1.6 %feature_gradient.1 = (bf16[1364,128]{1,0:T(8,128)(2,1)}, f32[8,128]{1,0:T(8,128)S(1)}) custom-call(f32[1408,128]{1,0:T(8,128)S(1)} %get-tuple-element.152.refs_0_, bf16[1408,128]{1,0:T(8,128)(2,1)S(1)} %collective-permute-done.2.refs_1_, f32[1,256]{1,0:T(1,128)} %bitcast.37, f32[8,128]{1,0:T(8,128)S(1)} %get-tuple-element.229.refs_3_), custom_call_target="tpu_custom_call" | custom-call | flops 1000000000 | bytes 1 | tf_op jit(solution)/shard_map/feature_gradient/pallas_call | solution.py:329
  109.6 1.3 %collective-permute-done.28.refs_1_ = bf16[576,256]{1,0:T(8,128)(2,1)S(1)} collective-permute-done((bf16[576,256]{1,0:T(8,128)(2,1)S(1)}, bf16[576,256]{1,0:T(8,128)(2,1)S(1)}, u32[]{:S(2)}, u32[]{:S(2)}) %collective-permute-start.28) | collective-permute-done | bytes 294944 | tf_op jit(solution)/shard_map/ppermute | solution.py:768
  111.1 1.7 %collective-permute-start.27 = (bf16[1152,256]{1,0:T(8,128)(2,1)S(1)}, bf16[1152,256]{1,0:T(8,128)(2,1)S(1)}, u32[]{:S(2)}, u32[]{:S(2)}) collective-permute-start(bf16[1152,256]{1,0:T(8,128)(2,1)S(1)} %get-tuple-element.232.refs_0_), channel_id=1, source_target_pairs={{0,2},{1,5},{2,0},{3,7},{4,6},{5,1},{6,4},{7,3},{8,10},{9,13},{10,... | collective-permute-start | bytes 1769480 | tf_op jit(solution)/shard_map/ppermute | solution.py:768
  112.7 1.2 head_gradients.1
  113.9 1.7 %write_0_own.1 = (f32[9216,256]{1,0:T(8,128)}, f32[4,256]{1,0:T(4,128)}, f32[4,256]{1,0:T(4,128)}, f32[8,128]{1,0:T(8,128)S(1)}) custom-call(bf16[1152,256]{1,0:T(8,128)(2,1)S(1)} %get-tuple-element.235.refs_0_, f32[8,256]{1,0:T(8,128)S(1)} %get-tuple-element.236.refs_1_, f32[8,256]{1,0:T(8,128)S(1)} %get-tuple-element.237.refs_2_, ...), custom_call_target="tpu_custom_call", output_to_operand_aliasing={{0}: (5, {})} | custom-call | flops 1500000000 | bytes 1 | tf_op jit(solution)/shard_map/write_0_own/pallas_call | solution.py:329
  115.6 1.1 write_1_own.1
  116.7 1.1 write_2_own.1
  117.8 3.1 %collective-permute-done.29.refs_2_ = bf16[1152,256]{1,0:T(8,128)(2,1)S(1)} collective-permute-done((bf16[1152,256]{1,0:T(8,128)(2,1)S(1)}, bf16[1152,256]{1,0:T(8,128)(2,1)S(1)}, u32[]{:S(2)}, u32[]{:S(2)}) %collective-permute-start.29) | collective-permute-done | bytes 589856 | tf_op jit(solution)/shard_map/ppermute | solution.py:768
  120.9 4.9 %collective-permute-done.27.refs_1_ = bf16[1152,256]{1,0:T(8,128)(2,1)S(1)} collective-permute-done((bf16[1152,256]{1,0:T(8,128)(2,1)S(1)}, bf16[1152,256]{1,0:T(8,128)(2,1)S(1)}, u32[]{:S(2)}, u32[]{:S(2)}) %collective-permute-start.27) | collective-permute-done | bytes 589856 | tf_op jit(solution)/shard_map/ppermute | solution.py:768
  125.8 2.0 %write_0_got.1 = (f32[9216,256]{1,0:T(8,128)}, f32[8,128]{1,0:T(8,128)}) custom-call(bf16[1152,256]{1,0:T(8,128)(2,1)S(1)} %collective-permute-done.26.refs_0_, bf16[1152,256]{1,0:T(8,128)(2,1)S(1)} %collective-permute-done.27.refs_1_, bf16[1152,256]{1,0:T(8,128)(2,1)S(1)} %collective-permute-done.29.refs_2_, ...), custom_call_target="tpu_custom_call", output_to_operand_aliasing={{0}: (3, {})} | custom-call | flops 3000000000 | bytes 1 | tf_op jit(solution)/shard_map/write_0_got/pallas_call | solution.py:329
  (35 shorter events, 1.3 us)
Async XLA Ops:
  0.6 2.0 %collective-permute-start = (bf16[1364,128]{1,0:T(8,128)(2,1)}, bf16[1364,128]{1,0:T(8,128)(2,1)S(1)}, u32[]{:S(2)}, u32[]{:S(2)}) collective-permute-start(bf16[1364,128]{1,0:T(8,128)(2,1)} %bitcast.24), channel_id=1, source_target_pairs={{0,1},{1,0},{2,3},{3,2},{4,5},{5,4},{6,7},{7,6},{8,9},{9,8},{10,11... | collective-permute-start | bytes 1047560 | tf_op jit(solution)/shard_map/ppermute | solution.py:870
  25.6 14.6 %collective-permute-start.1 = (bf16[1568,256]{1,0:T(8,128)(2,1)S(1)}, bf16[1568,256]{1,0:T(8,128)(2,1)S(1)}, u32[]{:S(2)}, u32[]{:S(2)}) collective-permute-start(bf16[1568,256]{1,0:T(8,128)(2,1)S(1)} %get-tuple-element.148), channel_id=1, source_target_pairs={{0,2},{1,5},{2,0},{3,7},{4,6},{5,1},{6,4},{7,3},{8,10},{9,13},{10,... | collective-permute-start | bytes 2408456 | tf_op jit(solution)/shard_map/ppermute | solution.py:768
  33.6 13.7 %collective-permute-start.5 = (bf16[1184,256]{1,0:T(8,128)(2,1)S(1)}, bf16[1184,256]{1,0:T(8,128)(2,1)S(1)}, u32[]{:S(2)}, u32[]{:S(2)}) collective-permute-start(bf16[1184,256]{1,0:T(8,128)(2,1)S(1)} %get-tuple-element.161), channel_id=1, source_target_pairs={{0,4},{1,9},{2,6},{3,11},{4,0},{5,13},{6,2},{7,15},{8,12},{9,1},{1... | collective-permute-start | bytes 1818632 | tf_op jit(solution)/shard_map/ppermute | solution.py:768
  40.7 8.0 %collective-permute-start.4 = (bf16[800,256]{1,0:T(8,128)(2,1)S(1)}, bf16[800,256]{1,0:T(8,128)(2,1)S(1)}, u32[]{:S(2)}, u32[]{:S(2)}) collective-permute-start(bf16[800,256]{1,0:T(8,128)(2,1)S(1)} %get-tuple-element.158), channel_id=1, source_target_pairs={{0,8},{1,3},{2,10},{3,1},{4,12},{5,7},{6,14},{7,5},{8,0},{9,11},{1... | collective-permute-start | bytes 1228808 | tf_op jit(solution)/shard_map/ppermute | solution.py:768
  47.5 9.2 %collective-permute-start.7 = (bf16[608,256]{1,0:T(8,128)(2,1)S(1)}, bf16[608,256]{1,0:T(8,128)(2,1)S(1)}, u32[]{:S(2)}, u32[]{:S(2)}) collective-permute-start(bf16[608,256]{1,0:T(8,128)(2,1)S(1)} %get-tuple-element.169), channel_id=1, source_target_pairs={{0,8},{1,3},{2,10},{3,1},{4,12},{5,7},{6,14},{7,5},{8,0},{9,11},{1... | collective-permute-start | bytes 933896 | tf_op jit(solution)/shard_map/ppermute | solution.py:768
  48.0 16.6 %collective-permute-start.3 = (bf16[1184,256]{1,0:T(8,128)(2,1)S(1)}, bf16[1184,256]{1,0:T(8,128)(2,1)S(1)}, u32[]{:S(2)}, u32[]{:S(2)}) collective-permute-start(bf16[1184,256]{1,0:T(8,128)(2,1)S(1)} %get-tuple-element.155), channel_id=1, source_target_pairs={{0,2},{1,5},{2,0},{3,7},{4,6},{5,1},{6,4},{7,3},{8,10},{9,13},{10,... | collective-permute-start | bytes 1818632 | tf_op jit(solution)/shard_map/ppermute | solution.py:768
  48.9 8.3 %collective-permute-start.6 = (bf16[416,256]{1,0:T(8,128)(2,1)S(1)}, bf16[416,256]{1,0:T(8,128)(2,1)S(1)}, u32[]{:S(2)}, u32[]{:S(2)}) collective-permute-start(bf16[416,256]{1,0:T(8,128)(2,1)S(1)} %get-tuple-element.166), channel_id=1, source_target_pairs={{0,4},{1,9},{2,6},{3,11},{4,0},{5,13},{6,2},{7,15},{8,12},{9,1},{1... | collective-permute-start | bytes 638984 | tf_op jit(solution)/shard_map/ppermute | solution.py:768
  50.0 17.8 %collective-permute-start.11 = (bf16[1184,256]{1,0:T(8,128)(2,1)S(1)}, bf16[1184,256]{1,0:T(8,128)(2,1)S(1)}, u32[]{:S(2)}, u32[]{:S(2)}) collective-permute-start(bf16[1184,256]{1,0:T(8,128)(2,1)S(1)} %get-tuple-element.183), channel_id=1, source_target_pairs={{0,8},{1,3},{2,10},{3,1},{4,12},{5,7},{6,14},{7,5},{8,0},{9,11},{1... | collective-permute-start | bytes 1818632 | tf_op jit(solution)/shard_map/ppermute | solution.py:768
  57.3 11.5 %collective-permute-start.10 = (bf16[416,256]{1,0:T(8,128)(2,1)S(1)}, bf16[416,256]{1,0:T(8,128)(2,1)S(1)}, u32[]{:S(2)}, u32[]{:S(2)}) collective-permute-start(bf16[416,256]{1,0:T(8,128)(2,1)S(1)} %get-tuple-element.180.refs_0_), channel_id=1, source_target_pairs={{0,16},{1,17},{2,18},{3,19},{4,20},{5,21},{6,22},{7,23},{8,24},{9,... | collective-permute-start | bytes 638984 | tf_op jit(solution)/shard_map/ppermute | solution.py:768
  64.8 9.7 %collective-permute-start.8 = (bf16[608,256]{1,0:T(8,128)(2,1)S(1)}, bf16[608,256]{1,0:T(8,128)(2,1)S(1)}, u32[]{:S(2)}, u32[]{:S(2)}) collective-permute-start(bf16[608,256]{1,0:T(8,128)(2,1)S(1)} %get-tuple-element.175), channel_id=1, source_target_pairs={{0,8},{1,3},{2,10},{3,1},{4,12},{5,7},{6,14},{7,5},{8,0},{9,11},{1... | collective-permute-start | bytes 933896 | tf_op jit(solution)/shard_map/ppermute | solution.py:768
  66.5 5.3 %collective-permute-start.9 = (bf16[320,256]{1,0:T(8,128)(2,1)S(1)}, bf16[320,256]{1,0:T(8,128)(2,1)S(1)}, u32[]{:S(2)}, u32[]{:S(2)}) collective-permute-start(bf16[320,256]{1,0:T(8,128)(2,1)S(1)} %get-tuple-element.178), channel_id=1, source_target_pairs={{0,2},{1,5},{2,0},{3,7},{4,6},{5,1},{6,4},{7,3},{8,10},{9,13},{10,... | collective-permute-start | bytes 491528 | tf_op jit(solution)/shard_map/ppermute | solution.py:768
  68.0 7.8 %collective-permute-start.14 = (bf16[608,256]{1,0:T(8,128)(2,1)S(1)}, bf16[608,256]{1,0:T(8,128)(2,1)S(1)}, u32[]{:S(2)}, u32[]{:S(2)}) collective-permute-start(bf16[608,256]{1,0:T(8,128)(2,1)S(1)} %get-tuple-element.195), channel_id=1, source_target_pairs={{0,2},{1,5},{2,0},{3,7},{4,6},{5,1},{6,4},{7,3},{8,10},{9,13},{10,... | collective-permute-start | bytes 933896 | tf_op jit(solution)/shard_map/ppermute | solution.py:768
  68.9 6.9 %collective-permute-start.15 = (bf16[416,256]{1,0:T(8,128)(2,1)S(1)}, bf16[416,256]{1,0:T(8,128)(2,1)S(1)}, u32[]{:S(2)}, u32[]{:S(2)}) collective-permute-start(bf16[416,256]{1,0:T(8,128)(2,1)S(1)} %get-tuple-element.197.refs_0_), channel_id=1, source_target_pairs={{0,4},{1,9},{2,6},{3,11},{4,0},{5,13},{6,2},{7,15},{8,12},{9,1},{1... | collective-permute-start | bytes 638984 | tf_op jit(solution)/shard_map/ppermute | solution.py:768
  71.9 9.6 %collective-permute-start.13 = (bf16[320,256]{1,0:T(8,128)(2,1)S(1)}, bf16[320,256]{1,0:T(8,128)(2,1)S(1)}, u32[]{:S(2)}, u32[]{:S(2)}) collective-permute-start(bf16[320,256]{1,0:T(8,128)(2,1)S(1)} %get-tuple-element.192.refs_0_), channel_id=1, source_target_pairs={{0,16},{1,17},{2,18},{3,19},{4,20},{5,21},{6,22},{7,23},{8,24},{9,... | collective-permute-start | bytes 491528 | tf_op jit(solution)/shard_map/ppermute | solution.py:768
  74.7 7.6 %collective-permute-start.12 = (bf16[320,256]{1,0:T(8,128)(2,1)S(1)}, bf16[320,256]{1,0:T(8,128)(2,1)S(1)}, u32[]{:S(2)}, u32[]{:S(2)}) collective-permute-start(bf16[320,256]{1,0:T(8,128)(2,1)S(1)} %get-tuple-element.190), channel_id=1, source_target_pairs={{0,4},{1,9},{2,6},{3,11},{4,0},{5,13},{6,2},{7,15},{8,12},{9,1},{1... | collective-permute-start | bytes 491528 | tf_op jit(solution)/shard_map/ppermute | solution.py:768
  76.0 7.6 %collective-permute-start.18 = (bf16[320,256]{1,0:T(8,128)(2,1)S(1)}, bf16[320,256]{1,0:T(8,128)(2,1)S(1)}, u32[]{:S(2)}, u32[]{:S(2)}) collective-permute-start(bf16[320,256]{1,0:T(8,128)(2,1)S(1)} %get-tuple-element.206), channel_id=1, source_target_pairs={{0,4},{1,9},{2,6},{3,11},{4,0},{5,13},{6,2},{7,15},{8,12},{9,1},{1... | collective-permute-start | bytes 491528 | tf_op jit(solution)/shard_map/ppermute | solution.py:768
  77.1 10.9 %collective-permute-start.17 = (bf16[768,256]{1,0:T(8,128)(2,1)S(1)}, bf16[768,256]{1,0:T(8,128)(2,1)S(1)}, u32[]{:S(2)}, u32[]{:S(2)}) collective-permute-start(bf16[768,256]{1,0:T(8,128)(2,1)S(1)} %get-tuple-element.204.refs_0_), channel_id=1, source_target_pairs={{0,8},{1,3},{2,10},{3,1},{4,12},{5,7},{6,14},{7,5},{8,0},{9,11},{1... | collective-permute-start | bytes 1179656 | tf_op jit(solution)/shard_map/ppermute | solution.py:768
  81.6 11.4 %collective-permute-start.21 = (bf16[320,256]{1,0:T(8,128)(2,1)S(1)}, bf16[320,256]{1,0:T(8,128)(2,1)S(1)}, u32[]{:S(2)}, u32[]{:S(2)}) collective-permute-start(bf16[320,256]{1,0:T(8,128)(2,1)S(1)} %get-tuple-element.214.refs_0_), channel_id=1, source_target_pairs={{0,2},{1,5},{2,0},{3,7},{4,6},{5,1},{6,4},{7,3},{8,10},{9,13},{10,... | collective-permute-start | bytes 491528 | tf_op jit(solution)/shard_map/ppermute | solution.py:768
  82.3 9.4 %collective-permute-start.16 = (bf16[320,256]{1,0:T(8,128)(2,1)S(1)}, bf16[320,256]{1,0:T(8,128)(2,1)S(1)}, u32[]{:S(2)}, u32[]{:S(2)}) collective-permute-start(bf16[320,256]{1,0:T(8,128)(2,1)S(1)} %get-tuple-element.202.refs_0_), channel_id=1, source_target_pairs={{0,16},{1,17},{2,18},{3,19},{4,20},{5,21},{6,22},{7,23},{8,24},{9,... | collective-permute-start | bytes 491528 | tf_op jit(solution)/shard_map/ppermute | solution.py:768
  88.1 18.6 %collective-permute-start.23 = (bf16[1536,256]{1,0:T(8,128)(2,1)S(1)}, bf16[1536,256]{1,0:T(8,128)(2,1)S(1)}, u32[]{:S(2)}, u32[]{:S(2)}) collective-permute-start(bf16[1536,256]{1,0:T(8,128)(2,1)S(1)} %get-tuple-element.219.refs_0_.refs_1_), channel_id=1, source_target_pairs={{0,2},{1,5},{2,0},{3,7},{4,6},{5,1},{6,4},{7,3},{8,10},{9,13},{10,... | collective-permute-start | bytes 2359304 | tf_op jit(solution)/shard_map/ppermute | solution.py:768
  88.2 10.4 %collective-permute-start.20 = (bf16[320,256]{1,0:T(8,128)(2,1)S(1)}, bf16[320,256]{1,0:T(8,128)(2,1)S(1)}, u32[]{:S(2)}, u32[]{:S(2)}) collective-permute-start(bf16[320,256]{1,0:T(8,128)(2,1)S(1)} %get-tuple-element.212.refs_0_), channel_id=1, source_target_pairs={{0,16},{1,17},{2,18},{3,19},{4,20},{5,21},{6,22},{7,23},{8,24},{9,... | collective-permute-start | bytes 491528 | tf_op jit(solution)/shard_map/ppermute | solution.py:768
  91.8 8.2 %collective-permute-start.19 = (bf16[320,256]{1,0:T(8,128)(2,1)S(1)}, bf16[320,256]{1,0:T(8,128)(2,1)S(1)}, u32[]{:S(2)}, u32[]{:S(2)}) collective-permute-start(bf16[320,256]{1,0:T(8,128)(2,1)S(1)} %get-tuple-element.211.refs_0_), channel_id=1, source_target_pairs={{0,4},{1,9},{2,6},{3,11},{4,0},{5,13},{6,2},{7,15},{8,12},{9,1},{1... | collective-permute-start | bytes 491528 | tf_op jit(solution)/shard_map/ppermute | solution.py:768
  93.1 12.7 %collective-permute-start.24 = (bf16[576,256]{1,0:T(8,128)(2,1)S(1)}, bf16[576,256]{1,0:T(8,128)(2,1)S(1)}, u32[]{:S(2)}, u32[]{:S(2)}) collective-permute-start(bf16[576,256]{1,0:T(8,128)(2,1)S(1)} %get-tuple-element.223.refs_0_), channel_id=1, source_target_pairs={{0,8},{1,3},{2,10},{3,1},{4,12},{5,7},{6,14},{7,5},{8,0},{9,11},{1... | collective-permute-start | bytes 884744 | tf_op jit(solution)/shard_map/ppermute | solution.py:768
  98.7 5.4 %collective-permute-start.25 = (bf16[320,256]{1,0:T(8,128)(2,1)S(1)}, bf16[320,256]{1,0:T(8,128)(2,1)S(1)}, u32[]{:S(2)}, u32[]{:S(2)}) collective-permute-start(bf16[320,256]{1,0:T(8,128)(2,1)S(1)} %get-tuple-element.224.refs_0_), channel_id=1, source_target_pairs={{0,4},{1,9},{2,6},{3,11},{4,0},{5,13},{6,2},{7,15},{8,12},{9,1},{1... | collective-permute-start | bytes 491528 | tf_op jit(solution)/shard_map/ppermute | solution.py:768
  100.0 7.9 %collective-permute-start.22 = (bf16[576,256]{1,0:T(8,128)(2,1)S(1)}, bf16[576,256]{1,0:T(8,128)(2,1)S(1)}, u32[]{:S(2)}, u32[]{:S(2)}) collective-permute-start(bf16[576,256]{1,0:T(8,128)(2,1)S(1)} %get-tuple-element.218.refs_0_), channel_id=1, source_target_pairs={{0,8},{1,3},{2,10},{3,1},{4,12},{5,7},{6,14},{7,5},{8,0},{9,11},{1... | collective-permute-start | bytes 884744 | tf_op jit(solution)/shard_map/ppermute | solution.py:768
  100.2 7.8 %collective-permute-start.2 = (bf16[1408,128]{1,0:T(8,128)(2,1)S(1)}, bf16[1408,128]{1,0:T(8,128)(2,1)S(1)}, u32[]{:S(2)}, u32[]{:S(2)}) collective-permute-start(bf16[1408,128]{1,0:T(8,128)(2,1)S(1)} %get-tuple-element.153), channel_id=1, source_target_pairs={{0,1},{1,0},{2,3},{3,2},{4,5},{5,4},{6,7},{7,6},{8,9},{9,8},{10,11... | collective-permute-start | bytes 1081352 | tf_op jit(solution)/shard_map/ppermute | solution.py:904
  104.1 6.8 %collective-permute-start.28 = (bf16[576,256]{1,0:T(8,128)(2,1)S(1)}, bf16[576,256]{1,0:T(8,128)(2,1)S(1)}, u32[]{:S(2)}, u32[]{:S(2)}) collective-permute-start(bf16[576,256]{1,0:T(8,128)(2,1)S(1)} %get-tuple-element.233.refs_0_), channel_id=1, source_target_pairs={{0,2},{1,5},{2,0},{3,7},{4,6},{5,1},{6,4},{7,3},{8,10},{9,13},{10,... | collective-permute-start | bytes 884744 | tf_op jit(solution)/shard_map/ppermute | solution.py:768
  105.9 12.0 %collective-permute-start.26 = (bf16[1152,256]{1,0:T(8,128)(2,1)S(1)}, bf16[1152,256]{1,0:T(8,128)(2,1)S(1)}, u32[]{:S(2)}, u32[]{:S(2)}) collective-permute-start(bf16[1152,256]{1,0:T(8,128)(2,1)S(1)} %get-tuple-element.231.refs_0_), channel_id=1, source_target_pairs={{0,4},{1,9},{2,6},{3,11},{4,0},{5,13},{6,2},{7,15},{8,12},{9,1},{1... | collective-permute-start | bytes 1769480 | tf_op jit(solution)/shard_map/ppermute | solution.py:768
  107.8 4.9 %collective-permute-start.30 = (bf16[800,256]{1,0:T(8,128)(2,1)S(1)}, bf16[800,256]{1,0:T(8,128)(2,1)S(1)}, u32[]{:S(2)}, u32[]{:S(2)}) collective-permute-start(bf16[800,256]{1,0:T(8,128)(2,1)S(1)} %get-tuple-element.240.refs_0_), channel_id=1, source_target_pairs={{0,1},{1,0},{2,3},{3,2},{4,5},{5,4},{6,7},{7,6},{8,9},{9,8},{10,11... | collective-permute-start | bytes 1228808 | tf_op jit(solution)/shard_map/ppermute | solution.py:914
  111.0 9.9 %collective-permute-start.29 = (bf16[1152,256]{1,0:T(8,128)(2,1)S(1)}, bf16[1152,256]{1,0:T(8,128)(2,1)S(1)}, u32[]{:S(2)}, u32[]{:S(2)}) collective-permute-start(bf16[1152,256]{1,0:T(8,128)(2,1)S(1)} %get-tuple-element.235.refs_0_), channel_id=1, source_target_pairs={{0,8},{1,3},{2,10},{3,1},{4,12},{5,7},{6,14},{7,5},{8,0},{9,11},{1... | collective-permute-start | bytes 1769480 | tf_op jit(solution)/shard_map/ppermute | solution.py:768
  111.1 14.8 %collective-permute-start.27 = (bf16[1152,256]{1,0:T(8,128)(2,1)S(1)}, bf16[1152,256]{1,0:T(8,128)(2,1)S(1)}, u32[]{:S(2)}, u32[]{:S(2)}) collective-permute-start(bf16[1152,256]{1,0:T(8,128)(2,1)S(1)} %get-tuple-element.232.refs_0_), channel_id=1, source_target_pairs={{0,2},{1,5},{2,0},{3,7},{4,6},{5,1},{6,4},{7,3},{8,10},{9,13},{10,... | collective-permute-start | bytes 1769480 | tf_op jit(solution)/shard_map/ppermute | solution.py:768
